TPU v7x, 32 devices: a whole 2x2x4 slice. The times are simulated.
32 devices in a mesh: tile: 8 (over z, y), sub: 4 (over x, core).
Axes of the slice: x: 2, y: 2, z: 4, core: 2. Of those that a mesh axis runs over, the one named last changes fastest.
Arguments:
- offsets: float32 [3, 32, 16, 1024], P(None, None, 'tile', 'sub'), may hold values from 0 to 1
- velocity: float32 [3, 32, 16, 1024], P(None, None, 'tile', 'sub'), may hold values from -1.5 to 1.5
- mass: float32 [32, 16, 1024], P(None, 'tile', 'sub'), may hold values from 0.015625 to 0.0625
- entropy: float32 [32, 16, 1024], P(None, 'tile', 'sub'), may hold values from 0.5 to 2
- active_counts: int32 [3, 16, 1024], P(None, 'tile', 'sub'), may hold values from 0 to 32, as said below
- targets: int32 [32, 16, 1024], P(None, 'tile', 'sub'), may hold values from 0 to 3, as said below
Outputs:
- arrived: float32 [8, 786432], P(None, ('tile', 'sub'))
Inputs may be any that keep to these rules, and one draw needn't show every extreme that they name: active_counts[0] is a cell's number of occupied slots, from 16 to 32; counts never rise from one level to the next; active_counts[1] is at most 16 and active_counts[2] at most 8, and these bounds and 32 are each reached in some cell. Active particles of a substep are the cell's first slots. `targets`: among one device's 16384 particles, no destination is named by more than 6144 of them, and one destination is named by exactly 6144.
All inputs are finite; a program needn't handle non-finite values.
Results may differ from a plain program's by a relative error of at most 0.0001.
Values sent between devices are 32-bit elements; how exact they have to be, the bound alone decides.
No kernel may reach another device: no remote copies, remote signals or barrier semaphores. Data moves between devices by JAX's collectives and lax.ppermute only.
A program may use at most 128 MiB of HBM per device.

v0:
```python
import functools
import math

import jax
import jax.numpy as jnp
from jax import lax
from jax.experimental import pallas as pl
from jax.experimental.pallas import tpu as pltpu
from jax.sharding import PartitionSpec as P

KERNEL_NORM = 21.0 / (2.0 * math.pi)
GAMMA = 5.0 / 3.0
TIME_STEP = 0.05
SOFTEN = 0.01
LANES = 128
ROWS = 8
VMEM = pl.BlockSpec(memory_space=pltpu.VMEM)
SMEM = pl.BlockSpec(memory_space=pltpu.SMEM)
PARAMS = pltpu.CompilerParams(vmem_limit_bytes=40 << 20)
MOTION, PRESSURE = 7, 3
SHIFTS = (-1, 0, 1)


def lane_of(shape):
    return lax.broadcasted_iota(jnp.int32, shape, 1)


def cost(pairs, ops):
    return pl.CostEstimate(flops=int(pairs * ops), bytes_accessed=1 << 20, transcendentals=0)


def pair_force(own, their, total):
    xi, yi, zi, ui, vi, wi, qi, ci, ri = own
    xj, yj, zj, uj, vj, wj, qj, cj, rj, mj = their
    dx, dy, dz = xi - xj, yi - yj, zi - zj
    squared = dx * dx + dy * dy + dz * dz
    radius = squared * lax.rsqrt(jnp.maximum(squared, 1e-30))
    remain = jnp.maximum(1.0 - radius, 0.0)
    approach = dx * (ui - uj) + dy * (vi - vj) + dz * (wi - wj)
    closing = jnp.minimum(approach, 0.0) * pl.reciprocal(squared + SOFTEN, approx=True)
    viscous = closing * (closing - (ci + cj)) * pl.reciprocal(ri + rj, approx=True)
    strength = (qi + qj + viscous) * ((remain * remain) * (remain * mj))
    return (total[0] + strength * dx, total[1] + strength * dy, total[2] + strength * dz)


def pair_density(own, their, total):
    xi, yi, zi = own
    xj, yj, zj, mj = their
    dx, dy, dz = xi - xj, yi - yj, zi - zj
    squared = dx * dx + dy * dy + dz * dz
    radius = squared * lax.rsqrt(jnp.maximum(squared, 1e-30))
    remain = jnp.maximum(1.0 - radius, 0.0)
    square = remain * remain
    return (total[0] + (square * square) * ((5.0 - 4.0 * remain) * mj),)


DENSITY = ((0, 1.0), (1, 1.0), (2, 1.0)), (), ((6, KERNEL_NORM),), pair_density, 1
FORCE = (
    tuple((c, 1.0) for c in range(3)) + tuple((c, 4.0) for c in range(3, 6)),
    ((0, 1.0), (1, 1.0), (2, 4.0)),
    ((6, 20.0 * KERNEL_NORM),),
    pair_force,
    3,
)


def store_shifted(shifted, col, row, lo, hi, blocks, left, right, is_y):
    lane = lane_of(blocks[0].shape)
    up = [pltpu.roll(v, 1, 1) for v in [left] + blocks]
    down = [pltpu.roll(v, LANES - 1, 1) for v in blocks + [right]]
    for b, block in enumerate(blocks):
        before = jnp.where(lane == 0, up[b], up[b + 1])
        after = jnp.where(lane == LANES - 1, down[b + 1], down[b])
        for s, value in zip(SHIFTS, (before, block, after)):
            if is_y and s:
                value = value + float(s)
            shifted[col, s + 1, b, row, lo:hi, :] = value


def fill_shifted(shifted, col, row, pieces, field, scale, group):
    for cells, left, right, lo, hi in pieces:
        count = cells.shape[-1] // LANES
        blocks = [cells[field, lo:hi, b * LANES : (b + 1) * LANES] for b in range(count)]
        left_end = pltpu.roll(left[lo:hi, :], LANES - 1 - group, 1)
        right_end = right[lo:hi, :]
        if group:
            right_end = pltpu.roll(right_end, LANES - group, 1)
        if scale != 1.0:
            blocks = [v * scale for v in blocks]
            left_end, right_end = left_end * scale, right_end * scale
        store_shifted(shifted, col, row, lo, hi, blocks, left_end, right_end, field == 1 and scale == 1.0 and row == 1)


def fill_column(shifted, col, kind, motion, pressure, group_of):
    moved, pressed, massed, _, _ = kind
    row = 0
    for pieces, fields, width in ((motion, moved, MOTION), (pressure, pressed, PRESSURE), (motion, massed, MOTION)):
        for field, scale in fields:
            fill_shifted(shifted, col, row, pieces(field), field, scale, group_of(field))
            row += 1


def add_pairs(kind, motion_ref, pressure_ref, shifted, x, sources, limit, first, last, fold):
    moved, pressed, _, pair, width = kind
    slots = shifted.shape[-2]
    blocks = shifted.shape[2]
    rows = shifted.shape[3]
    group = min(limit // ROWS, 2 if width == 3 else 4)
    unroll = 4 if group > 1 else 8
    low_col, low_shift = sources[0]

    def lane_block(b, carry):
        lanes = pl.ds(pl.multiple_of(b * LANES, LANES), LANES)
        for part in range(limit // (ROWS * group)):
            spans = [slice((part * group + v) * ROWS, (part * group + v + 1) * ROWS) for v in range(group)]
            own = []
            for span in spans:
                values = [motion_ref[x, f, span, lanes] * s if s != 1.0 else motion_ref[x, f, span, lanes] for f, s in moved]
                values += [pressure_ref[x, f, span, lanes] * s if s != 1.0 else pressure_ref[x, f, span, lanes] for f, s in pressed]
                own.append(values)

            def source(at, totals):
                col = at // 3
                shift = at - 3 * col
                offset = (col + low_shift).astype(jnp.float32)
                mine = [[v[0] - offset] + v[1:] for v in own]

                def step(outer, totals):
                    totals = list(totals)
                    for inner in range(unroll):
                        slot = outer * unroll + inner
                        their = [
                            jnp.broadcast_to(shifted[col + low_col, shift, b, r, pl.ds(slot, 1), :], (ROWS, LANES))
                            for r in range(rows)
                        ]
                        for v in range(group):
                            totals[v] = pair(mine[v], their, totals[v])
                    return tuple(totals)

                return lax.fori_loop(0, slots // unroll, step, totals)

            totals = tuple(first(x, span, lanes) for span in spans)
            totals = lax.fori_loop(0, 3 * len(sources), source, totals)
            for span, total in zip(spans, totals):
                last(x, span, lanes, total)
        return carry

    lax.fori_loop(0, blocks, lane_block, 0)


def own_sources(x, columns):
    return [(c, c - x) for c in range(columns) if abs(c - x) <= 1]


def pack_ends(field_of, fields, columns, left_ref, right_ref):
    for ref, at_last in ((left_ref, False), (right_ref, True)):
        lane = None
        packed = None
        for group in range(fields * columns):
            block = field_of(group // columns, group % columns, at_last)
            if lane is None:
                lane = lane_of(block.shape)
                packed = jnp.zeros(block.shape, jnp.float32)
            turn = (group + 1) % LANES if at_last else group
            packed = jnp.where(lane == group, pltpu.roll(block, turn, 1) if turn else block, packed)
        ref[...] = packed


def end_block(ref, column, field, at_last, limit):
    width = ref.shape[-1]
    lanes = slice(width - LANES, width) if at_last else slice(0, LANES)
    return ref[column, field, :limit, lanes]


def first_ends(motion):
    columns, _, slots, _ = motion.shape

    def kernel(motion_ref, left_ref, right_ref):
        pack_ends(
            lambda f, c, last: end_block(motion_ref, c, f, last, slots), MOTION, columns, left_ref, right_ref
        )

    ends = jax.ShapeDtypeStruct((slots, LANES), jnp.float32)
    return pl.pallas_call(kernel, out_shape=(ends, ends), in_specs=[VMEM], out_specs=(VMEM, VMEM), compiler_params=PARAMS)(motion)


def bounds_of(arrays, axis):
    spans, lo = [], 0
    for index, array in enumerate(arrays):
        hi = array.shape[axis]
        if hi > lo:
            spans.append((index, lo, hi))
            lo = hi
    return spans


def own_part(kind, motion, pressure, ends_m, ends_p, limit):
    columns, _, slots, width = motion.shape
    moved, pressed, massed, _, outs = kind
    flat_m = [e for pair in ends_m for e in pair]
    flat_p = [e for pair in ends_p for e in pair]
    spans_m = bounds_of([e[0] for e in ends_m], 0)
    spans_p = bounds_of([e[0] for e in ends_p], 0)
    inputs = [motion] + ([pressure] if pressed else []) + flat_m + flat_p
    rows = len(moved) + len(pressed) + len(massed)

    def kernel(*refs):
        refs = list(refs)
        motion_ref = refs.pop(0)
        pressure_ref = refs.pop(0) if pressed else None
        m_refs = refs[: len(flat_m)]
        p_refs = refs[len(flat_m) : len(flat_m) + len(flat_p)]
        out_ref, shifted = refs[-2:]
        for c in range(columns):

            def motion_pieces(field):
                spans = spans_m if field < 6 else [(len(ends_m) - 1, 0, slots)]
                return [(motion_ref.at[c], m_refs[2 * i], m_refs[2 * i + 1], lo, hi) for i, lo, hi in spans]

            def pressure_pieces(field):
                return [(pressure_ref.at[c], p_refs[2 * i], p_refs[2 * i + 1], lo, hi) for i, lo, hi in spans_p]

            fill_column(shifted, c, kind, motion_pieces, pressure_pieces, lambda f: f * columns + c)
        zero = jnp.zeros((ROWS, LANES), jnp.float32)

        def last(x, span, lanes, total):
            for k in range(outs):
                out_ref[x, k, span, lanes] = total[k]

        for x in range(columns):
            add_pairs(kind, motion_ref, pressure_ref, shifted, x, own_sources(x, columns), limit, lambda *_: (zero,) * outs, last, None)

    return pl.pallas_call(
        kernel,
        out_shape=jax.ShapeDtypeStruct((columns, outs, limit, width), jnp.float32),
        in_specs=[VMEM] * len(inputs),
        out_specs=VMEM,
        scratch_shapes=[pltpu.VMEM((columns, 3, width // LANES, rows, slots, LANES), jnp.float32)],
        compiler_params=PARAMS,
        cost_estimate=cost(limit * slots * 3 * (3 * columns - 2) * width, 60 if outs == 3 else 30),
    )(*inputs)


def halo_sums(kind, refs, columns, slots, counts, limit, out_first, out_last, motion_ref, pressure_ref, shifted):
    moved, pressed, massed, _, outs = kind
    for side in range(2):
        m_refs, p_refs = refs[side]
        column = columns - 1 if side == 0 else 0
        spans_m = bounds_of(m_refs, 1)
        spans_p = bounds_of(p_refs, 1)

        def pieces(history, spans):
            out = []
            for i, lo, hi in spans:
                ref = history[i]
                plane = ref.shape[0] - 1
                out.append((ref, ref.at[plane, :, 0:LANES], ref.at[plane, :, LANES : 2 * LANES], lo, hi))
            return out

        def motion_pieces(field):
            return pieces(m_refs, spans_m if field < 6 else [(len(m_refs) - 1, 0, slots)])

        fill_column(shifted, side, kind, motion_pieces, lambda f: pieces(p_refs, spans_p), lambda f: f * columns + column)
        x, shift = (0, -1) if side == 0 else (columns - 1, 1)
        add_pairs(kind, motion_ref, pressure_ref, shifted, x, [(side, shift)], limit, out_first[side], out_last[side], None)


def density_rest(motion, partial, messages, density, entropy, counts, level, limit, slots_sent):
    columns, _, slots, width = motion.shape
    (m_left, m_right) = messages
    first = density is None
    inputs = [motion, partial, entropy, counts] + ([] if first else [density]) + m_left + m_right
    n_in, n_m = len(inputs), len(m_left)
    rows = 4

    def kernel(*refs):
        motion_ref, partial_ref, entropy_ref, counts_ref = refs[:4]
        old_ref = None if first else refs[4]
        m_refs = refs[n_in - 2 * n_m : n_in]
        press_ref, left_ref, right_ref, shifted, sums = refs[n_in:]
        sums[...] = partial_ref[...]

        def start(x, span, lanes):
            return (sums[x, 0, span, lanes],)

        def end(x, span, lanes, total):
            sums[x, 0, span, lanes] = total[0]

        halo_sums(
            DENSITY, ((m_refs[:n_m], ()), (m_refs[n_m:], ())), columns, slots, counts_ref, limit,
            (start, start), (end, end), motion_ref, None, shifted,
        )
        for x in range(columns):
            count = counts_ref[level, x : x + 1, :]
            for lo in range(0, slots, ROWS):
                span = slice(lo, lo + ROWS)
                if lo >= limit:
                    if first:
                        value = jnp.ones((ROWS, width), jnp.float32)
                    else:
                        for f in range(3):
                            press_ref[x, f, span, :] = old_ref[x, f, span, :]
                        continue
                else:
                    slot = lax.broadcasted_iota(jnp.int32, (ROWS, width), 0) + lo
                    before = jnp.ones((ROWS, width), jnp.float32) if first else old_ref[x, 2, span, :]
                    value = jnp.where(slot < count, sums[x, 0, span, :], before)
                pressure = entropy_ref[x, span, :] * jnp.exp(jnp.log(value) * (GAMMA - 2.0))
                press_ref[x, 0, span, :] = pressure
                press_ref[x, 1, span, :] = jnp.sqrt(GAMMA * pressure * value)
                press_ref[x, 2, span, :] = value
        pack_ends(lambda f, c, last: end_block(press_ref, c, f, last, slots_sent), PRESSURE, columns, left_ref, right_ref)

    ends = jax.ShapeDtypeStruct((slots_sent, LANES), jnp.float32)
    return pl.pallas_call(
        kernel,
        out_shape=(jax.ShapeDtypeStruct((columns, PRESSURE, slots, width), jnp.float32), ends, ends),
        in_specs=[VMEM] * n_in,
        out_specs=(VMEM,) * 3,
        scratch_shapes=[
            pltpu.VMEM((2, 3, width // LANES, rows, slots, LANES), jnp.float32),
            pltpu.VMEM((columns, 1, limit, width), jnp.float32),
        ],
        compiler_params=PARAMS,
        cost_estimate=cost(limit * slots * 6 * width, 30),
    )(*inputs)


def force_rest(motion, pressure, partial, messages_m, messages_p, counts, level, limit, slots_sent):
    columns, _, slots, width = motion.shape
    n_m, n_p = len(messages_m[0]), len(messages_p[0])
    inputs = [motion, pressure, partial, counts] + messages_m[0] + messages_p[0] + messages_m[1] + messages_p[1]
    n_in = len(inputs)
    rows = 10
    ends = jax.ShapeDtypeStruct((slots_sent, LANES), jnp.float32)
    outs = (jax.ShapeDtypeStruct(motion.shape, jnp.float32),) + ((ends, ends) if slots_sent else ())

    def kernel(*refs):
        motion_ref, pressure_ref, partial_ref, counts_ref = refs[:4]
        sides = []
        for side in range(2):
            at = 4 + side * (n_m + n_p)
            sides.append((refs[at : at + n_m], refs[at + n_m : at + n_m + n_p]))
        new_ref = refs[n_in]
        shifted, sums = refs[-2:]
        sums[...] = partial_ref[...]

        def start(x, span, lanes):
            return tuple(sums[x, k, span, lanes] for k in range(3))

        def end(x, span, lanes, total):
            for k in range(3):
                sums[x, k, span, lanes] = total[k]

        halo_sums(FORCE, sides, columns, slots, counts_ref, limit, (start, start), (end, end), motion_ref, pressure_ref, shifted)
        for x in range(columns):
            count = counts_ref[level, x : x + 1, :]
            new_ref[x, 6, :, :] = motion_ref[x, 6, :, :]
            if limit < slots:
                for f in range(6):
                    new_ref[x, f, limit:, :] = motion_ref[x, f, limit:, :]
            for lo in range(0, limit, ROWS):
                span = slice(lo, lo + ROWS)
                active = lax.broadcasted_iota(jnp.int32, (ROWS, width), 0) + lo < count
                for k in range(3):
                    place, speed = motion_ref[x, k, span, :], motion_ref[x, 3 + k, span, :]
                    faster = speed + TIME_STEP * sums[x, k, span, :]
                    new_ref[x, 3 + k, span, :] = jnp.where(active, faster, speed)
                    new_ref[x, k, span, :] = jnp.where(active, place + TIME_STEP * faster, place)
        if slots_sent:
            left_ref, right_ref = refs[n_in + 1 : n_in + 3]
            pack_ends(lambda f, c, last: end_block(new_ref, c, f, last, slots_sent), 6, columns, left_ref, right_ref)

    made = pl.pallas_call(
        kernel,
        out_shape=outs,
        in_specs=[VMEM] * n_in,
        out_specs=(VMEM,) * len(outs),
        scratch_shapes=[
            pltpu.VMEM((2, 3, width // LANES, rows, slots, LANES), jnp.float32),
            pltpu.VMEM((columns, 3, limit, width), jnp.float32),
        ],
        compiler_params=PARAMS,
        cost_estimate=cost(limit * slots * 6 * width, 60),
    )(*inputs)
    return made if slots_sent else (made[0], None, None)


def ranks(destination, parts):
    rows, width = destination.shape

    def kernel(dest_ref, place_ref, meta_ref):
        dest = dest_ref[...]
        low = lax.broadcasted_iota(jnp.int32, (width, width), 0)
        upto = jnp.where(low <= lane_of((width, width)), 1.0, 0.0).astype(jnp.bfloat16)
        above = lax.broadcasted_iota(jnp.int32, (rows, rows), 0) > lane_of((rows, rows))
        above = jnp.where(above, 1.0, 0.0).astype(jnp.bfloat16)
        lane = lane_of((rows, LANES))
        meta = jnp.zeros((rows, LANES), jnp.float32)
        place = jnp.zeros((rows, width), jnp.float32)
        start = jnp.zeros((rows, 1), jnp.float32)
        for d in range(parts):
            mask = jnp.where(dest == d, 1.0, 0.0)
            inside = jnp.dot(mask.astype(jnp.bfloat16), upto, preferred_element_type=jnp.float32)
            count = inside[:, width - 1 : width]
            wide = jnp.broadcast_to(count, (rows, LANES))
            before = jnp.dot(above, wide.astype(jnp.bfloat16), preferred_element_type=jnp.float32)
            place = place + mask * (inside - 1.0 + start)
            meta = jnp.where(lane == d, before, meta)
            meta = jnp.where(lane == parts + d, jnp.broadcast_to(start, (rows, LANES)), meta)
            meta = jnp.where(lane == 2 * parts + d, before + wide, meta)
            start = start + count
        place_ref[...] = place.astype(jnp.int32)
        meta_ref[...] = meta.astype(jnp.int32)

    return pl.pallas_call(
        kernel,
        out_shape=(jax.ShapeDtypeStruct((rows, width), jnp.int32), jax.ShapeDtypeStruct((rows, LANES), jnp.int32)),
        in_specs=[VMEM],
        out_specs=(VMEM, VMEM),
        compiler_params=PARAMS,
    )(destination)


def compact(motion, pressure, place, meta, parts, capacity):
    columns, _, slots, width = motion.shape
    chunks = width // LANES
    total = -(-capacity // LANES)

    def kernel(motion_ref, pressure_ref, place_ref, meta_ref, out_ref, local, lists):
        lane = lane_of((ROWS, LANES))

        def do_group(group, carry):
            span = pl.ds(pl.multiple_of(group * ROWS, ROWS), ROWS)
            fields = [
                [motion_ref[x, f, span, :] for f in range(6)] + [pressure_ref[x, 2, span, :], motion_ref[x, 6, span, :]]
                for x in range(columns)
            ]
            for s in range(ROWS):
                for x in range(columns):
                    state = jnp.concatenate([v[s : s + 1, :] for v in fields[x]], axis=0)
                    high = state.astype(jnp.bfloat16).astype(jnp.float32)
                    rest = state - high
                    middle = rest.astype(jnp.bfloat16).astype(jnp.float32)
                    lowest = rest - middle
                    stacked = jnp.concatenate([high, middle, lowest], axis=0).astype(jnp.bfloat16)
                    row = (group * ROWS + s) * columns + x
                    wanted = place_ref[pl.ds(row, 1), :]
                    hot = jnp.where(lax.broadcasted_iota(jnp.int32, (width, width), 0) == wanted, 1.0, 0.0)
                    moved = lax.dot_general(
                        stacked, hot.astype(jnp.bfloat16), (((1,), (1,)), ((), ())), preferred_element_type=jnp.float32
                    )
                    moved = moved[0:8] + moved[8:16] + moved[16:24]
                    buffer = (s * columns + x) % 4
                    for c in range(chunks):
                        local[buffer, c + 1] = moved[:, c * LANES : (c + 1) * LANES]
                    for d in range(parts):
                        base = meta_ref[row, d]
                        begin = meta_ref[row, parts + d]
                        chunk = lax.shift_right_logical(base, 7)
                        off = lax.bitwise_and(base, LANES - 1)
                        turn = lax.bitwise_and(off - begin, LANES - 1)
                        at = lax.shift_right_logical(begin, 7)
                        at = at + jnp.where(off < lax.bitwise_and(begin, LANES - 1), 1, 0)
                        turned = [pltpu.roll(local[buffer, at + k], turn, 1) for k in range(chunks + 2)]
                        for k in range(chunks + 1):
                            value = jnp.where(lane >= turn, turned[k + 1], turned[k])
                            if k == 0:
                                value = jnp.where(lane >= off, value, lists[d, chunk])
                            lists[d, chunk + k] = value
            return carry

        lax.fori_loop(0, slots // ROWS, do_group, 0)
        for d in range(parts):
            count = meta_ref[slots * columns - 1, 2 * parts + d]
            for c in range(total):
                out_ref[d, :, c * LANES : (c + 1) * LANES] = jnp.where(lane + c * LANES < count, lists[d, c], 0.0)

    return pl.pallas_call(
        kernel,
        out_shape=jax.ShapeDtypeStruct((parts, 8, capacity), jnp.float32),
        in_specs=[VMEM, VMEM, VMEM, SMEM],
        out_specs=VMEM,
        scratch_shapes=[
            pltpu.VMEM((4, 2 * chunks + 4, ROWS, LANES), jnp.float32),
            pltpu.VMEM((parts, total + chunks + 2, ROWS, LANES), jnp.float32),
        ],
        compiler_params=PARAMS,
    )(motion, pressure, place, meta)


def pass_on(value, axis, step):
    count = lax.axis_size(axis)
    return lax.ppermute(value, axis, [(i, (i + step) % count) for i in range(count)])


def swap_ends(left_ends, right_ends):
    return pass_on(right_ends, "sub", 1), pass_on(left_ends, "sub", -1)


def swap_columns(cells, fields, limit, ends):
    width = cells.shape[-1]
    plane = jnp.concatenate(ends, axis=1)
    plane = jnp.pad(plane, ((0, 0), (0, width - plane.shape[1])))[None]
    first = jnp.concatenate([cells[0, :fields, :limit], plane], axis=0)
    final = jnp.concatenate([cells[-1, :fields, :limit], plane], axis=0)
    return pass_on(final, "tile", 1), pass_on(first, "tile", -1)


def shards(offsets, velocity, mass, entropy, active_counts, targets):
    slots, columns, width = mass.shape
    levels = active_counts.shape[0]
    parts = lax.axis_size("sub")
    slot_index = lax.broadcasted_iota(jnp.int32, mass.shape, 0)
    mass_live = jnp.where(slot_index < active_counts[0][None], mass, 0.0)
    motion = jnp.concatenate([offsets, velocity, mass_live[None]], axis=0).transpose(2, 0, 1, 3)
    entropy = entropy.transpose(1, 0, 2)
    limits = (slots, slots // 2, slots // 4)
    pressure = None
    ends_m, ends_p = [], []
    left_m, right_m, left_p, right_p = [], [], [], []
    made = first_ends(motion)
    place, meta = ranks(targets.reshape(slots * columns, width), parts)
    for level in range(levels):
        limit = limits[level]
        sent = limits[max(level - 1, 0)]
        fields = MOTION if level == 0 else 6
        ends_m.insert(0, swap_ends(*made))
        from_left, from_right = swap_columns(motion, fields, sent, ends_m[0])
        left_m.insert(0, from_left)
        right_m.insert(0, from_right)
        partial = own_part(DENSITY, motion, None, ends_m, [], limit)
        pressure, *made = density_rest(motion, partial, (left_m, right_m), pressure, entropy, active_counts, level, limit, limit)
        ends_p.insert(0, swap_ends(*made))
        from_left, from_right = swap_columns(pressure, PRESSURE, limit, ends_p[0])
        left_p.insert(0, from_left)
        right_p.insert(0, from_right)
        partial = own_part(FORCE, motion, pressure, ends_m, ends_p, limit)
        more = limit if level < levels - 1 else 0
        motion, *made = force_rest(
            motion, pressure, partial, (left_m, right_m), (left_p, right_p), active_counts, level, limit, more
        )
    capacity = 3 * slots * columns * width // 8
    lists = compact(motion, pressure, place, meta[:, : 3 * parts], parts, capacity)
    arrived = lax.all_to_all(lists, "sub", split_axis=0, concat_axis=0, tiled=True)
    return arrived.transpose(1, 0, 2).reshape(8, parts * capacity)


def solution(mesh):
    placed = (
        P(None, None, "tile", "sub"),
        P(None, None, "tile", "sub"),
        P(None, "tile", "sub"),
        P(None, "tile", "sub"),
        P(None, "tile", "sub"),
        P(None, "tile", "sub"),
    )
    return jax.shard_map(
        shards, mesh=mesh, in_specs=placed, out_specs=P(None, ("tile", "sub")), check_vma=False
    )
```

profile of v0, /device:TPU:0, one launch (start us, length us, event | category | flops | bytes accessed | tf_op | source)
XLA Modules:
  0.0 181.8 jit_solution(4903175609672325310)
XLA Ops:
  2.6 2.0 %collective-permute-start.1 = (f32[32,128]{1,0:T(8,128)S(1)}, f32[32,128]{1,0:T(8,128)S(1)}, u32[]{:S(2)}, u32[]{:S(2)}) collective-permute-start(f32[32,128]{1,0:T(8,128)S(1)} %get-tuple-element.25), channel_id=1, source_target_pairs={{0,3},{1,0},{2,1},{3,2},{4,7},{5,4},{6,5},{7,6},{8,11},{9,8},{10,9... | collective-permute-start | bytes 49160 | tf_op jit(solution)/shard_map/ppermute | solution.py:494
  6.1 2.3 %collective-permute-start.2 = (f32[8,32,256]{2,1,0:T(8,128)S(1)}, f32[8,32,256]{2,1,0:T(8,128)S(1)}, u32[]{:S(2)}, u32[]{:S(2)}) collective-permute-start(f32[8,32,256]{2,1,0:T(8,128)S(1)} %get-tuple-element.60), channel_id=1, source_target_pairs={{0,4},{4,8},{8,12},{12,16},{16,20},{20,24},{24,28},{28,0},{1,5},{5... | collective-permute-start | bytes 786440 | tf_op jit(solution)/shard_map/ppermute | solution.py:494
  8.4 3.1 %collective-permute-start.3 = (f32[8,32,256]{2,1,0:T(8,128)S(1)}, f32[8,32,256]{2,1,0:T(8,128)S(1)}, u32[]{:S(2)}, u32[]{:S(2)}) collective-permute-start(f32[8,32,256]{2,1,0:T(8,128)S(1)} %get-tuple-element.59), channel_id=1, source_target_pairs={{0,28},{4,0},{8,4},{12,8},{16,12},{20,16},{24,20},{28,24},{1,29},{... | collective-permute-start | bytes 786440 | tf_op jit(solution)/shard_map/ppermute | solution.py:494
  11.5 11.0 %shard_map.65.refs_1_ = f32[2,1,32,256]{3,2,1,0:T(8,128)S(1)} custom-call(f32[2,7,32,256]{3,2,1,0:T(8,128)S(1)} %maximum_bitcast_fusion.motion_ref.refs_0_, f32[32,128]{1,0:T(8,128)S(1)} %collective-permute-done.refs_1_.refs_2_.refs_3_.refs_4_.refs_5_.refs_6_, f32[32,128]{1,0:T(8,128)S(1)} %collective-permute-done.1.refs_2_.refs_3_.refs_4_.refs_5_.refs_6_.refs_7_), custom_call_target="tpu_custom_call" | custom-call | flops 94371840 | bytes 1048576 | tf_op jit(solution)/shard_map/pallas_call | solution.py:233
  22.9 5.9 %shard_map.66 = (f32[2,3,32,256]{3,2,1,0:T(8,128)S(1)}, f32[32,128]{1,0:T(8,128)S(1)}, f32[32,128]{1,0:T(8,128)S(1)}) custom-call(f32[2,7,32,256]{3,2,1,0:T(8,128)S(1)} %maximum_bitcast_fusion.motion_ref.refs_0_, f32[2,1,32,256]{3,2,1,0:T(8,128)S(1)} %shard_map.65.refs_1_, f32[2,32,256]{2,1,0:T(8,128)S(1)} %bitcast.49, s32[3,2,256]{2,1,0:T(2,128)S(1)} %copy-done, ...), custom_call_target="tpu_custom_call" | custom-call | flops 47185920 | bytes 1048576 | tf_op jit(solution)/shard_map/pallas_call | solution.py:315
  30.6 1.4 collective-permute-done.4.refs_4_.refs_8_.refs_12_
  32.1 4.7 %collective-permute-start.7 = (f32[4,32,256]{2,1,0:T(8,128)S(1)}, f32[4,32,256]{2,1,0:T(8,128)S(1)}, u32[]{:S(2)}, u32[]{:S(2)}) collective-permute-start(f32[4,32,256]{2,1,0:T(8,128)S(1)} %get-tuple-element.57), channel_id=1, source_target_pairs={{0,28},{4,0},{8,4},{12,8},{16,12},{20,16},{24,20},{28,24},{1,29},{... | collective-permute-start | bytes 393224 | tf_op jit(solution)/shard_map/ppermute | solution.py:494
  36.8 24.1 %shard_map.67.refs_2_ = f32[2,3,32,256]{3,2,1,0:T(8,128)S(1)} custom-call(f32[2,7,32,256]{3,2,1,0:T(8,128)S(1)} %maximum_bitcast_fusion.motion_ref.refs_0_, f32[2,3,32,256]{3,2,1,0:T(8,128)S(1)} %get-tuple-element.26.refs_1_.refs_4_, f32[32,128]{1,0:T(8,128)S(1)} %collective-permute-done.refs_1_.refs_2_.refs_3_.refs_4_.refs_5_.refs_6_, ...), custom_call_target="tpu_custom_call" | custom-call | flops 188743680 | bytes 1048576 | tf_op jit(solution)/shard_map/pallas_call | solution.py:233
  60.9 13.1 %shard_map.68 = (f32[2,7,32,256]{3,2,1,0:T(8,128)S(1)}, f32[32,128]{1,0:T(8,128)S(1)}, f32[32,128]{1,0:T(8,128)S(1)}) custom-call(f32[2,7,32,256]{3,2,1,0:T(8,128)S(1)} %maximum_bitcast_fusion.motion_ref.refs_0_, f32[2,3,32,256]{3,2,1,0:T(8,128)S(1)} %get-tuple-element.26.refs_1_.refs_4_, f32[2,3,32,256]{3,2,1,0:T(8,128)S(1)} %shard_map.67.refs_2_, ...), custom_call_target="tpu_custom_call" | custom-call | flops 94371840 | bytes 1048576 | tf_op jit(solution)/shard_map/pallas_call | solution.py:374
  77.4 4.7 %collective-permute-start.11 = (f32[7,32,256]{2,1,0:T(8,128)S(1)}, f32[7,32,256]{2,1,0:T(8,128)S(1)}, u32[]{:S(2)}, u32[]{:S(2)}) collective-permute-start(f32[7,32,256]{2,1,0:T(8,128)S(1)} %get-tuple-element.55), channel_id=1, source_target_pairs={{0,28},{4,0},{8,4},{12,8},{16,12},{20,16},{24,20},{28,24},{1,29},{... | collective-permute-start | bytes 688136 | tf_op jit(solution)/shard_map/ppermute | solution.py:494
  82.1 7.4 %shard_map.69.refs_1_ = f32[2,1,16,256]{3,2,1,0:T(8,128)S(1)} custom-call(f32[2,7,32,256]{3,2,1,0:T(8,128)S(1)} %get-tuple-element.29.refs_0_, f32[32,128]{1,0:T(8,128)S(1)} %collective-permute-done.8.refs_1_.refs_2_.refs_3_.refs_4_, f32[32,128]{1,0:T(8,128)S(1)} %collective-permute-done.9.refs_2_.refs_3_.refs_4_.refs_5_, ...), custom_call_target="tpu_custom_call" | custom-call | flops 47185920 | bytes 1048576 | tf_op jit(solution)/shard_map/pallas_call | solution.py:233
  90.5 4.1 %shard_map.70 = (f32[2,3,32,256]{3,2,1,0:T(8,128)S(1)}, f32[16,128]{1,0:T(8,128)S(1)}, f32[16,128]{1,0:T(8,128)S(1)}) custom-call(f32[2,7,32,256]{3,2,1,0:T(8,128)S(1)} %get-tuple-element.29.refs_0_, f32[2,1,16,256]{3,2,1,0:T(8,128)S(1)} %shard_map.69.refs_1_, f32[2,32,256]{2,1,0:T(8,128)S(1)} %bitcast.50, s32[3,2,256]{2,1,0:T(2,128)S(1)} %copy-done, ...), custom_call_target="tpu_custom_call" | custom-call | flops 23592960 | bytes 1048576 | tf_op jit(solution)/shard_map/pallas_call | solution.py:315
  94.7 1.6 collective-permute-start.13
  97.8 4.7 %collective-permute-start.15 = (f32[4,16,256]{2,1,0:T(8,128)S(1)}, f32[4,16,256]{2,1,0:T(8,128)S(1)}, u32[]{:S(2)}, u32[]{:S(2)}) collective-permute-start(f32[4,16,256]{2,1,0:T(8,128)S(1)} %get-tuple-element.63), channel_id=1, source_target_pairs={{0,28},{4,0},{8,4},{12,8},{16,12},{20,16},{24,20},{28,24},{1,29},{... | collective-permute-start | bytes 196616 | tf_op jit(solution)/shard_map/ppermute | solution.py:494
  102.5 13.3 %shard_map.71.refs_2_ = f32[2,3,16,256]{3,2,1,0:T(8,128)S(1)} custom-call(f32[2,7,32,256]{3,2,1,0:T(8,128)S(1)} %get-tuple-element.29.refs_0_, f32[2,3,32,256]{3,2,1,0:T(8,128)S(1)} %get-tuple-element.32.refs_1_.refs_4_, f32[32,128]{1,0:T(8,128)S(1)} %collective-permute-done.8.refs_1_.refs_2_.refs_3_.refs_4_, ...), custom_call_target="tpu_custom_call" | custom-call | flops 94371840 | bytes 1048576 | tf_op jit(solution)/shard_map/pallas_call | solution.py:233
  115.9 7.7 %shard_map.72 = (f32[2,7,32,256]{3,2,1,0:T(8,128)S(1)}, f32[16,128]{1,0:T(8,128)S(1)}, f32[16,128]{1,0:T(8,128)S(1)}) custom-call(f32[2,7,32,256]{3,2,1,0:T(8,128)S(1)} %get-tuple-element.29.refs_0_, f32[2,3,32,256]{3,2,1,0:T(8,128)S(1)} %get-tuple-element.32.refs_1_.refs_4_, f32[2,3,16,256]{3,2,1,0:T(8,128)S(1)} %shard_map.71.refs_2_, ...), custom_call_target="tpu_custom_call" | custom-call | flops 47185920 | bytes 1048576 | tf_op jit(solution)/shard_map/pallas_call | solution.py:374
  126.8 4.7 %collective-permute-start.19 = (f32[7,16,256]{2,1,0:T(8,128)S(1)}, f32[7,16,256]{2,1,0:T(8,128)S(1)}, u32[]{:S(2)}, u32[]{:S(2)}) collective-permute-start(f32[7,16,256]{2,1,0:T(8,128)S(1)} %get-tuple-element.61), channel_id=1, source_target_pairs={{0,28},{4,0},{8,4},{12,8},{16,12},{20,16},{24,20},{28,24},{1,29},{... | collective-permute-start | bytes 344072 | tf_op jit(solution)/shard_map/ppermute | solution.py:494
  131.5 4.4 %shard_map.73.refs_1_ = f32[2,1,8,256]{3,2,1,0:T(8,128)S(1)} custom-call(f32[2,7,32,256]{3,2,1,0:T(8,128)S(1)} %get-tuple-element.35.refs_0_, f32[16,128]{1,0:T(8,128)S(1)} %collective-permute-done.16.refs_1_.refs_2_, f32[16,128]{1,0:T(8,128)S(1)} %collective-permute-done.17.refs_2_.refs_3_, ...), custom_call_target="tpu_custom_call" | custom-call | flops 23592960 | bytes 1048576 | tf_op jit(solution)/shard_map/pallas_call | solution.py:233
  135.9 2.5 %shard_map.74 = (f32[2,3,32,256]{3,2,1,0:T(8,128)S(1)}, f32[8,128]{1,0:T(8,128)S(1)}, f32[8,128]{1,0:T(8,128)S(1)}) custom-call(f32[2,7,32,256]{3,2,1,0:T(8,128)S(1)} %get-tuple-element.35.refs_0_, f32[2,1,8,256]{3,2,1,0:T(8,128)S(1)} %shard_map.73.refs_1_, f32[2,32,256]{2,1,0:T(8,128)S(1)} %bitcast.51, s32[3,2,256]{2,1,0:T(2,128)S(1)} %copy-done, ...), custom_call_target="tpu_custom_call" | custom-call | flops 11796480 | bytes 1048576 | tf_op jit(solution)/shard_map/pallas_call | solution.py:315
  141.6 4.7 %collective-permute-start.23 = (f32[4,8,256]{2,1,0:T(8,128)S(1)}, f32[4,8,256]{2,1,0:T(8,128)S(1)}, u32[]{:S(2)}, u32[]{:S(2)}) collective-permute-start(f32[4,8,256]{2,1,0:T(8,128)S(1)} %get-tuple-element.65), channel_id=1, source_target_pairs={{0,28},{4,0},{8,4},{12,8},{16,12},{20,16},{24,20},{28,24},{1,29},{... | collective-permute-start | bytes 98312 | tf_op jit(solution)/shard_map/ppermute | solution.py:494
  147.2 9.1 %shard_map.75.refs_2_ = f32[2,3,8,256]{3,2,1,0:T(8,128)S(1)} custom-call(f32[2,7,32,256]{3,2,1,0:T(8,128)S(1)} %get-tuple-element.35.refs_0_, f32[2,3,32,256]{3,2,1,0:T(8,128)S(1)} %get-tuple-element.38.refs_1_.pressure_ref, f32[16,128]{1,0:T(8,128)S(1)} %collective-permute-done.16.refs_1_.refs_2_, f32[16,128]{1,0:T(8,128)S(1)} %collective-permute-done.17.refs_2_.refs_3_, ...), custom_call_target="tpu_custom_call" | custom-call | flops 47185920 | bytes 1048576 | tf_op jit(solution)/shard_map/pallas_call | solution.py:233
  156.3 5.8 %shard_map.76.motion_ref = f32[2,7,32,256]{3,2,1,0:T(8,128)S(1)} custom-call(f32[2,7,32,256]{3,2,1,0:T(8,128)S(1)} %get-tuple-element.35.refs_0_, f32[2,3,32,256]{3,2,1,0:T(8,128)S(1)} %get-tuple-element.38.refs_1_.pressure_ref, f32[2,3,8,256]{3,2,1,0:T(8,128)S(1)} %shard_map.75.refs_2_, s32[3,2,256]{2,1,0:T(2,128)S(1)} %copy-done, ...), custom_call_target="tpu_custom_call" | custom-call | flops 23592960 | bytes 1048576 | tf_op jit(solution)/shard_map/pallas_call | solution.py:374
  162.1 4.6 %shard_map.78 = f32[4,8,6144]{2,1,0:T(8,128)S(1)} custom-call(f32[2,7,32,256]{3,2,1,0:T(8,128)S(1)} %shard_map.76.motion_ref, f32[2,3,32,256]{3,2,1,0:T(8,128)S(1)} %get-tuple-element.38.refs_1_.pressure_ref, s32[64,256]{1,0:T(8,128)S(1)} %get-tuple-element.41.place_ref, s32[64,12]{1,0:T(8,128)S(1)} %bitcast.52), custom_call_target="tpu_custom_call" | custom-call | tf_op jit(solution)/shard_map/pallas_call | solution.py:479
  166.7 14.2 %all_to_all.5 = f32[4,8,6144]{2,1,0:T(8,128)S(1)} all-to-all(f32[4,8,6144]{2,1,0:T(8,128)S(1)} %shard_map.78), channel_id=1, replica_groups=mesh['tile'=8,'sub'=4] {'sub'}, dimensions={0} | all-to-all | bytes 1572864 | tf_op jit(solution)/shard_map/all_to_all | solution.py:545
  (76 shorter events, 20.6 us)
Async XLA Ops:
  2.1 3.9 %collective-permute-start = (f32[32,128]{1,0:T(8,128)S(1)}, f32[32,128]{1,0:T(8,128)S(1)}, u32[]{:S(2)}, u32[]{:S(2)}) collective-permute-start(f32[32,128]{1,0:T(8,128)S(1)} %get-tuple-element.24), channel_id=1, source_target_pairs={{0,1},{1,2},{2,3},{3,0},{4,5},{5,6},{6,7},{7,4},{8,9},{9,10},{10,1... | collective-permute-start | bytes 49160 | tf_op jit(solution)/shard_map/ppermute | solution.py:494
  2.6 3.4 %collective-permute-start.1 = (f32[32,128]{1,0:T(8,128)S(1)}, f32[32,128]{1,0:T(8,128)S(1)}, u32[]{:S(2)}, u32[]{:S(2)}) collective-permute-start(f32[32,128]{1,0:T(8,128)S(1)} %get-tuple-element.25), channel_id=1, source_target_pairs={{0,3},{1,0},{2,1},{3,2},{4,7},{5,4},{6,5},{7,6},{8,11},{9,8},{10,9... | collective-permute-start | bytes 49160 | tf_op jit(solution)/shard_map/ppermute | solution.py:494
  6.1 16.4 %collective-permute-start.2 = (f32[8,32,256]{2,1,0:T(8,128)S(1)}, f32[8,32,256]{2,1,0:T(8,128)S(1)}, u32[]{:S(2)}, u32[]{:S(2)}) collective-permute-start(f32[8,32,256]{2,1,0:T(8,128)S(1)} %get-tuple-element.60), channel_id=1, source_target_pairs={{0,4},{4,8},{8,12},{12,16},{16,20},{20,24},{24,28},{28,0},{1,5},{5... | collective-permute-start | bytes 786440 | tf_op jit(solution)/shard_map/ppermute | solution.py:494
  8.4 14.5 %collective-permute-start.3 = (f32[8,32,256]{2,1,0:T(8,128)S(1)}, f32[8,32,256]{2,1,0:T(8,128)S(1)}, u32[]{:S(2)}, u32[]{:S(2)}) collective-permute-start(f32[8,32,256]{2,1,0:T(8,128)S(1)} %get-tuple-element.59), channel_id=1, source_target_pairs={{0,28},{4,0},{8,4},{12,8},{16,12},{20,16},{24,20},{28,24},{1,29},{... | collective-permute-start | bytes 786440 | tf_op jit(solution)/shard_map/ppermute | solution.py:494
  28.8 3.2 %collective-permute-start.4 = (f32[32,128]{1,0:T(8,128)S(1)}, f32[32,128]{1,0:T(8,128)S(1)}, u32[]{:S(2)}, u32[]{:S(2)}) collective-permute-start(f32[32,128]{1,0:T(8,128)S(1)} %get-tuple-element.27), channel_id=1, source_target_pairs={{0,1},{1,2},{2,3},{3,0},{4,5},{5,6},{6,7},{7,4},{8,9},{9,10},{10,1... | collective-permute-start | bytes 49160 | tf_op jit(solution)/shard_map/ppermute | solution.py:494
  29.8 2.3 %collective-permute-start.5 = (f32[32,128]{1,0:T(8,128)S(1)}, f32[32,128]{1,0:T(8,128)S(1)}, u32[]{:S(2)}, u32[]{:S(2)}) collective-permute-start(f32[32,128]{1,0:T(8,128)S(1)} %get-tuple-element.28), channel_id=1, source_target_pairs={{0,3},{1,0},{2,1},{3,2},{4,7},{5,4},{6,5},{7,6},{8,11},{9,8},{10,9... | collective-permute-start | bytes 49160 | tf_op jit(solution)/shard_map/ppermute | solution.py:494
  32.0 28.9 %collective-permute-start.6 = (f32[4,32,256]{2,1,0:T(8,128)S(1)}, f32[4,32,256]{2,1,0:T(8,128)S(1)}, u32[]{:S(2)}, u32[]{:S(2)}) collective-permute-start(f32[4,32,256]{2,1,0:T(8,128)S(1)} %get-tuple-element.58), channel_id=1, source_target_pairs={{0,4},{4,8},{8,12},{12,16},{16,20},{20,24},{24,28},{28,0},{1,5},{5... | collective-permute-start | bytes 393224 | tf_op jit(solution)/shard_map/ppermute | solution.py:494
  32.1 28.8 %collective-permute-start.7 = (f32[4,32,256]{2,1,0:T(8,128)S(1)}, f32[4,32,256]{2,1,0:T(8,128)S(1)}, u32[]{:S(2)}, u32[]{:S(2)}) collective-permute-start(f32[4,32,256]{2,1,0:T(8,128)S(1)} %get-tuple-element.57), channel_id=1, source_target_pairs={{0,28},{4,0},{8,4},{12,8},{16,12},{20,16},{24,20},{28,24},{1,29},{... | collective-permute-start | bytes 393224 | tf_op jit(solution)/shard_map/ppermute | solution.py:494
  74.0 3.2 %collective-permute-start.8 = (f32[32,128]{1,0:T(8,128)S(1)}, f32[32,128]{1,0:T(8,128)S(1)}, u32[]{:S(2)}, u32[]{:S(2)}) collective-permute-start(f32[32,128]{1,0:T(8,128)S(1)} %get-tuple-element.30), channel_id=1, source_target_pairs={{0,1},{1,2},{2,3},{3,0},{4,5},{5,6},{6,7},{7,4},{8,9},{9,10},{10,1... | collective-permute-start | bytes 49160 | tf_op jit(solution)/shard_map/ppermute | solution.py:494
  74.9 2.4 %collective-permute-start.9 = (f32[32,128]{1,0:T(8,128)S(1)}, f32[32,128]{1,0:T(8,128)S(1)}, u32[]{:S(2)}, u32[]{:S(2)}) collective-permute-start(f32[32,128]{1,0:T(8,128)S(1)} %get-tuple-element.31), channel_id=1, source_target_pairs={{0,3},{1,0},{2,1},{3,2},{4,7},{5,4},{6,5},{7,6},{8,11},{9,8},{10,9... | collective-permute-start | bytes 49160 | tf_op jit(solution)/shard_map/ppermute | solution.py:494
  77.3 12.2 %collective-permute-start.10 = (f32[7,32,256]{2,1,0:T(8,128)S(1)}, f32[7,32,256]{2,1,0:T(8,128)S(1)}, u32[]{:S(2)}, u32[]{:S(2)}) collective-permute-start(f32[7,32,256]{2,1,0:T(8,128)S(1)} %get-tuple-element.56), channel_id=1, source_target_pairs={{0,4},{4,8},{8,12},{12,16},{16,20},{20,24},{24,28},{28,0},{1,5},{5... | collective-permute-start | bytes 688136 | tf_op jit(solution)/shard_map/ppermute | solution.py:494
  77.4 13.1 %collective-permute-start.11 = (f32[7,32,256]{2,1,0:T(8,128)S(1)}, f32[7,32,256]{2,1,0:T(8,128)S(1)}, u32[]{:S(2)}, u32[]{:S(2)}) collective-permute-start(f32[7,32,256]{2,1,0:T(8,128)S(1)} %get-tuple-element.55), channel_id=1, source_target_pairs={{0,28},{4,0},{8,4},{12,8},{16,12},{20,16},{24,20},{28,24},{1,29},{... | collective-permute-start | bytes 688136 | tf_op jit(solution)/shard_map/ppermute | solution.py:494
  94.5 3.1 %collective-permute-start.12 = (f32[16,128]{1,0:T(8,128)S(1)}, f32[16,128]{1,0:T(8,128)S(1)}, u32[]{:S(2)}, u32[]{:S(2)}) collective-permute-start(f32[16,128]{1,0:T(8,128)S(1)} %get-tuple-element.33), channel_id=1, source_target_pairs={{0,1},{1,2},{2,3},{3,0},{4,5},{5,6},{6,7},{7,4},{8,9},{9,10},{10,1... | collective-permute-start | bytes 24584 | tf_op jit(solution)/shard_map/ppermute | solution.py:494
  94.7 3.0 %collective-permute-start.13 = (f32[16,128]{1,0:T(8,128)S(1)}, f32[16,128]{1,0:T(8,128)S(1)}, u32[]{:S(2)}, u32[]{:S(2)}) collective-permute-start(f32[16,128]{1,0:T(8,128)S(1)} %get-tuple-element.34), channel_id=1, source_target_pairs={{0,3},{1,0},{2,1},{3,2},{4,7},{5,4},{6,5},{7,6},{8,11},{9,8},{10,9... | collective-permute-start | bytes 24584 | tf_op jit(solution)/shard_map/ppermute | solution.py:494
  97.7 18.1 %collective-permute-start.14 = (f32[4,16,256]{2,1,0:T(8,128)S(1)}, f32[4,16,256]{2,1,0:T(8,128)S(1)}, u32[]{:S(2)}, u32[]{:S(2)}) collective-permute-start(f32[4,16,256]{2,1,0:T(8,128)S(1)} %get-tuple-element.64), channel_id=1, source_target_pairs={{0,4},{4,8},{8,12},{12,16},{16,20},{20,24},{24,28},{28,0},{1,5},{5... | collective-permute-start | bytes 196616 | tf_op jit(solution)/shard_map/ppermute | solution.py:494
  97.8 18.1 %collective-permute-start.15 = (f32[4,16,256]{2,1,0:T(8,128)S(1)}, f32[4,16,256]{2,1,0:T(8,128)S(1)}, u32[]{:S(2)}, u32[]{:S(2)}) collective-permute-start(f32[4,16,256]{2,1,0:T(8,128)S(1)} %get-tuple-element.63), channel_id=1, source_target_pairs={{0,28},{4,0},{8,4},{12,8},{16,12},{20,16},{24,20},{28,24},{1,29},{... | collective-permute-start | bytes 196616 | tf_op jit(solution)/shard_map/ppermute | solution.py:494
  123.5 3.1 %collective-permute-start.16 = (f32[16,128]{1,0:T(8,128)S(1)}, f32[16,128]{1,0:T(8,128)S(1)}, u32[]{:S(2)}, u32[]{:S(2)}) collective-permute-start(f32[16,128]{1,0:T(8,128)S(1)} %get-tuple-element.36), channel_id=1, source_target_pairs={{0,1},{1,2},{2,3},{3,0},{4,5},{5,6},{6,7},{7,4},{8,9},{9,10},{10,1... | collective-permute-start | bytes 24584 | tf_op jit(solution)/shard_map/ppermute | solution.py:494
  124.6 2.1 %collective-permute-start.17 = (f32[16,128]{1,0:T(8,128)S(1)}, f32[16,128]{1,0:T(8,128)S(1)}, u32[]{:S(2)}, u32[]{:S(2)}) collective-permute-start(f32[16,128]{1,0:T(8,128)S(1)} %get-tuple-element.37), channel_id=1, source_target_pairs={{0,3},{1,0},{2,1},{3,2},{4,7},{5,4},{6,5},{7,6},{8,11},{9,8},{10,9... | collective-permute-start | bytes 24584 | tf_op jit(solution)/shard_map/ppermute | solution.py:494
  126.7 9.2 %collective-permute-start.18 = (f32[7,16,256]{2,1,0:T(8,128)S(1)}, f32[7,16,256]{2,1,0:T(8,128)S(1)}, u32[]{:S(2)}, u32[]{:S(2)}) collective-permute-start(f32[7,16,256]{2,1,0:T(8,128)S(1)} %get-tuple-element.62), channel_id=1, source_target_pairs={{0,4},{4,8},{8,12},{12,16},{16,20},{20,24},{24,28},{28,0},{1,5},{5... | collective-permute-start | bytes 344072 | tf_op jit(solution)/shard_map/ppermute | solution.py:494
  126.8 9.1 %collective-permute-start.19 = (f32[7,16,256]{2,1,0:T(8,128)S(1)}, f32[7,16,256]{2,1,0:T(8,128)S(1)}, u32[]{:S(2)}, u32[]{:S(2)}) collective-permute-start(f32[7,16,256]{2,1,0:T(8,128)S(1)} %get-tuple-element.61), channel_id=1, source_target_pairs={{0,28},{4,0},{8,4},{12,8},{16,12},{20,16},{24,20},{28,24},{1,29},{... | collective-permute-start | bytes 344072 | tf_op jit(solution)/shard_map/ppermute | solution.py:494
  138.4 3.1 %collective-permute-start.20 = (f32[8,128]{1,0:T(8,128)S(1)}, f32[8,128]{1,0:T(8,128)S(1)}, u32[]{:S(2)}, u32[]{:S(2)}) collective-permute-start(f32[8,128]{1,0:T(8,128)S(1)} %get-tuple-element.39), channel_id=1, source_target_pairs={{0,1},{1,2},{2,3},{3,0},{4,5},{5,6},{6,7},{7,4},{8,9},{9,10},{10,1... | collective-permute-start | bytes 12296 | tf_op jit(solution)/shard_map/ppermute | solution.py:494
  139.5 2.1 %collective-permute-start.21 = (f32[8,128]{1,0:T(8,128)S(1)}, f32[8,128]{1,0:T(8,128)S(1)}, u32[]{:S(2)}, u32[]{:S(2)}) collective-permute-start(f32[8,128]{1,0:T(8,128)S(1)} %get-tuple-element.40), channel_id=1, source_target_pairs={{0,3},{1,0},{2,1},{3,2},{4,7},{5,4},{6,5},{7,6},{8,11},{9,8},{10,9... | collective-permute-start | bytes 12296 | tf_op jit(solution)/shard_map/ppermute | solution.py:494
  141.5 14.8 %collective-permute-start.22 = (f32[4,8,256]{2,1,0:T(8,128)S(1)}, f32[4,8,256]{2,1,0:T(8,128)S(1)}, u32[]{:S(2)}, u32[]{:S(2)}) collective-permute-start(f32[4,8,256]{2,1,0:T(8,128)S(1)} %get-tuple-element.66), channel_id=1, source_target_pairs={{0,4},{4,8},{8,12},{12,16},{16,20},{20,24},{24,28},{28,0},{1,5},{5... | collective-permute-start | bytes 98312 | tf_op jit(solution)/shard_map/ppermute | solution.py:494
  141.6 14.7 %collective-permute-start.23 = (f32[4,8,256]{2,1,0:T(8,128)S(1)}, f32[4,8,256]{2,1,0:T(8,128)S(1)}, u32[]{:S(2)}, u32[]{:S(2)}) collective-permute-start(f32[4,8,256]{2,1,0:T(8,128)S(1)} %get-tuple-element.65), channel_id=1, source_target_pairs={{0,28},{4,0},{8,4},{12,8},{16,12},{20,16},{24,20},{28,24},{1,29},{... | collective-permute-start | bytes 98312 | tf_op jit(solution)/shard_map/ppermute | solution.py:494
  (5 other events, 12.8 us)
where the time goes:
time: 182 us
  Pallas kernels  114 us (63%)
  starting transfers between devices  40.8 us (22%)
  blocking collectives  14.2 us (8%)
  waiting for transfers between devices  9.65 us (5%)
  local copies, waits for them, and re-layouts  2.9 us (2%)
    pallas_call x6, Pallas kernels, own_part(): pl.pallas_call(kernel, out_shape=jax.ShapeDtypeStruct((columns, outs, lim...  69.3 us
    ppermute x24, starting transfers between devices, pass_on(): lax.ppermute(value, axis, [(i, (i + step) % count) for i in range(count)])  40.8 us
    pallas_call x3, Pallas kernels, force_rest(): pl.pallas_call(kernel, out_shape=outs, in_specs=[VMEM] * n_in, out_specs=...  26.5 us
    all_to_all x1, blocking collectives, shards(): lax.all_to_all(lists, 'sub', split_axis=0, concat_axis=0, tiled=True)  14.2 us
    pallas_call x3, Pallas kernels, density_rest(): pl.pallas_call(kernel, out_shape=(jax.ShapeDtypeStruct((columns, PRESSURE...  12.4 us
    ppermute x24, waiting for transfers between devices, pass_on(): lax.ppermute(value, axis, [(i, (i + step) % count) for i in range(count)])  9.65 us
    pallas_call x1, Pallas kernels, compact(): pl.pallas_call(kernel, out_shape=jax.ShapeDtypeStruct((parts, 8, capacity...  4.57 us
  transfers between devices with their start and end apart: 24, of which 9 were waited for; matrix products, arithmetic and copies ran while one was open for 0% of the time, Pallas kernels for 39%

commit v1 on v0

--- a/solution.py
+++ b/solution.py
@@ -26,7 +26,7 @@
 
 
 def cost(pairs, ops):
-    return pl.CostEstimate(flops=int(pairs * ops), bytes_accessed=1 << 20, transcendentals=0)
+    return pl.CostEstimate(flops=int(pairs * ops * 140), bytes_accessed=1 << 20, transcendentals=0)
 
 
 def pair_force(own, their, total):
@@ -64,49 +64,49 @@
 )
 
 
-def store_shifted(shifted, col, row, lo, hi, blocks, left, right, is_y):
-    lane = lane_of(blocks[0].shape)
-    up = [pltpu.roll(v, 1, 1) for v in [left] + blocks]
-    down = [pltpu.roll(v, LANES - 1, 1) for v in blocks + [right]]
-    for b, block in enumerate(blocks):
-        before = jnp.where(lane == 0, up[b], up[b + 1])
-        after = jnp.where(lane == LANES - 1, down[b + 1], down[b])
-        for s, value in zip(SHIFTS, (before, block, after)):
-            if is_y and s:
-                value = value + float(s)
-            shifted[col, s + 1, b, row, lo:hi, :] = value
-
-
-def fill_shifted(shifted, col, row, pieces, field, scale, group):
+def fill_shifted(shifted, col, row, pieces, field, scale, group, shifts, is_y):
     for cells, left, right, lo, hi in pieces:
         count = cells.shape[-1] // LANES
         blocks = [cells[field, lo:hi, b * LANES : (b + 1) * LANES] for b in range(count)]
-        left_end = pltpu.roll(left[lo:hi, :], LANES - 1 - group, 1)
-        right_end = right[lo:hi, :]
-        if group:
-            right_end = pltpu.roll(right_end, LANES - group, 1)
         if scale != 1.0:
             blocks = [v * scale for v in blocks]
-            left_end, right_end = left_end * scale, right_end * scale
-        store_shifted(shifted, col, row, lo, hi, blocks, left_end, right_end, field == 1 and scale == 1.0 and row == 1)
-
-
-def fill_column(shifted, col, kind, motion, pressure, group_of):
+        lane = lane_of(blocks[0].shape)
+        for at, shift in enumerate(shifts):
+            values = blocks
+            if shift == -1:
+                turned = [pltpu.roll(v, 1, 1) for v in blocks]
+                end = pltpu.roll(left[lo:hi, :], (LANES - group) % LANES, 1) if group else left[lo:hi, :]
+                turned = [end if scale == 1.0 else end * scale] + turned
+                values = [jnp.where(lane == 0, turned[b], turned[b + 1]) for b in range(count)]
+            elif shift == 1:
+                turned = [pltpu.roll(v, LANES - 1, 1) for v in blocks]
+                end = pltpu.roll(right[lo:hi, :], LANES - 1 - group, 1)
+                turned.append(end if scale == 1.0 else end * scale)
+                values = [jnp.where(lane == LANES - 1, turned[b + 1], turned[b]) for b in range(count)]
+            if is_y and shift:
+                values = [v + float(shift) for v in values]
+            for b in range(count):
+                shifted[col, at, b, row, lo:hi, :] = values[b]
+
+
+def fill_column(shifted, col, kind, motion, pressure, group_of, shifts):
     moved, pressed, massed, _, _ = kind
     row = 0
-    for pieces, fields, width in ((motion, moved, MOTION), (pressure, pressed, PRESSURE), (motion, massed, MOTION)):
+    for pieces, fields in ((motion, moved), (pressure, pressed), (motion, massed)):
         for field, scale in fields:
-            fill_shifted(shifted, col, row, pieces(field), field, scale, group_of(field))
+            is_y = fields is moved and field == 1
+            fill_shifted(shifted, col, row, pieces(field), field, scale, group_of(field), shifts, is_y)
             row += 1
 
 
-def add_pairs(kind, motion_ref, pressure_ref, shifted, x, sources, limit, first, last, fold):
+def add_pairs(kind, motion_ref, pressure_ref, shifted, x, sources, limit, first, last):
     moved, pressed, _, pair, width = kind
     slots = shifted.shape[-2]
     blocks = shifted.shape[2]
     rows = shifted.shape[3]
     group = min(limit // ROWS, 2 if width == 3 else 4)
-    unroll = 4 if group > 1 else 8
+    unroll = min(slots, 16 // group if width == 3 else 32 // group)
+    forms = shifted.shape[1]
     low_col, low_shift = sources[0]
 
     def lane_block(b, carry):
@@ -120,8 +120,8 @@
                 own.append(values)
 
             def source(at, totals):
-                col = at // 3
-                shift = at - 3 * col
+                col = at // forms
+                shift = at - forms * col
                 offset = (col + low_shift).astype(jnp.float32)
                 mine = [[v[0] - offset] + v[1:] for v in own]
 
@@ -140,7 +140,7 @@
                 return lax.fori_loop(0, slots // unroll, step, totals)
 
             totals = tuple(first(x, span, lanes) for span in spans)
-            totals = lax.fori_loop(0, 3 * len(sources), source, totals)
+            totals = lax.fori_loop(0, forms * len(sources), source, totals)
             for span, total in zip(spans, totals):
                 last(x, span, lanes, total)
         return carry
@@ -194,14 +194,18 @@
     return spans
 
 
-def own_part(kind, motion, pressure, ends_m, ends_p, limit):
+def own_part(kind, motion, pressure, ends_m, ends_p, limit, shifts, partial=None):
     columns, _, slots, width = motion.shape
     moved, pressed, massed, _, outs = kind
+    inner = shifts == (0,)
+    if inner:
+        ends_m = ends_p = []
     flat_m = [e for pair in ends_m for e in pair]
     flat_p = [e for pair in ends_p for e in pair]
-    spans_m = bounds_of([e[0] for e in ends_m], 0)
-    spans_p = bounds_of([e[0] for e in ends_p], 0)
-    inputs = [motion] + ([pressure] if pressed else []) + flat_m + flat_p
+    whole = [(0, 0, slots)]
+    spans_m = whole if inner else bounds_of([e[0] for e in ends_m], 0)
+    spans_p = whole if inner else bounds_of([e[0] for e in ends_p], 0)
+    inputs = [motion] + ([pressure] if pressed else []) + flat_m + flat_p + ([] if partial is None else [partial])
     rows = len(moved) + len(pressed) + len(massed)
 
     def kernel(*refs):
@@ -210,59 +214,79 @@
         pressure_ref = refs.pop(0) if pressed else None
         m_refs = refs[: len(flat_m)]
         p_refs = refs[len(flat_m) : len(flat_m) + len(flat_p)]
+        partial_ref = None if partial is None else refs[-3]
         out_ref, shifted = refs[-2:]
+
+        def pieces(cells, ends, spans):
+            if inner:
+                return [(cells, None, None, 0, slots)]
+            return [(cells, ends[2 * i], ends[2 * i + 1], lo, hi) for i, lo, hi in spans]
+
         for c in range(columns):
 
             def motion_pieces(field):
-                spans = spans_m if field < 6 else [(len(ends_m) - 1, 0, slots)]
-                return [(motion_ref.at[c], m_refs[2 * i], m_refs[2 * i + 1], lo, hi) for i, lo, hi in spans]
+                return pieces(motion_ref.at[c], m_refs, spans_m if field < 6 else [(len(ends_m) - 1, 0, slots)])
 
             def pressure_pieces(field):
-                return [(pressure_ref.at[c], p_refs[2 * i], p_refs[2 * i + 1], lo, hi) for i, lo, hi in spans_p]
-
-            fill_column(shifted, c, kind, motion_pieces, pressure_pieces, lambda f: f * columns + c)
+                return pieces(pressure_ref.at[c], p_refs, spans_p)
+
+            fill_column(shifted, c, kind, motion_pieces, pressure_pieces, lambda f: f * columns + c, shifts)
         zero = jnp.zeros((ROWS, LANES), jnp.float32)
+
+        def first(x, span, lanes):
+            if partial is None:
+                return (zero,) * outs
+            return tuple(partial_ref[x, k, span, lanes] for k in range(outs))
 
         def last(x, span, lanes, total):
             for k in range(outs):
                 out_ref[x, k, span, lanes] = total[k]
 
         for x in range(columns):
-            add_pairs(kind, motion_ref, pressure_ref, shifted, x, own_sources(x, columns), limit, lambda *_: (zero,) * outs, last, None)
+            add_pairs(kind, motion_ref, pressure_ref, shifted, x, own_sources(x, columns), limit, first, last)
 
     return pl.pallas_call(
         kernel,
         out_shape=jax.ShapeDtypeStruct((columns, outs, limit, width), jnp.float32),
         in_specs=[VMEM] * len(inputs),
         out_specs=VMEM,
-        scratch_shapes=[pltpu.VMEM((columns, 3, width // LANES, rows, slots, LANES), jnp.float32)],
+        scratch_shapes=[pltpu.VMEM((columns, len(shifts), width // LANES, rows, slots, LANES), jnp.float32)],
         compiler_params=PARAMS,
-        cost_estimate=cost(limit * slots * 3 * (3 * columns - 2) * width, 60 if outs == 3 else 30),
+        cost_estimate=cost(limit * slots * len(shifts) * (3 * columns - 2) * width, 60 if outs == 3 else 30),
     )(*inputs)
 
 
-def halo_sums(kind, refs, columns, slots, counts, limit, out_first, out_last, motion_ref, pressure_ref, shifted):
-    moved, pressed, massed, _, outs = kind
+def halo_sums(kind, refs, columns, slots, limit, first, last, motion_ref, pressure_ref, shifted):
     for side in range(2):
         m_refs, p_refs = refs[side]
         column = columns - 1 if side == 0 else 0
-        spans_m = bounds_of(m_refs, 1)
-        spans_p = bounds_of(p_refs, 1)
+        spans_m = bounds_of([ends for _, ends in m_refs], 0)
+        spans_p = bounds_of([ends for _, ends in p_refs], 0)
 
         def pieces(history, spans):
             out = []
             for i, lo, hi in spans:
-                ref = history[i]
-                plane = ref.shape[0] - 1
-                out.append((ref, ref.at[plane, :, 0:LANES], ref.at[plane, :, LANES : 2 * LANES], lo, hi))
+                cells, ends = history[i]
+                out.append((cells, ends.at[:, 0:LANES], ends.at[:, LANES : 2 * LANES], lo, hi))
             return out
 
         def motion_pieces(field):
             return pieces(m_refs, spans_m if field < 6 else [(len(m_refs) - 1, 0, slots)])
 
-        fill_column(shifted, side, kind, motion_pieces, lambda f: pieces(p_refs, spans_p), lambda f: f * columns + column)
+        def pressure_pieces(field):
+            return pieces(p_refs, spans_p)
+
+        fill_column(shifted, side, kind, motion_pieces, pressure_pieces, lambda f: f * columns + column, SHIFTS)
         x, shift = (0, -1) if side == 0 else (columns - 1, 1)
-        add_pairs(kind, motion_ref, pressure_ref, shifted, x, [(side, shift)], limit, out_first[side], out_last[side], None)
+        add_pairs(kind, motion_ref, pressure_ref, shifted, x, [(side, shift)], limit, first, last)
+
+
+def paired(refs):
+    return [(refs[i], refs[i + 1]) for i in range(0, len(refs), 2)]
+
+
+def with_own_ends(refs):
+    return [(ref, ref.at[ref.shape[0] - 1]) for ref in refs]
 
 
 def density_rest(motion, partial, messages, density, entropy, counts, level, limit, slots_sent):
@@ -286,10 +310,8 @@
         def end(x, span, lanes, total):
             sums[x, 0, span, lanes] = total[0]
 
-        halo_sums(
-            DENSITY, ((m_refs[:n_m], ()), (m_refs[n_m:], ())), columns, slots, counts_ref, limit,
-            (start, start), (end, end), motion_ref, None, shifted,
-        )
+        sides = ((paired(m_refs[:n_m]), []), (paired(m_refs[n_m:]), []))
+        halo_sums(DENSITY, sides, columns, slots, limit, start, end, motion_ref, None, shifted)
         for x in range(columns):
             count = counts_ref[level, x : x + 1, :]
             for lo in range(0, slots, ROWS):
@@ -340,7 +362,7 @@
         sides = []
         for side in range(2):
             at = 4 + side * (n_m + n_p)
-            sides.append((refs[at : at + n_m], refs[at + n_m : at + n_m + n_p]))
+            sides.append((paired(refs[at : at + n_m]), with_own_ends(refs[at + n_m : at + n_m + n_p])))
         new_ref = refs[n_in]
         shifted, sums = refs[-2:]
         sums[...] = partial_ref[...]
@@ -352,7 +374,7 @@
             for k in range(3):
                 sums[x, k, span, lanes] = total[k]
 
-        halo_sums(FORCE, sides, columns, slots, counts_ref, limit, (start, start), (end, end), motion_ref, pressure_ref, shifted)
+        halo_sums(FORCE, sides, columns, slots, limit, start, end, motion_ref, pressure_ref, shifted)
         for x in range(columns):
             count = counts_ref[level, x : x + 1, :]
             new_ref[x, 6, :, :] = motion_ref[x, 6, :, :]
@@ -498,13 +520,13 @@
     return pass_on(right_ends, "sub", 1), pass_on(left_ends, "sub", -1)
 
 
-def swap_columns(cells, fields, limit, ends):
-    width = cells.shape[-1]
+def swap_columns(first, final):
+    return pass_on(final, "tile", 1), pass_on(first, "tile", -1)
+
+
+def beside(ends, width):
     plane = jnp.concatenate(ends, axis=1)
-    plane = jnp.pad(plane, ((0, 0), (0, width - plane.shape[1])))[None]
-    first = jnp.concatenate([cells[0, :fields, :limit], plane], axis=0)
-    final = jnp.concatenate([cells[-1, :fields, :limit], plane], axis=0)
-    return pass_on(final, "tile", 1), pass_on(first, "tile", -1)
+    return jnp.pad(plane, ((0, 0), (0, width - plane.shape[1])))
 
 
 def shards(offsets, velocity, mass, entropy, active_counts, targets):
@@ -525,17 +547,24 @@
         limit = limits[level]
         sent = limits[max(level - 1, 0)]
         fields = MOTION if level == 0 else 6
+        cells = swap_columns(motion[0, :fields, :sent], motion[-1, :fields, :sent])
         ends_m.insert(0, swap_ends(*made))
-        from_left, from_right = swap_columns(motion, fields, sent, ends_m[0])
-        left_m.insert(0, from_left)
-        right_m.insert(0, from_right)
-        partial = own_part(DENSITY, motion, None, ends_m, [], limit)
+        partial = own_part(DENSITY, motion, None, ends_m, [], limit, (0,))
+        plane = beside(ends_m[0], width)
+        corners = swap_columns(plane, plane)
+        partial = own_part(DENSITY, motion, None, ends_m, [], limit, (-1, 1), partial)
+        left_m[:0] = [cells[0], corners[0]]
+        right_m[:0] = [cells[1], corners[1]]
         pressure, *made = density_rest(motion, partial, (left_m, right_m), pressure, entropy, active_counts, level, limit, limit)
         ends_p.insert(0, swap_ends(*made))
-        from_left, from_right = swap_columns(pressure, PRESSURE, limit, ends_p[0])
-        left_p.insert(0, from_left)
-        right_p.insert(0, from_right)
-        partial = own_part(FORCE, motion, pressure, ends_m, ends_p, limit)
+        partial = own_part(FORCE, motion, pressure, ends_m, ends_p, limit, (0,))
+        plane = beside(ends_p[0], width)[None]
+        first = jnp.concatenate([pressure[0, :, :limit], plane], axis=0)
+        final = jnp.concatenate([pressure[-1, :, :limit], plane], axis=0)
+        cells = swap_columns(first, final)
+        left_p.insert(0, cells[0])
+        right_p.insert(0, cells[1])
+        partial = own_part(FORCE, motion, pressure, ends_m, ends_p, limit, (-1, 1), partial)
         more = limit if level < levels - 1 else 0
         motion, *made = force_rest(
             motion, pressure, partial, (left_m, right_m), (left_p, right_p), active_counts, level, limit, more

time: 182 us -> 167 us (0.918)
  Pallas kernels: 114 us -> 93.2 us
  starting transfers between devices: 40.8 us -> 55 us
  waiting for transfers between devices: 9.65 us -> 0.08 us
    ppermute x24 -> x30, starting transfers between devices: 40.8 us -> 55 us  [pass_on(): lax.ppermute(value, axis, [(i, (i + step) % count) for i in range(count)])]
    pallas_call x6 -> x12, Pallas kernels: 69.3 us -> 56.5 us  [own_part(): pl.pallas_call(kernel, out_shape=jax.ShapeDtypeStruct((columns, outs, lim...]
    ppermute x24 -> x30, waiting for transfers between devices: 9.65 us -> 0.08 us  [pass_on(): lax.ppermute(value, axis, [(i, (i + step) % count) for i in range(count)])]
    pallas_call x3, Pallas kernels: 26.5 us -> 21.2 us  [force_rest(): pl.pallas_call(kernel, out_shape=outs, in_specs=[VMEM] * n_in, out_specs=...]
    pallas_call x3, Pallas kernels: 12.4 us -> 9.95 us  [density_rest(): pl.pallas_call(kernel, out_shape=(jax.ShapeDtypeStruct((columns, PRESSURE...]
  transfers between devices with their start and end apart: 24 -> 30, of which waited for: 9 -> 0; matrix products, arithmetic and copies ran while one was open for 0% -> 0% of each run, Pallas kernels for 39% -> 34%
where the time goes in v1:
time: 167 us
  Pallas kernels  93.2 us (56%)
  starting transfers between devices  55 us (33%)
  blocking collectives  14.3 us (9%)
  local copies, waits for them, and re-layouts  3.74 us (2%)
    pallas_call x12, Pallas kernels, own_part(): pl.pallas_call(kernel, out_shape=jax.ShapeDtypeStruct((columns, outs, lim...  56.5 us
    ppermute x30, starting transfers between devices, pass_on(): lax.ppermute(value, axis, [(i, (i + step) % count) for i in range(count)])  55 us
    pallas_call x3, Pallas kernels, force_rest(): pl.pallas_call(kernel, out_shape=outs, in_specs=[VMEM] * n_in, out_specs=...  21.2 us
    all_to_all x1, blocking collectives, shards(): lax.all_to_all(lists, 'sub', split_axis=0, concat_axis=0, tiled=True)  14.3 us
    pallas_call x3, Pallas kernels, density_rest(): pl.pallas_call(kernel, out_shape=(jax.ShapeDtypeStruct((columns, PRESSURE...  9.95 us
    pallas_call x1, Pallas kernels, compact(): pl.pallas_call(kernel, out_shape=jax.ShapeDtypeStruct((parts, 8, capacity...  4.57 us
    unnamed x17, local copies, waits for them, and re-layouts  3.58 us
  transfers between devices with their start and end apart: 30, of which 0 were waited for; matrix products, arithmetic and copies ran while one was open for 0% of the time, Pallas kernels for 34%

profile of v1, /device:TPU:0, one launch (start us, length us, event | category | flops | bytes accessed | tf_op | source)
XLA Modules:
  0.0 167.0 jit_solution(6916097071103187777)
XLA Ops:
  7.0 3.1 %collective-permute-start.4 = (f32[7,32,256]{2,1,0:T(8,128)S(1)}, f32[7,32,256]{2,1,0:T(8,128)S(1)}, u32[]{:S(2)}, u32[]{:S(2)}) collective-permute-start(f32[7,32,256]{2,1,0:T(8,128)S(1)} %get-tuple-element.47), channel_id=1, source_target_pairs={{0,28},{4,0},{8,4},{12,8},{16,12},{20,16},{24,20},{28,24},{1,29},{... | collective-permute-start | bytes 688136 | tf_op jit(solution)/shard_map/ppermute | solution.py:516
  10.1 3.1 %shard_map.65.refs_3_ = f32[2,1,32,256]{3,2,1,0:T(8,128)S(1)} custom-call(f32[2,7,32,256]{3,2,1,0:T(8,128)S(1)} %maximum_bitcast_fusion.motion_ref.refs_0_), custom_call_target="tpu_custom_call" | custom-call | flops 4404019200 | bytes 1048576 | tf_op jit(solution)/shard_map/pallas_call | solution.py:248
  15.1 4.7 %collective-permute-start.5 = (f32[32,256]{1,0:T(8,128)S(1)}, f32[32,256]{1,0:T(8,128)S(1)}, u32[]{:S(2)}, u32[]{:S(2)}) collective-permute-start(f32[32,256]{1,0:T(8,128)S(1)} %constant_dynamic-update-slice_fusion), channel_id=1, source_target_pairs={{0,28},{4,0},{8,4},{12,8},{16,12},{20,16},{24,20},{28,24},{1,29},{... | collective-permute-start | bytes 98312 | tf_op jit(solution)/shard_map/ppermute | solution.py:516
  19.8 6.6 %shard_map.66.refs_1_ = f32[2,1,32,256]{3,2,1,0:T(8,128)S(1)} custom-call(f32[2,7,32,256]{3,2,1,0:T(8,128)S(1)} %maximum_bitcast_fusion.motion_ref.refs_0_, f32[32,128]{1,0:T(8,128)S(1)} %collective-permute-done.refs_1_.refs_2_.refs_3_.refs_4_.refs_5_.refs_6_, f32[32,128]{1,0:T(8,128)S(1)} %collective-permute-done.1.refs_2_.refs_3_.refs_4_.refs_5_.refs_6_.refs_7_, ...), custom_call_target="tpu_custom_call" | custom-call | flops 8808038400 | bytes 1048576 | tf_op jit(solution)/shard_map/pallas_call | solution.py:248
  26.4 5.2 %shard_map.67 = (f32[2,3,32,256]{3,2,1,0:T(8,128)S(1)}, f32[32,128]{1,0:T(8,128)S(1)}, f32[32,128]{1,0:T(8,128)S(1)}) custom-call(f32[2,7,32,256]{3,2,1,0:T(8,128)S(1)} %maximum_bitcast_fusion.motion_ref.refs_0_, f32[2,1,32,256]{3,2,1,0:T(8,128)S(1)} %shard_map.66.refs_1_, f32[2,32,256]{2,1,0:T(8,128)S(1)} %bitcast.43, s32[3,2,256]{2,1,0:T(2,128)S(1)} %copy-done, ...), custom_call_target="tpu_custom_call" | custom-call | flops 6606028800 | bytes 1048576 | tf_op jit(solution)/shard_map/pallas_call | solution.py:337
  33.5 7.1 %shard_map.68.refs_6_ = f32[2,3,32,256]{3,2,1,0:T(8,128)S(1)} custom-call(f32[2,7,32,256]{3,2,1,0:T(8,128)S(1)} %maximum_bitcast_fusion.motion_ref.refs_0_, f32[2,3,32,256]{3,2,1,0:T(8,128)S(1)} %get-tuple-element.26.refs_1_.refs_4_), custom_call_target="tpu_custom_call" | custom-call | flops 8808038400 | bytes 1048576 | tf_op jit(solution)/shard_map/pallas_call | solution.py:248
  40.7 4.7 %collective-permute-start.9 = (f32[4,32,256]{2,1,0:T(8,128)S(1)}, f32[4,32,256]{2,1,0:T(8,128)S(1)}, u32[]{:S(2)}, u32[]{:S(2)}) collective-permute-start(f32[4,32,256]{2,1,0:T(8,128)S(1)} %get-tuple-element.55), channel_id=1, source_target_pairs={{0,28},{4,0},{8,4},{12,8},{16,12},{20,16},{24,20},{28,24},{1,29},{... | collective-permute-start | bytes 393224 | tf_op jit(solution)/shard_map/ppermute | solution.py:516
  45.4 14.7 %shard_map.69.refs_2_ = f32[2,3,32,256]{3,2,1,0:T(8,128)S(1)} custom-call(f32[2,7,32,256]{3,2,1,0:T(8,128)S(1)} %maximum_bitcast_fusion.motion_ref.refs_0_, f32[2,3,32,256]{3,2,1,0:T(8,128)S(1)} %get-tuple-element.26.refs_1_.refs_4_, f32[32,128]{1,0:T(8,128)S(1)} %collective-permute-done.refs_1_.refs_2_.refs_3_.refs_4_.refs_5_.refs_6_, ...), custom_call_target="tpu_custom_call" | custom-call | flops 17616076800 | bytes 1048576 | tf_op jit(solution)/shard_map/pallas_call | solution.py:248
  60.1 11.6 %shard_map.70 = (f32[2,7,32,256]{3,2,1,0:T(8,128)S(1)}, f32[32,128]{1,0:T(8,128)S(1)}, f32[32,128]{1,0:T(8,128)S(1)}) custom-call(f32[2,7,32,256]{3,2,1,0:T(8,128)S(1)} %maximum_bitcast_fusion.motion_ref.refs_0_, f32[2,3,32,256]{3,2,1,0:T(8,128)S(1)} %get-tuple-element.26.refs_1_.refs_4_, f32[2,3,32,256]{3,2,1,0:T(8,128)S(1)} %shard_map.69.refs_2_, ...), custom_call_target="tpu_custom_call" | custom-call | flops 13212057600 | bytes 1048576 | tf_op jit(solution)/shard_map/pallas_call | solution.py:396
  75.2 4.7 %collective-permute-start.14 = (f32[6,32,256]{2,1,0:T(8,128)S(1)}, f32[6,32,256]{2,1,0:T(8,128)S(1)}, u32[]{:S(2)}, u32[]{:S(2)}) collective-permute-start(f32[6,32,256]{2,1,0:T(8,128)S(1)} %get-tuple-element.45), channel_id=1, source_target_pairs={{0,28},{4,0},{8,4},{12,8},{16,12},{20,16},{24,20},{28,24},{1,29},{... | collective-permute-start | bytes 589832 | tf_op jit(solution)/shard_map/ppermute | solution.py:516
  80.0 4.7 %collective-permute-start.15 = (f32[32,256]{1,0:T(8,128)S(1)}, f32[32,256]{1,0:T(8,128)S(1)}, u32[]{:S(2)}, u32[]{:S(2)}) collective-permute-start(f32[32,256]{1,0:T(8,128)S(1)} %constant_dynamic-update-slice_fusion.2), channel_id=1, source_target_pairs={{0,28},{4,0},{8,4},{12,8},{16,12},{20,16},{24,20},{28,24},{1,29},{... | collective-permute-start | bytes 98312 | tf_op jit(solution)/shard_map/ppermute | solution.py:516
  84.7 3.4 %shard_map.72.refs_1_ = f32[2,1,16,256]{3,2,1,0:T(8,128)S(1)} custom-call(f32[2,7,32,256]{3,2,1,0:T(8,128)S(1)} %get-tuple-element.29.refs_0_, f32[32,128]{1,0:T(8,128)S(1)} %collective-permute-done.10.refs_1_.refs_2_.refs_3_.refs_4_, f32[32,128]{1,0:T(8,128)S(1)} %collective-permute-done.11.refs_2_.refs_3_.refs_4_.refs_5_, ...), custom_call_target="tpu_custom_call" | custom-call | flops 4404019200 | bytes 1048576 | tf_op jit(solution)/shard_map/pallas_call | solution.py:248
  88.2 3.0 %shard_map.73 = (f32[2,3,32,256]{3,2,1,0:T(8,128)S(1)}, f32[16,128]{1,0:T(8,128)S(1)}, f32[16,128]{1,0:T(8,128)S(1)}) custom-call(f32[2,7,32,256]{3,2,1,0:T(8,128)S(1)} %get-tuple-element.29.refs_0_, f32[2,1,16,256]{3,2,1,0:T(8,128)S(1)} %shard_map.72.refs_1_, f32[2,32,256]{2,1,0:T(8,128)S(1)} %bitcast.44, s32[3,2,256]{2,1,0:T(2,128)S(1)} %copy-done, ...), custom_call_target="tpu_custom_call" | custom-call | flops 3303014400 | bytes 1048576 | tf_op jit(solution)/shard_map/pallas_call | solution.py:337
  93.0 3.6 %shard_map.74.refs_10_ = f32[2,3,16,256]{3,2,1,0:T(8,128)S(1)} custom-call(f32[2,7,32,256]{3,2,1,0:T(8,128)S(1)} %get-tuple-element.29.refs_0_, f32[2,3,32,256]{3,2,1,0:T(8,128)S(1)} %get-tuple-element.32.refs_1_.refs_4_), custom_call_target="tpu_custom_call" | custom-call | flops 4404019200 | bytes 1048576 | tf_op jit(solution)/shard_map/pallas_call | solution.py:248
  96.7 4.7 %collective-permute-start.19 = (f32[4,16,256]{2,1,0:T(8,128)S(1)}, f32[4,16,256]{2,1,0:T(8,128)S(1)}, u32[]{:S(2)}, u32[]{:S(2)}) collective-permute-start(f32[4,16,256]{2,1,0:T(8,128)S(1)} %get-tuple-element.57), channel_id=1, source_target_pairs={{0,28},{4,0},{8,4},{12,8},{16,12},{20,16},{24,20},{28,24},{1,29},{... | collective-permute-start | bytes 196616 | tf_op jit(solution)/shard_map/ppermute | solution.py:516
  101.4 7.7 %shard_map.75.refs_2_ = f32[2,3,16,256]{3,2,1,0:T(8,128)S(1)} custom-call(f32[2,7,32,256]{3,2,1,0:T(8,128)S(1)} %get-tuple-element.29.refs_0_, f32[2,3,32,256]{3,2,1,0:T(8,128)S(1)} %get-tuple-element.32.refs_1_.refs_4_, f32[32,128]{1,0:T(8,128)S(1)} %collective-permute-done.10.refs_1_.refs_2_.refs_3_.refs_4_, ...), custom_call_target="tpu_custom_call" | custom-call | flops 8808038400 | bytes 1048576 | tf_op jit(solution)/shard_map/pallas_call | solution.py:248
  109.1 6.2 %shard_map.76 = (f32[2,7,32,256]{3,2,1,0:T(8,128)S(1)}, f32[16,128]{1,0:T(8,128)S(1)}, f32[16,128]{1,0:T(8,128)S(1)}) custom-call(f32[2,7,32,256]{3,2,1,0:T(8,128)S(1)} %get-tuple-element.29.refs_0_, f32[2,3,32,256]{3,2,1,0:T(8,128)S(1)} %get-tuple-element.32.refs_1_.refs_4_, f32[2,3,16,256]{3,2,1,0:T(8,128)S(1)} %shard_map.75.refs_2_, ...), custom_call_target="tpu_custom_call" | custom-call | flops 6606028800 | bytes 1048576 | tf_op jit(solution)/shard_map/pallas_call | solution.py:396
  117.9 4.7 %collective-permute-start.24 = (f32[6,16,256]{2,1,0:T(8,128)S(1)}, f32[6,16,256]{2,1,0:T(8,128)S(1)}, u32[]{:S(2)}, u32[]{:S(2)}) collective-permute-start(f32[6,16,256]{2,1,0:T(8,128)S(1)} %get-tuple-element.43), channel_id=1, source_target_pairs={{0,28},{4,0},{8,4},{12,8},{16,12},{20,16},{24,20},{28,24},{1,29},{... | collective-permute-start | bytes 294920 | tf_op jit(solution)/shard_map/ppermute | solution.py:516
  122.7 4.7 %collective-permute-start.25 = (f32[16,256]{1,0:T(8,128)S(1)}, f32[16,256]{1,0:T(8,128)S(1)}, u32[]{:S(2)}, u32[]{:S(2)}) collective-permute-start(f32[16,256]{1,0:T(8,128)S(1)} %constant_dynamic-update-slice_fusion.4), channel_id=1, source_target_pairs={{0,28},{4,0},{8,4},{12,8},{16,12},{20,16},{24,20},{28,24},{1,29},{... | collective-permute-start | bytes 49160 | tf_op jit(solution)/shard_map/ppermute | solution.py:516
  134.9 4.7 %collective-permute-start.29 = (f32[4,8,256]{2,1,0:T(8,128)S(1)}, f32[4,8,256]{2,1,0:T(8,128)S(1)}, u32[]{:S(2)}, u32[]{:S(2)}) collective-permute-start(f32[4,8,256]{2,1,0:T(8,128)S(1)} %get-tuple-element.59), channel_id=1, source_target_pairs={{0,28},{4,0},{8,4},{12,8},{16,12},{20,16},{24,20},{28,24},{1,29},{... | collective-permute-start | bytes 98312 | tf_op jit(solution)/shard_map/ppermute | solution.py:516
  139.7 4.2 %shard_map.81.refs_2_ = f32[2,3,8,256]{3,2,1,0:T(8,128)S(1)} custom-call(f32[2,7,32,256]{3,2,1,0:T(8,128)S(1)} %get-tuple-element.35.refs_0_, f32[2,3,32,256]{3,2,1,0:T(8,128)S(1)} %get-tuple-element.38.refs_1_.pressure_ref, f32[16,128]{1,0:T(8,128)S(1)} %collective-permute-done.20.refs_1_.refs_2_, f32[16,128]{1,0:T(8,128)S(1)} %collective-permute-done.21.refs_2_.refs_3_, ...), custom_call_target="tpu_custom_call" | custom-call | flops 4404019200 | bytes 1048576 | tf_op jit(solution)/shard_map/pallas_call | solution.py:248
  143.9 3.4 %shard_map.82.motion_ref = f32[2,7,32,256]{3,2,1,0:T(8,128)S(1)} custom-call(f32[2,7,32,256]{3,2,1,0:T(8,128)S(1)} %get-tuple-element.35.refs_0_, f32[2,3,32,256]{3,2,1,0:T(8,128)S(1)} %get-tuple-element.38.refs_1_.pressure_ref, f32[2,3,8,256]{3,2,1,0:T(8,128)S(1)} %shard_map.81.refs_2_, s32[3,2,256]{2,1,0:T(2,128)S(1)} %copy-done, ...), custom_call_target="tpu_custom_call" | custom-call | flops 3303014400 | bytes 1048576 | tf_op jit(solution)/shard_map/pallas_call | solution.py:396
  147.3 4.6 %shard_map.84 = f32[4,8,6144]{2,1,0:T(8,128)S(1)} custom-call(f32[2,7,32,256]{3,2,1,0:T(8,128)S(1)} %shard_map.82.motion_ref, f32[2,3,32,256]{3,2,1,0:T(8,128)S(1)} %get-tuple-element.38.refs_1_.pressure_ref, s32[64,256]{1,0:T(8,128)S(1)} %get-tuple-element.41.place_ref, s32[64,12]{1,0:T(8,128)S(1)} %bitcast.46), custom_call_target="tpu_custom_call" | custom-call | tf_op jit(solution)/shard_map/pallas_call | solution.py:501
  151.9 14.3 %all_to_all.5 = f32[4,8,6144]{2,1,0:T(8,128)S(1)} all-to-all(f32[4,8,6144]{2,1,0:T(8,128)S(1)} %shard_map.84), channel_id=1, replica_groups=mesh['tile'=8,'sub'=4] {'sub'}, dimensions={0} | all-to-all | bytes 1572864 | tf_op jit(solution)/shard_map/all_to_all | solution.py:574
  (94 shorter events, 27.1 us)
Async XLA Ops:
  2.1 12.9 %collective-permute-start = (f32[32,128]{1,0:T(8,128)S(1)}, f32[32,128]{1,0:T(8,128)S(1)}, u32[]{:S(2)}, u32[]{:S(2)}) collective-permute-start(f32[32,128]{1,0:T(8,128)S(1)} %get-tuple-element.24), channel_id=1, source_target_pairs={{0,1},{1,2},{2,3},{3,0},{4,5},{5,6},{6,7},{7,4},{8,9},{9,10},{10,1... | collective-permute-start | bytes 49160 | tf_op jit(solution)/shard_map/ppermute | solution.py:516
  2.6 12.4 %collective-permute-start.1 = (f32[32,128]{1,0:T(8,128)S(1)}, f32[32,128]{1,0:T(8,128)S(1)}, u32[]{:S(2)}, u32[]{:S(2)}) collective-permute-start(f32[32,128]{1,0:T(8,128)S(1)} %get-tuple-element.25), channel_id=1, source_target_pairs={{0,3},{1,0},{2,1},{3,2},{4,7},{5,4},{6,5},{7,6},{8,11},{9,8},{10,9... | collective-permute-start | bytes 49160 | tf_op jit(solution)/shard_map/ppermute | solution.py:516
  4.6 21.7 %collective-permute-start.2 = (f32[7,32,256]{2,1,0:T(8,128)S(1)}, f32[7,32,256]{2,1,0:T(8,128)S(1)}, u32[]{:S(2)}, u32[]{:S(2)}) collective-permute-start(f32[7,32,256]{2,1,0:T(8,128)S(1)} %get-tuple-element.48), channel_id=1, source_target_pairs={{0,4},{4,8},{8,12},{12,16},{16,20},{20,24},{24,28},{28,0},{1,5},{5... | collective-permute-start | bytes 688136 | tf_op jit(solution)/shard_map/ppermute | solution.py:516
  7.0 19.4 %collective-permute-start.4 = (f32[7,32,256]{2,1,0:T(8,128)S(1)}, f32[7,32,256]{2,1,0:T(8,128)S(1)}, u32[]{:S(2)}, u32[]{:S(2)}) collective-permute-start(f32[7,32,256]{2,1,0:T(8,128)S(1)} %get-tuple-element.47), channel_id=1, source_target_pairs={{0,28},{4,0},{8,4},{12,8},{16,12},{20,16},{24,20},{28,24},{1,29},{... | collective-permute-start | bytes 688136 | tf_op jit(solution)/shard_map/ppermute | solution.py:516
  15.0 11.3 %collective-permute-start.3 = (f32[32,256]{1,0:T(8,128)S(1)}, f32[32,256]{1,0:T(8,128)S(1)}, u32[]{:S(2)}, u32[]{:S(2)}) collective-permute-start(f32[32,256]{1,0:T(8,128)S(1)} %constant_dynamic-update-slice_fusion), channel_id=1, source_target_pairs={{0,4},{4,8},{8,12},{12,16},{16,20},{20,24},{24,28},{28,0},{1,5},{5... | collective-permute-start | bytes 98312 | tf_op jit(solution)/shard_map/ppermute | solution.py:516
  15.1 11.3 %collective-permute-start.5 = (f32[32,256]{1,0:T(8,128)S(1)}, f32[32,256]{1,0:T(8,128)S(1)}, u32[]{:S(2)}, u32[]{:S(2)}) collective-permute-start(f32[32,256]{1,0:T(8,128)S(1)} %constant_dynamic-update-slice_fusion), channel_id=1, source_target_pairs={{0,28},{4,0},{8,4},{12,8},{16,12},{20,16},{24,20},{28,24},{1,29},{... | collective-permute-start | bytes 98312 | tf_op jit(solution)/shard_map/ppermute | solution.py:516
  31.7 8.9 %collective-permute-start.6 = (f32[32,128]{1,0:T(8,128)S(1)}, f32[32,128]{1,0:T(8,128)S(1)}, u32[]{:S(2)}, u32[]{:S(2)}) collective-permute-start(f32[32,128]{1,0:T(8,128)S(1)} %get-tuple-element.27), channel_id=1, source_target_pairs={{0,1},{1,2},{2,3},{3,0},{4,5},{5,6},{6,7},{7,4},{8,9},{9,10},{10,1... | collective-permute-start | bytes 49160 | tf_op jit(solution)/shard_map/ppermute | solution.py:516
  31.7 8.8 %collective-permute-start.7 = (f32[32,128]{1,0:T(8,128)S(1)}, f32[32,128]{1,0:T(8,128)S(1)}, u32[]{:S(2)}, u32[]{:S(2)}) collective-permute-start(f32[32,128]{1,0:T(8,128)S(1)} %get-tuple-element.28), channel_id=1, source_target_pairs={{0,3},{1,0},{2,1},{3,2},{4,7},{5,4},{6,5},{7,6},{8,11},{9,8},{10,9... | collective-permute-start | bytes 49160 | tf_op jit(solution)/shard_map/ppermute | solution.py:516
  40.6 19.5 %collective-permute-start.8 = (f32[4,32,256]{2,1,0:T(8,128)S(1)}, f32[4,32,256]{2,1,0:T(8,128)S(1)}, u32[]{:S(2)}, u32[]{:S(2)}) collective-permute-start(f32[4,32,256]{2,1,0:T(8,128)S(1)} %get-tuple-element.56), channel_id=1, source_target_pairs={{0,4},{4,8},{8,12},{12,16},{16,20},{20,24},{24,28},{28,0},{1,5},{5... | collective-permute-start | bytes 393224 | tf_op jit(solution)/shard_map/ppermute | solution.py:516
  40.7 19.4 %collective-permute-start.9 = (f32[4,32,256]{2,1,0:T(8,128)S(1)}, f32[4,32,256]{2,1,0:T(8,128)S(1)}, u32[]{:S(2)}, u32[]{:S(2)}) collective-permute-start(f32[4,32,256]{2,1,0:T(8,128)S(1)} %get-tuple-element.55), channel_id=1, source_target_pairs={{0,28},{4,0},{8,4},{12,8},{16,12},{20,16},{24,20},{28,24},{1,29},{... | collective-permute-start | bytes 393224 | tf_op jit(solution)/shard_map/ppermute | solution.py:516
  71.7 8.2 %collective-permute-start.10 = (f32[32,128]{1,0:T(8,128)S(1)}, f32[32,128]{1,0:T(8,128)S(1)}, u32[]{:S(2)}, u32[]{:S(2)}) collective-permute-start(f32[32,128]{1,0:T(8,128)S(1)} %get-tuple-element.30), channel_id=1, source_target_pairs={{0,1},{1,2},{2,3},{3,0},{4,5},{5,6},{6,7},{7,4},{8,9},{9,10},{10,1... | collective-permute-start | bytes 49160 | tf_op jit(solution)/shard_map/ppermute | solution.py:516
  75.2 13.0 %collective-permute-start.12 = (f32[6,32,256]{2,1,0:T(8,128)S(1)}, f32[6,32,256]{2,1,0:T(8,128)S(1)}, u32[]{:S(2)}, u32[]{:S(2)}) collective-permute-start(f32[6,32,256]{2,1,0:T(8,128)S(1)} %get-tuple-element.46), channel_id=1, source_target_pairs={{0,4},{4,8},{8,12},{12,16},{16,20},{20,24},{24,28},{28,0},{1,5},{5... | collective-permute-start | bytes 589832 | tf_op jit(solution)/shard_map/ppermute | solution.py:516
  75.2 13.0 %collective-permute-start.14 = (f32[6,32,256]{2,1,0:T(8,128)S(1)}, f32[6,32,256]{2,1,0:T(8,128)S(1)}, u32[]{:S(2)}, u32[]{:S(2)}) collective-permute-start(f32[6,32,256]{2,1,0:T(8,128)S(1)} %get-tuple-element.45), channel_id=1, source_target_pairs={{0,28},{4,0},{8,4},{12,8},{16,12},{20,16},{24,20},{28,24},{1,29},{... | collective-permute-start | bytes 589832 | tf_op jit(solution)/shard_map/ppermute | solution.py:516
  79.9 8.2 %collective-permute-start.13 = (f32[32,256]{1,0:T(8,128)S(1)}, f32[32,256]{1,0:T(8,128)S(1)}, u32[]{:S(2)}, u32[]{:S(2)}) collective-permute-start(f32[32,256]{1,0:T(8,128)S(1)} %constant_dynamic-update-slice_fusion.2), channel_id=1, source_target_pairs={{0,4},{4,8},{8,12},{12,16},{16,20},{20,24},{24,28},{28,0},{1,5},{5... | collective-permute-start | bytes 98312 | tf_op jit(solution)/shard_map/ppermute | solution.py:516
  80.0 8.2 %collective-permute-start.15 = (f32[32,256]{1,0:T(8,128)S(1)}, f32[32,256]{1,0:T(8,128)S(1)}, u32[]{:S(2)}, u32[]{:S(2)}) collective-permute-start(f32[32,256]{1,0:T(8,128)S(1)} %constant_dynamic-update-slice_fusion.2), channel_id=1, source_target_pairs={{0,28},{4,0},{8,4},{12,8},{16,12},{20,16},{24,20},{28,24},{1,29},{... | collective-permute-start | bytes 98312 | tf_op jit(solution)/shard_map/ppermute | solution.py:516
  96.6 12.5 %collective-permute-start.18 = (f32[4,16,256]{2,1,0:T(8,128)S(1)}, f32[4,16,256]{2,1,0:T(8,128)S(1)}, u32[]{:S(2)}, u32[]{:S(2)}) collective-permute-start(f32[4,16,256]{2,1,0:T(8,128)S(1)} %get-tuple-element.58), channel_id=1, source_target_pairs={{0,4},{4,8},{8,12},{12,16},{16,20},{20,24},{24,28},{28,0},{1,5},{5... | collective-permute-start | bytes 196616 | tf_op jit(solution)/shard_map/ppermute | solution.py:516
  96.7 12.4 %collective-permute-start.19 = (f32[4,16,256]{2,1,0:T(8,128)S(1)}, f32[4,16,256]{2,1,0:T(8,128)S(1)}, u32[]{:S(2)}, u32[]{:S(2)}) collective-permute-start(f32[4,16,256]{2,1,0:T(8,128)S(1)} %get-tuple-element.57), channel_id=1, source_target_pairs={{0,28},{4,0},{8,4},{12,8},{16,12},{20,16},{24,20},{28,24},{1,29},{... | collective-permute-start | bytes 196616 | tf_op jit(solution)/shard_map/ppermute | solution.py:516
  115.2 7.4 %collective-permute-start.20 = (f32[16,128]{1,0:T(8,128)S(1)}, f32[16,128]{1,0:T(8,128)S(1)}, u32[]{:S(2)}, u32[]{:S(2)}) collective-permute-start(f32[16,128]{1,0:T(8,128)S(1)} %get-tuple-element.36), channel_id=1, source_target_pairs={{0,1},{1,2},{2,3},{3,0},{4,5},{5,6},{6,7},{7,4},{8,9},{9,10},{10,1... | collective-permute-start | bytes 24584 | tf_op jit(solution)/shard_map/ppermute | solution.py:516
  117.9 11.5 %collective-permute-start.22 = (f32[6,16,256]{2,1,0:T(8,128)S(1)}, f32[6,16,256]{2,1,0:T(8,128)S(1)}, u32[]{:S(2)}, u32[]{:S(2)}) collective-permute-start(f32[6,16,256]{2,1,0:T(8,128)S(1)} %get-tuple-element.44), channel_id=1, source_target_pairs={{0,4},{4,8},{8,12},{12,16},{16,20},{20,24},{24,28},{28,0},{1,5},{5... | collective-permute-start | bytes 294920 | tf_op jit(solution)/shard_map/ppermute | solution.py:516
  117.9 11.5 %collective-permute-start.24 = (f32[6,16,256]{2,1,0:T(8,128)S(1)}, f32[6,16,256]{2,1,0:T(8,128)S(1)}, u32[]{:S(2)}, u32[]{:S(2)}) collective-permute-start(f32[6,16,256]{2,1,0:T(8,128)S(1)} %get-tuple-element.43), channel_id=1, source_target_pairs={{0,28},{4,0},{8,4},{12,8},{16,12},{20,16},{24,20},{28,24},{1,29},{... | collective-permute-start | bytes 294920 | tf_op jit(solution)/shard_map/ppermute | solution.py:516
  122.7 6.7 %collective-permute-start.23 = (f32[16,256]{1,0:T(8,128)S(1)}, f32[16,256]{1,0:T(8,128)S(1)}, u32[]{:S(2)}, u32[]{:S(2)}) collective-permute-start(f32[16,256]{1,0:T(8,128)S(1)} %constant_dynamic-update-slice_fusion.4), channel_id=1, source_target_pairs={{0,4},{4,8},{8,12},{12,16},{16,20},{20,24},{24,28},{28,0},{1,5},{5... | collective-permute-start | bytes 49160 | tf_op jit(solution)/shard_map/ppermute | solution.py:516
  122.7 6.7 %collective-permute-start.25 = (f32[16,256]{1,0:T(8,128)S(1)}, f32[16,256]{1,0:T(8,128)S(1)}, u32[]{:S(2)}, u32[]{:S(2)}) collective-permute-start(f32[16,256]{1,0:T(8,128)S(1)} %constant_dynamic-update-slice_fusion.4), channel_id=1, source_target_pairs={{0,28},{4,0},{8,4},{12,8},{16,12},{20,16},{24,20},{28,24},{1,29},{... | collective-permute-start | bytes 49160 | tf_op jit(solution)/shard_map/ppermute | solution.py:516
  134.9 9.0 %collective-permute-start.28 = (f32[4,8,256]{2,1,0:T(8,128)S(1)}, f32[4,8,256]{2,1,0:T(8,128)S(1)}, u32[]{:S(2)}, u32[]{:S(2)}) collective-permute-start(f32[4,8,256]{2,1,0:T(8,128)S(1)} %get-tuple-element.60), channel_id=1, source_target_pairs={{0,4},{4,8},{8,12},{12,16},{16,20},{20,24},{24,28},{28,0},{1,5},{5... | collective-permute-start | bytes 98312 | tf_op jit(solution)/shard_map/ppermute | solution.py:516
  134.9 8.9 %collective-permute-start.29 = (f32[4,8,256]{2,1,0:T(8,128)S(1)}, f32[4,8,256]{2,1,0:T(8,128)S(1)}, u32[]{:S(2)}, u32[]{:S(2)}) collective-permute-start(f32[4,8,256]{2,1,0:T(8,128)S(1)} %get-tuple-element.59), channel_id=1, source_target_pairs={{0,28},{4,0},{8,4},{12,8},{16,12},{20,16},{24,20},{28,24},{1,29},{... | collective-permute-start | bytes 98312 | tf_op jit(solution)/shard_map/ppermute | solution.py:516
  (11 other events, 40.6 us)

commit v2 on v1

--- a/solution.py
+++ b/solution.py
@@ -26,7 +26,7 @@
 
 
 def cost(pairs, ops):
-    return pl.CostEstimate(flops=int(pairs * ops * 140), bytes_accessed=1 << 20, transcendentals=0)
+    return pl.CostEstimate(flops=int(pairs * ops * 15), bytes_accessed=1 << 20, transcendentals=0)
 
 
 def pair_force(own, their, total):
@@ -64,10 +64,10 @@
 )
 
 
-def fill_shifted(shifted, col, row, pieces, field, scale, group, shifts, is_y):
+def fill_shifted(shifted, col, row, pieces, scale, group, shifts, is_y):
     for cells, left, right, lo, hi in pieces:
         count = cells.shape[-1] // LANES
-        blocks = [cells[field, lo:hi, b * LANES : (b + 1) * LANES] for b in range(count)]
+        blocks = [cells[lo:hi, b * LANES : (b + 1) * LANES] for b in range(count)]
         if scale != 1.0:
             blocks = [v * scale for v in blocks]
         lane = lane_of(blocks[0].shape)
@@ -95,7 +95,7 @@
     for pieces, fields in ((motion, moved), (pressure, pressed), (motion, massed)):
         for field, scale in fields:
             is_y = fields is moved and field == 1
-            fill_shifted(shifted, col, row, pieces(field), field, scale, group_of(field), shifts, is_y)
+            fill_shifted(shifted, col, row, pieces(field), scale, group_of(field), shifts, is_y)
             row += 1
 
 
@@ -184,10 +184,9 @@
     return pl.pallas_call(kernel, out_shape=(ends, ends), in_specs=[VMEM], out_specs=(VMEM, VMEM), compiler_params=PARAMS)(motion)
 
 
-def bounds_of(arrays, axis):
+def bounds_of(sizes):
     spans, lo = [], 0
-    for index, array in enumerate(arrays):
-        hi = array.shape[axis]
+    for index, hi in enumerate(sizes):
         if hi > lo:
             spans.append((index, lo, hi))
             lo = hi
@@ -203,8 +202,8 @@
     flat_m = [e for pair in ends_m for e in pair]
     flat_p = [e for pair in ends_p for e in pair]
     whole = [(0, 0, slots)]
-    spans_m = whole if inner else bounds_of([e[0] for e in ends_m], 0)
-    spans_p = whole if inner else bounds_of([e[0] for e in ends_p], 0)
+    spans_m = whole if inner else bounds_of([e[0].shape[0] for e in ends_m])
+    spans_p = whole if inner else bounds_of([e[0].shape[0] for e in ends_p])
     inputs = [motion] + ([pressure] if pressed else []) + flat_m + flat_p + ([] if partial is None else [partial])
     rows = len(moved) + len(pressed) + len(massed)
 
@@ -225,10 +224,10 @@
         for c in range(columns):
 
             def motion_pieces(field):
-                return pieces(motion_ref.at[c], m_refs, spans_m if field < 6 else [(len(ends_m) - 1, 0, slots)])
+                return pieces(motion_ref.at[c, field], m_refs, spans_m if field < 6 else [(len(ends_m) - 1, 0, slots)])
 
             def pressure_pieces(field):
-                return pieces(pressure_ref.at[c], p_refs, spans_p)
+                return pieces(pressure_ref.at[c, field], p_refs, spans_p)
 
             fill_column(shifted, c, kind, motion_pieces, pressure_pieces, lambda f: f * columns + c, shifts)
         zero = jnp.zeros((ROWS, LANES), jnp.float32)
@@ -256,40 +255,42 @@
     )(*inputs)
 
 
-def halo_sums(kind, refs, columns, slots, limit, first, last, motion_ref, pressure_ref, shifted):
+def halo_sums(kind, refs, columns, slots, limit, first, last, motion_ref, pressure_ref, shifted, sizes_m, sizes_p):
+    spans_m, spans_p = bounds_of(sizes_m), bounds_of(sizes_p)
     for side in range(2):
         m_refs, p_refs = refs[side]
         column = columns - 1 if side == 0 else 0
-        spans_m = bounds_of([ends for _, ends in m_refs], 0)
-        spans_p = bounds_of([ends for _, ends in p_refs], 0)
-
-        def pieces(history, spans):
+
+        def field_of(ref, at, size):
+            return ref.at[at : at + size]
+
+        def piece(cells, ends, lo, hi):
+            return (cells, ends.at[:, 0:LANES], ends.at[:, LANES : 2 * LANES], lo, hi)
+
+        def motion_pieces(field):
             out = []
-            for i, lo, hi in spans:
-                cells, ends = history[i]
-                out.append((cells, ends.at[:, 0:LANES], ends.at[:, LANES : 2 * LANES], lo, hi))
+            for i, lo, hi in spans_m if field < 6 else [(len(sizes_m) - 1, 0, slots)]:
+                size = sizes_m[i]
+                ends = field_of(m_refs[i], (4 if i == len(sizes_m) - 1 else 3) * size, size)
+                if field < 3 or field == 6:
+                    cells = field_of(m_refs[i], min(field, 3) * size, size)
+                else:
+                    cells = field_of(p_refs[i], 4 * sizes_p[i] + (field - 3) * size, size)
+                out.append(piece(cells, ends, lo, hi))
             return out
 
-        def motion_pieces(field):
-            return pieces(m_refs, spans_m if field < 6 else [(len(m_refs) - 1, 0, slots)])
-
         def pressure_pieces(field):
-            return pieces(p_refs, spans_p)
+            return [
+                piece(field_of(p_refs[i], field * sizes_p[i], sizes_p[i]), field_of(p_refs[i], 3 * sizes_p[i], sizes_p[i]), lo, hi)
+                for i, lo, hi in spans_p
+            ]
 
         fill_column(shifted, side, kind, motion_pieces, pressure_pieces, lambda f: f * columns + column, SHIFTS)
         x, shift = (0, -1) if side == 0 else (columns - 1, 1)
         add_pairs(kind, motion_ref, pressure_ref, shifted, x, [(side, shift)], limit, first, last)
 
 
-def paired(refs):
-    return [(refs[i], refs[i + 1]) for i in range(0, len(refs), 2)]
-
-
-def with_own_ends(refs):
-    return [(ref, ref.at[ref.shape[0] - 1]) for ref in refs]
-
-
-def density_rest(motion, partial, messages, density, entropy, counts, level, limit, slots_sent):
+def density_rest(motion, partial, messages, sizes, density, entropy, counts, level, limit, slots_sent):
     columns, _, slots, width = motion.shape
     (m_left, m_right) = messages
     first = density is None
@@ -310,8 +311,8 @@
         def end(x, span, lanes, total):
             sums[x, 0, span, lanes] = total[0]
 
-        sides = ((paired(m_refs[:n_m]), []), (paired(m_refs[n_m:]), []))
-        halo_sums(DENSITY, sides, columns, slots, limit, start, end, motion_ref, None, shifted)
+        sides = ((m_refs[:n_m], []), (m_refs[n_m:], []))
+        halo_sums(DENSITY, sides, columns, slots, limit, start, end, motion_ref, None, shifted, sizes, [])
         for x in range(columns):
             count = counts_ref[level, x : x + 1, :]
             for lo in range(0, slots, ROWS):
@@ -348,7 +349,7 @@
     )(*inputs)
 
 
-def force_rest(motion, pressure, partial, messages_m, messages_p, counts, level, limit, slots_sent):
+def force_rest(motion, pressure, partial, messages_m, messages_p, sizes_m, sizes_p, counts, level, limit, slots_sent):
     columns, _, slots, width = motion.shape
     n_m, n_p = len(messages_m[0]), len(messages_p[0])
     inputs = [motion, pressure, partial, counts] + messages_m[0] + messages_p[0] + messages_m[1] + messages_p[1]
@@ -362,7 +363,7 @@
         sides = []
         for side in range(2):
             at = 4 + side * (n_m + n_p)
-            sides.append((paired(refs[at : at + n_m]), with_own_ends(refs[at + n_m : at + n_m + n_p])))
+            sides.append((refs[at : at + n_m], refs[at + n_m : at + n_m + n_p]))
         new_ref = refs[n_in]
         shifted, sums = refs[-2:]
         sums[...] = partial_ref[...]
@@ -374,7 +375,9 @@
             for k in range(3):
                 sums[x, k, span, lanes] = total[k]
 
-        halo_sums(FORCE, sides, columns, slots, limit, start, end, motion_ref, pressure_ref, shifted)
+        halo_sums(
+            FORCE, sides, columns, slots, limit, start, end, motion_ref, pressure_ref, shifted, sizes_m, sizes_p
+        )
         for x in range(columns):
             count = counts_ref[level, x : x + 1, :]
             new_ref[x, 6, :, :] = motion_ref[x, 6, :, :]
@@ -520,8 +523,14 @@
     return pass_on(right_ends, "sub", 1), pass_on(left_ends, "sub", -1)
 
 
-def swap_columns(first, final):
+def swap_columns(parts_of):
+    first = jnp.concatenate(parts_of(0), axis=0)
+    final = jnp.concatenate(parts_of(-1), axis=0)
     return pass_on(final, "tile", 1), pass_on(first, "tile", -1)
+
+
+def rows_of(fields):
+    return fields.reshape(-1, fields.shape[-1])
 
 
 def beside(ends, width):
@@ -539,35 +548,36 @@
     entropy = entropy.transpose(1, 0, 2)
     limits = (slots, slots // 2, slots // 4)
     pressure = None
-    ends_m, ends_p = [], []
+    ends_m, ends_p, sizes_m, sizes_p = [], [], [], []
     left_m, right_m, left_p, right_p = [], [], [], []
     made = first_ends(motion)
     place, meta = ranks(targets.reshape(slots * columns, width), parts)
     for level in range(levels):
         limit = limits[level]
         sent = limits[max(level - 1, 0)]
-        fields = MOTION if level == 0 else 6
-        cells = swap_columns(motion[0, :fields, :sent], motion[-1, :fields, :sent])
         ends_m.insert(0, swap_ends(*made))
         partial = own_part(DENSITY, motion, None, ends_m, [], limit, (0,))
+        ends_m[0], partial = lax.optimization_barrier((ends_m[0], partial))
         plane = beside(ends_m[0], width)
-        corners = swap_columns(plane, plane)
+        masses = (lambda c: [motion[c, 6]]) if level == 0 else (lambda c: [])
+        cells = swap_columns(lambda c: [rows_of(motion[c, :3, :sent]), *masses(c), plane])
+        sizes_m.insert(0, sent)
+        left_m.insert(0, cells[0])
+        right_m.insert(0, cells[1])
         partial = own_part(DENSITY, motion, None, ends_m, [], limit, (-1, 1), partial)
-        left_m[:0] = [cells[0], corners[0]]
-        right_m[:0] = [cells[1], corners[1]]
-        pressure, *made = density_rest(motion, partial, (left_m, right_m), pressure, entropy, active_counts, level, limit, limit)
+        pressure, *made = density_rest(motion, partial, (left_m, right_m), sizes_m, pressure, entropy, active_counts, level, limit, limit)
         ends_p.insert(0, swap_ends(*made))
         partial = own_part(FORCE, motion, pressure, ends_m, ends_p, limit, (0,))
-        plane = beside(ends_p[0], width)[None]
-        first = jnp.concatenate([pressure[0, :, :limit], plane], axis=0)
-        final = jnp.concatenate([pressure[-1, :, :limit], plane], axis=0)
-        cells = swap_columns(first, final)
+        ends_p[0], partial = lax.optimization_barrier((ends_p[0], partial))
+        plane = beside(ends_p[0], width)
+        cells = swap_columns(lambda c: [rows_of(pressure[c, :, :limit]), plane, rows_of(motion[c, 3:6, :sent])])
+        sizes_p.insert(0, limit)
         left_p.insert(0, cells[0])
         right_p.insert(0, cells[1])
         partial = own_part(FORCE, motion, pressure, ends_m, ends_p, limit, (-1, 1), partial)
         more = limit if level < levels - 1 else 0
         motion, *made = force_rest(
-            motion, pressure, partial, (left_m, right_m), (left_p, right_p), active_counts, level, limit, more
+            motion, pressure, partial, (left_m, right_m), (left_p, right_p), sizes_m, sizes_p, active_counts, level, limit, more
         )
     capacity = 3 * slots * columns * width // 8
     lists = compact(motion, pressure, place, meta[:, : 3 * parts], parts, capacity)

time: 167 us -> 154 us (0.922)
  starting transfers between devices: 55 us -> 41.4 us
    ppermute x30 -> x24, starting transfers between devices: 55 us -> 41.4 us  [pass_on(): lax.ppermute(value, axis, [(i, (i + step) % count) for i in range(count)])]
    unnamed x17 -> x20, local copies, waits for them, and re-layouts: 3.58 us -> 2.78 us
  transfers between devices with their start and end apart: 30 -> 24, of which waited for: 0 -> 3; matrix products, arithmetic and copies ran while one was open for 0% -> 0% of each run, Pallas kernels for 34% -> 37%
where the time goes in v2:
time: 154 us
  Pallas kernels  93.2 us (61%)
  starting transfers between devices  41.4 us (27%)
  blocking collectives  14.1 us (9%)
  local copies, waits for them, and re-layouts  2.95 us (2%)
  waiting for transfers between devices  1.68 us (1%)
    pallas_call x12, Pallas kernels, own_part(): pl.pallas_call(kernel, out_shape=jax.ShapeDtypeStruct((columns, outs, lim...  56.5 us
    ppermute x24, starting transfers between devices, pass_on(): lax.ppermute(value, axis, [(i, (i + step) % count) for i in range(count)])  41.4 us
    pallas_call x3, Pallas kernels, force_rest(): pl.pallas_call(kernel, out_shape=outs, in_specs=[VMEM] * n_in, out_specs=...  21.2 us
    all_to_all x1, blocking collectives, shards(): lax.all_to_all(lists, 'sub', split_axis=0, concat_axis=0, tiled=True)  14.1 us
    pallas_call x3, Pallas kernels, density_rest(): pl.pallas_call(kernel, out_shape=(jax.ShapeDtypeStruct((columns, PRESSURE...  9.93 us
    pallas_call x1, Pallas kernels, compact(): pl.pallas_call(kernel, out_shape=jax.ShapeDtypeStruct((parts, 8, capacity...  4.57 us
  transfers between devices with their start and end apart: 24, of which 3 were waited for; matrix products, arithmetic and copies ran while one was open for 0% of the time, Pallas kernels for 37%

profile of v2, /device:TPU:0, one launch (start us, length us, event | category | flops | bytes accessed | tf_op | source)
XLA Modules:
  0.0 154.0 jit_solution(1859262395458444150)
XLA Ops:
  2.6 2.0 %collective-permute-start.1 = (f32[32,128]{1,0:T(8,128)S(1)}, f32[32,128]{1,0:T(8,128)S(1)}, u32[]{:S(2)}, u32[]{:S(2)}) collective-permute-start(f32[32,128]{1,0:T(8,128)S(1)} %get-tuple-element.43), channel_id=1, source_target_pairs={{0,3},{1,0},{2,1},{3,2},{4,7},{5,4},{6,5},{7,6},{8,11},{9,8},{10,9... | collective-permute-start | bytes 49160 | tf_op jit(solution)/shard_map/ppermute | solution.py:519
  4.7 3.1 %shard_map.65.refs_3_ = f32[2,1,32,256]{3,2,1,0:T(8,128)S(1)} custom-call(f32[2,7,32,256]{3,2,1,0:T(8,128)S(1)} %maximum_bitcast_fusion.motion_ref.refs_0_), custom_call_target="tpu_custom_call" | custom-call | flops 471859200 | bytes 1048576 | tf_op jit(solution)/shard_map/pallas_call | solution.py:247
  7.9 2.3 %collective-permute-start.2 = (f32[160,256]{1,0:T(8,128)S(1)}, f32[160,256]{1,0:T(8,128)S(1)}, u32[]{:S(2)}, u32[]{:S(2)}) collective-permute-start(f32[160,256]{1,0:T(8,128)S(1)} %get-tuple-element.104), channel_id=1, source_target_pairs={{0,4},{4,8},{8,12},{12,16},{16,20},{20,24},{24,28},{28,0},{1,5},{5... | collective-permute-start | bytes 491528 | tf_op jit(solution)/shard_map/ppermute | solution.py:519
  10.2 3.1 %collective-permute-start.3 = (f32[160,256]{1,0:T(8,128)S(1)}, f32[160,256]{1,0:T(8,128)S(1)}, u32[]{:S(2)}, u32[]{:S(2)}) collective-permute-start(f32[160,256]{1,0:T(8,128)S(1)} %get-tuple-element.103), channel_id=1, source_target_pairs={{0,28},{4,0},{8,4},{12,8},{16,12},{20,16},{24,20},{28,24},{1,29},{... | collective-permute-start | bytes 491528 | tf_op jit(solution)/shard_map/ppermute | solution.py:519
  13.3 6.6 %shard_map.66.refs_1_ = f32[2,1,32,256]{3,2,1,0:T(8,128)S(1)} custom-call(f32[2,7,32,256]{3,2,1,0:T(8,128)S(1)} %maximum_bitcast_fusion.motion_ref.refs_0_, f32[32,128]{1,0:T(8,128)S(1)} %collective-permute-done.refs_1_.refs_2_.refs_3_.refs_4_.refs_5_.refs_6_, f32[32,128]{1,0:T(8,128)S(1)} %collective-permute-done.1.refs_2_.refs_3_.refs_4_.refs_5_.refs_6_.refs_7_, ...), custom_call_target="tpu_custom_call" | custom-call | flops 943718400 | bytes 1048576 | tf_op jit(solution)/shard_map/pallas_call | solution.py:247
  19.9 5.2 %shard_map.67 = (f32[2,3,32,256]{3,2,1,0:T(8,128)S(1)}, f32[32,128]{1,0:T(8,128)S(1)}, f32[32,128]{1,0:T(8,128)S(1)}) custom-call(f32[2,7,32,256]{3,2,1,0:T(8,128)S(1)} %maximum_bitcast_fusion.motion_ref.refs_0_, f32[2,1,32,256]{3,2,1,0:T(8,128)S(1)} %shard_map.66.refs_1_, f32[2,32,256]{2,1,0:T(8,128)S(1)} %bitcast.37, s32[3,2,256]{2,1,0:T(2,128)S(1)} %copy-done, ...), custom_call_target="tpu_custom_call" | custom-call | flops 707788800 | bytes 1048576 | tf_op jit(solution)/shard_map/pallas_call | solution.py:338
  27.0 7.1 %shard_map.68.refs_6_ = f32[2,3,32,256]{3,2,1,0:T(8,128)S(1)} custom-call(f32[2,7,32,256]{3,2,1,0:T(8,128)S(1)} %maximum_bitcast_fusion.motion_ref.refs_0_, f32[2,3,32,256]{3,2,1,0:T(8,128)S(1)} %get-tuple-element.47.refs_1_.refs_4_), custom_call_target="tpu_custom_call" | custom-call | flops 943718400 | bytes 1048576 | tf_op jit(solution)/shard_map/pallas_call | solution.py:247
  34.2 4.7 %collective-permute-start.7 = (f32[224,256]{1,0:T(8,128)S(1)}, f32[224,256]{1,0:T(8,128)S(1)}, u32[]{:S(2)}, u32[]{:S(2)}) collective-permute-start(f32[224,256]{1,0:T(8,128)S(1)} %get-tuple-element.101), channel_id=1, source_target_pairs={{0,28},{4,0},{8,4},{12,8},{16,12},{20,16},{24,20},{28,24},{1,29},{... | collective-permute-start | bytes 688136 | tf_op jit(solution)/shard_map/ppermute | solution.py:519
  38.9 14.7 %shard_map.69.refs_2_ = f32[2,3,32,256]{3,2,1,0:T(8,128)S(1)} custom-call(f32[2,7,32,256]{3,2,1,0:T(8,128)S(1)} %maximum_bitcast_fusion.motion_ref.refs_0_, f32[2,3,32,256]{3,2,1,0:T(8,128)S(1)} %get-tuple-element.47.refs_1_.refs_4_, f32[32,128]{1,0:T(8,128)S(1)} %collective-permute-done.refs_1_.refs_2_.refs_3_.refs_4_.refs_5_.refs_6_, ...), custom_call_target="tpu_custom_call" | custom-call | flops 1887436800 | bytes 1048576 | tf_op jit(solution)/shard_map/pallas_call | solution.py:247
  53.6 11.6 %shard_map.70 = (f32[2,7,32,256]{3,2,1,0:T(8,128)S(1)}, f32[32,128]{1,0:T(8,128)S(1)}, f32[32,128]{1,0:T(8,128)S(1)}) custom-call(f32[2,7,32,256]{3,2,1,0:T(8,128)S(1)} %maximum_bitcast_fusion.motion_ref.refs_0_, f32[2,3,32,256]{3,2,1,0:T(8,128)S(1)} %get-tuple-element.47.refs_1_.refs_4_, f32[2,3,32,256]{3,2,1,0:T(8,128)S(1)} %shard_map.69.refs_2_, ...), custom_call_target="tpu_custom_call" | custom-call | flops 1415577600 | bytes 1048576 | tf_op jit(solution)/shard_map/pallas_call | solution.py:399
  68.8 4.7 %collective-permute-start.11 = (f32[128,256]{1,0:T(8,128)S(1)}, f32[128,256]{1,0:T(8,128)S(1)}, u32[]{:S(2)}, u32[]{:S(2)}) collective-permute-start(f32[128,256]{1,0:T(8,128)S(1)} %get-tuple-element.99), channel_id=1, source_target_pairs={{0,28},{4,0},{8,4},{12,8},{16,12},{20,16},{24,20},{28,24},{1,29},{... | collective-permute-start | bytes 393224 | tf_op jit(solution)/shard_map/ppermute | solution.py:519
  73.5 3.4 %shard_map.72.refs_1_ = f32[2,1,16,256]{3,2,1,0:T(8,128)S(1)} custom-call(f32[2,7,32,256]{3,2,1,0:T(8,128)S(1)} %get-tuple-element.53.refs_0_, f32[32,128]{1,0:T(8,128)S(1)} %collective-permute-done.8.refs_1_.refs_2_.refs_3_.refs_4_, f32[32,128]{1,0:T(8,128)S(1)} %collective-permute-done.9.refs_2_.refs_3_.refs_4_.refs_5_, ...), custom_call_target="tpu_custom_call" | custom-call | flops 471859200 | bytes 1048576 | tf_op jit(solution)/shard_map/pallas_call | solution.py:247
  77.5 3.0 %shard_map.73 = (f32[2,3,32,256]{3,2,1,0:T(8,128)S(1)}, f32[16,128]{1,0:T(8,128)S(1)}, f32[16,128]{1,0:T(8,128)S(1)}) custom-call(f32[2,7,32,256]{3,2,1,0:T(8,128)S(1)} %get-tuple-element.53.refs_0_, f32[2,1,16,256]{3,2,1,0:T(8,128)S(1)} %shard_map.72.refs_1_, f32[2,32,256]{2,1,0:T(8,128)S(1)} %bitcast.38, s32[3,2,256]{2,1,0:T(2,128)S(1)} %copy-done, ...), custom_call_target="tpu_custom_call" | custom-call | flops 353894400 | bytes 1048576 | tf_op jit(solution)/shard_map/pallas_call | solution.py:338
  82.2 3.6 %shard_map.74.refs_10_ = f32[2,3,16,256]{3,2,1,0:T(8,128)S(1)} custom-call(f32[2,7,32,256]{3,2,1,0:T(8,128)S(1)} %get-tuple-element.53.refs_0_, f32[2,3,32,256]{3,2,1,0:T(8,128)S(1)} %get-tuple-element.59.refs_1_.refs_4_), custom_call_target="tpu_custom_call" | custom-call | flops 471859200 | bytes 1048576 | tf_op jit(solution)/shard_map/pallas_call | solution.py:247
  85.9 4.9 %collective-permute-start.15 = (f32[160,256]{1,0:T(8,128)S(1)}, f32[160,256]{1,0:T(8,128)S(1)}, u32[]{:S(2)}, u32[]{:S(2)}) collective-permute-start(f32[160,256]{1,0:T(8,128)S(1)} %get-tuple-element.107), channel_id=1, source_target_pairs={{0,28},{4,0},{8,4},{12,8},{16,12},{20,16},{24,20},{28,24},{1,29},{... | collective-permute-start | bytes 491528 | tf_op jit(solution)/shard_map/ppermute | solution.py:519
  90.8 7.7 %shard_map.75.refs_2_ = f32[2,3,16,256]{3,2,1,0:T(8,128)S(1)} custom-call(f32[2,7,32,256]{3,2,1,0:T(8,128)S(1)} %get-tuple-element.53.refs_0_, f32[2,3,32,256]{3,2,1,0:T(8,128)S(1)} %get-tuple-element.59.refs_1_.refs_4_, f32[32,128]{1,0:T(8,128)S(1)} %collective-permute-done.8.refs_1_.refs_2_.refs_3_.refs_4_, ...), custom_call_target="tpu_custom_call" | custom-call | flops 943718400 | bytes 1048576 | tf_op jit(solution)/shard_map/pallas_call | solution.py:247
  98.5 6.1 %shard_map.76 = (f32[2,7,32,256]{3,2,1,0:T(8,128)S(1)}, f32[16,128]{1,0:T(8,128)S(1)}, f32[16,128]{1,0:T(8,128)S(1)}) custom-call(f32[2,7,32,256]{3,2,1,0:T(8,128)S(1)} %get-tuple-element.53.refs_0_, f32[2,3,32,256]{3,2,1,0:T(8,128)S(1)} %get-tuple-element.59.refs_1_.refs_4_, f32[2,3,16,256]{3,2,1,0:T(8,128)S(1)} %shard_map.75.refs_2_, ...), custom_call_target="tpu_custom_call" | custom-call | flops 707788800 | bytes 1048576 | tf_op jit(solution)/shard_map/pallas_call | solution.py:399
  107.9 4.7 %collective-permute-start.19 = (f32[64,256]{1,0:T(8,128)S(1)}, f32[64,256]{1,0:T(8,128)S(1)}, u32[]{:S(2)}, u32[]{:S(2)}) collective-permute-start(f32[64,256]{1,0:T(8,128)S(1)} %get-tuple-element.105), channel_id=1, source_target_pairs={{0,28},{4,0},{8,4},{12,8},{16,12},{20,16},{24,20},{28,24},{1,29},{... | collective-permute-start | bytes 196616 | tf_op jit(solution)/shard_map/ppermute | solution.py:519
  112.7 2.0 %shard_map.78.refs_1_ = f32[2,1,8,256]{3,2,1,0:T(8,128)S(1)} custom-call(f32[2,7,32,256]{3,2,1,0:T(8,128)S(1)} %get-tuple-element.65.refs_0_, f32[16,128]{1,0:T(8,128)S(1)} %collective-permute-done.16.refs_1_.refs_2_, f32[16,128]{1,0:T(8,128)S(1)} %collective-permute-done.17.refs_2_.refs_3_, ...), custom_call_target="tpu_custom_call" | custom-call | flops 235929600 | bytes 1048576 | tf_op jit(solution)/shard_map/pallas_call | solution.py:247
  120.9 5.0 %collective-permute-start.23 = (f32[80,256]{1,0:T(8,128)S(1)}, f32[80,256]{1,0:T(8,128)S(1)}, u32[]{:S(2)}, u32[]{:S(2)}) collective-permute-start(f32[80,256]{1,0:T(8,128)S(1)} %get-tuple-element.109), channel_id=1, source_target_pairs={{0,28},{4,0},{8,4},{12,8},{16,12},{20,16},{24,20},{28,24},{1,29},{... | collective-permute-start | bytes 245768 | tf_op jit(solution)/shard_map/ppermute | solution.py:519
  126.8 4.2 %shard_map.81.refs_2_ = f32[2,3,8,256]{3,2,1,0:T(8,128)S(1)} custom-call(f32[2,7,32,256]{3,2,1,0:T(8,128)S(1)} %get-tuple-element.65.refs_0_, f32[2,3,32,256]{3,2,1,0:T(8,128)S(1)} %get-tuple-element.71.refs_1_.pressure_ref, f32[16,128]{1,0:T(8,128)S(1)} %collective-permute-done.16.refs_1_.refs_2_, f32[16,128]{1,0:T(8,128)S(1)} %collective-permute-done.17.refs_2_.refs_3_, ...), custom_call_target="tpu_custom_call" | custom-call | flops 471859200 | bytes 1048576 | tf_op jit(solution)/shard_map/pallas_call | solution.py:247
  131.0 3.4 %shard_map.82.motion_ref = f32[2,7,32,256]{3,2,1,0:T(8,128)S(1)} custom-call(f32[2,7,32,256]{3,2,1,0:T(8,128)S(1)} %get-tuple-element.65.refs_0_, f32[2,3,32,256]{3,2,1,0:T(8,128)S(1)} %get-tuple-element.71.refs_1_.pressure_ref, f32[2,3,8,256]{3,2,1,0:T(8,128)S(1)} %shard_map.81.refs_2_, s32[3,2,256]{2,1,0:T(2,128)S(1)} %copy-done, ...), custom_call_target="tpu_custom_call" | custom-call | flops 353894400 | bytes 1048576 | tf_op jit(solution)/shard_map/pallas_call | solution.py:399
  134.4 4.6 %shard_map.84 = f32[4,8,6144]{2,1,0:T(8,128)S(1)} custom-call(f32[2,7,32,256]{3,2,1,0:T(8,128)S(1)} %shard_map.82.motion_ref, f32[2,3,32,256]{3,2,1,0:T(8,128)S(1)} %get-tuple-element.71.refs_1_.pressure_ref, s32[64,256]{1,0:T(8,128)S(1)} %get-tuple-element.77.place_ref, s32[64,12]{1,0:T(8,128)S(1)} %bitcast.40), custom_call_target="tpu_custom_call" | custom-call | tf_op jit(solution)/shard_map/pallas_call | solution.py:504
  139.0 14.1 %all_to_all.5 = f32[4,8,6144]{2,1,0:T(8,128)S(1)} all-to-all(f32[4,8,6144]{2,1,0:T(8,128)S(1)} %shard_map.84), channel_id=1, replica_groups=mesh['tile'=8,'sub'=4] {'sub'}, dimensions={0} | all-to-all | bytes 1572864 | tf_op jit(solution)/shard_map/all_to_all | solution.py:584
  (89 shorter events, 21.7 us)
Async XLA Ops:
  2.1 5.7 %collective-permute-start = (f32[32,128]{1,0:T(8,128)S(1)}, f32[32,128]{1,0:T(8,128)S(1)}, u32[]{:S(2)}, u32[]{:S(2)}) collective-permute-start(f32[32,128]{1,0:T(8,128)S(1)} %get-tuple-element.42), channel_id=1, source_target_pairs={{0,1},{1,2},{2,3},{3,0},{4,5},{5,6},{6,7},{7,4},{8,9},{9,10},{10,1... | collective-permute-start | bytes 49160 | tf_op jit(solution)/shard_map/ppermute | solution.py:519
  2.6 5.2 %collective-permute-start.1 = (f32[32,128]{1,0:T(8,128)S(1)}, f32[32,128]{1,0:T(8,128)S(1)}, u32[]{:S(2)}, u32[]{:S(2)}) collective-permute-start(f32[32,128]{1,0:T(8,128)S(1)} %get-tuple-element.43), channel_id=1, source_target_pairs={{0,3},{1,0},{2,1},{3,2},{4,7},{5,4},{6,5},{7,6},{8,11},{9,8},{10,9... | collective-permute-start | bytes 49160 | tf_op jit(solution)/shard_map/ppermute | solution.py:519
  7.9 12.0 %collective-permute-start.2 = (f32[160,256]{1,0:T(8,128)S(1)}, f32[160,256]{1,0:T(8,128)S(1)}, u32[]{:S(2)}, u32[]{:S(2)}) collective-permute-start(f32[160,256]{1,0:T(8,128)S(1)} %get-tuple-element.104), channel_id=1, source_target_pairs={{0,4},{4,8},{8,12},{12,16},{16,20},{20,24},{24,28},{28,0},{1,5},{5... | collective-permute-start | bytes 491528 | tf_op jit(solution)/shard_map/ppermute | solution.py:519
  10.2 9.7 %collective-permute-start.3 = (f32[160,256]{1,0:T(8,128)S(1)}, f32[160,256]{1,0:T(8,128)S(1)}, u32[]{:S(2)}, u32[]{:S(2)}) collective-permute-start(f32[160,256]{1,0:T(8,128)S(1)} %get-tuple-element.103), channel_id=1, source_target_pairs={{0,28},{4,0},{8,4},{12,8},{16,12},{20,16},{24,20},{28,24},{1,29},{... | collective-permute-start | bytes 491528 | tf_op jit(solution)/shard_map/ppermute | solution.py:519
  25.2 8.9 %collective-permute-start.4 = (f32[32,128]{1,0:T(8,128)S(1)}, f32[32,128]{1,0:T(8,128)S(1)}, u32[]{:S(2)}, u32[]{:S(2)}) collective-permute-start(f32[32,128]{1,0:T(8,128)S(1)} %get-tuple-element.48), channel_id=1, source_target_pairs={{0,1},{1,2},{2,3},{3,0},{4,5},{5,6},{6,7},{7,4},{8,9},{9,10},{10,1... | collective-permute-start | bytes 49160 | tf_op jit(solution)/shard_map/ppermute | solution.py:519
  25.2 8.8 %collective-permute-start.5 = (f32[32,128]{1,0:T(8,128)S(1)}, f32[32,128]{1,0:T(8,128)S(1)}, u32[]{:S(2)}, u32[]{:S(2)}) collective-permute-start(f32[32,128]{1,0:T(8,128)S(1)} %get-tuple-element.49), channel_id=1, source_target_pairs={{0,3},{1,0},{2,1},{3,2},{4,7},{5,4},{6,5},{7,6},{8,11},{9,8},{10,9... | collective-permute-start | bytes 49160 | tf_op jit(solution)/shard_map/ppermute | solution.py:519
  34.1 19.5 %collective-permute-start.6 = (f32[224,256]{1,0:T(8,128)S(1)}, f32[224,256]{1,0:T(8,128)S(1)}, u32[]{:S(2)}, u32[]{:S(2)}) collective-permute-start(f32[224,256]{1,0:T(8,128)S(1)} %get-tuple-element.102), channel_id=1, source_target_pairs={{0,4},{4,8},{8,12},{12,16},{16,20},{20,24},{24,28},{28,0},{1,5},{5... | collective-permute-start | bytes 688136 | tf_op jit(solution)/shard_map/ppermute | solution.py:519
  34.2 19.4 %collective-permute-start.7 = (f32[224,256]{1,0:T(8,128)S(1)}, f32[224,256]{1,0:T(8,128)S(1)}, u32[]{:S(2)}, u32[]{:S(2)}) collective-permute-start(f32[224,256]{1,0:T(8,128)S(1)} %get-tuple-element.101), channel_id=1, source_target_pairs={{0,28},{4,0},{8,4},{12,8},{16,12},{20,16},{24,20},{28,24},{1,29},{... | collective-permute-start | bytes 688136 | tf_op jit(solution)/shard_map/ppermute | solution.py:519
  65.3 3.4 %collective-permute-start.8 = (f32[32,128]{1,0:T(8,128)S(1)}, f32[32,128]{1,0:T(8,128)S(1)}, u32[]{:S(2)}, u32[]{:S(2)}) collective-permute-start(f32[32,128]{1,0:T(8,128)S(1)} %get-tuple-element.54), channel_id=1, source_target_pairs={{0,1},{1,2},{2,3},{3,0},{4,5},{5,6},{6,7},{7,4},{8,9},{9,10},{10,1... | collective-permute-start | bytes 49160 | tf_op jit(solution)/shard_map/ppermute | solution.py:519
  65.3 3.3 %collective-permute-start.9 = (f32[32,128]{1,0:T(8,128)S(1)}, f32[32,128]{1,0:T(8,128)S(1)}, u32[]{:S(2)}, u32[]{:S(2)}) collective-permute-start(f32[32,128]{1,0:T(8,128)S(1)} %get-tuple-element.55), channel_id=1, source_target_pairs={{0,3},{1,0},{2,1},{3,2},{4,7},{5,4},{6,5},{7,6},{8,11},{9,8},{10,9... | collective-permute-start | bytes 49160 | tf_op jit(solution)/shard_map/ppermute | solution.py:519
  68.7 8.7 %collective-permute-start.10 = (f32[128,256]{1,0:T(8,128)S(1)}, f32[128,256]{1,0:T(8,128)S(1)}, u32[]{:S(2)}, u32[]{:S(2)}) collective-permute-start(f32[128,256]{1,0:T(8,128)S(1)} %get-tuple-element.100), channel_id=1, source_target_pairs={{0,4},{4,8},{8,12},{12,16},{16,20},{20,24},{24,28},{28,0},{1,5},{5... | collective-permute-start | bytes 393224 | tf_op jit(solution)/shard_map/ppermute | solution.py:519
  68.8 8.7 %collective-permute-start.11 = (f32[128,256]{1,0:T(8,128)S(1)}, f32[128,256]{1,0:T(8,128)S(1)}, u32[]{:S(2)}, u32[]{:S(2)}) collective-permute-start(f32[128,256]{1,0:T(8,128)S(1)} %get-tuple-element.99), channel_id=1, source_target_pairs={{0,28},{4,0},{8,4},{12,8},{16,12},{20,16},{24,20},{28,24},{1,29},{... | collective-permute-start | bytes 393224 | tf_op jit(solution)/shard_map/ppermute | solution.py:519
  80.4 5.4 %collective-permute-start.12 = (f32[16,128]{1,0:T(8,128)S(1)}, f32[16,128]{1,0:T(8,128)S(1)}, u32[]{:S(2)}, u32[]{:S(2)}) collective-permute-start(f32[16,128]{1,0:T(8,128)S(1)} %get-tuple-element.60), channel_id=1, source_target_pairs={{0,1},{1,2},{2,3},{3,0},{4,5},{5,6},{6,7},{7,4},{8,9},{9,10},{10,1... | collective-permute-start | bytes 24584 | tf_op jit(solution)/shard_map/ppermute | solution.py:519
  80.9 4.9 %collective-permute-start.13 = (f32[16,128]{1,0:T(8,128)S(1)}, f32[16,128]{1,0:T(8,128)S(1)}, u32[]{:S(2)}, u32[]{:S(2)}) collective-permute-start(f32[16,128]{1,0:T(8,128)S(1)} %get-tuple-element.61), channel_id=1, source_target_pairs={{0,3},{1,0},{2,1},{3,2},{4,7},{5,4},{6,5},{7,6},{8,11},{9,8},{10,9... | collective-permute-start | bytes 24584 | tf_op jit(solution)/shard_map/ppermute | solution.py:519
  85.9 12.6 %collective-permute-start.14 = (f32[160,256]{1,0:T(8,128)S(1)}, f32[160,256]{1,0:T(8,128)S(1)}, u32[]{:S(2)}, u32[]{:S(2)}) collective-permute-start(f32[160,256]{1,0:T(8,128)S(1)} %get-tuple-element.108), channel_id=1, source_target_pairs={{0,4},{4,8},{8,12},{12,16},{16,20},{20,24},{24,28},{28,0},{1,5},{5... | collective-permute-start | bytes 491528 | tf_op jit(solution)/shard_map/ppermute | solution.py:519
  85.9 12.6 %collective-permute-start.15 = (f32[160,256]{1,0:T(8,128)S(1)}, f32[160,256]{1,0:T(8,128)S(1)}, u32[]{:S(2)}, u32[]{:S(2)}) collective-permute-start(f32[160,256]{1,0:T(8,128)S(1)} %get-tuple-element.107), channel_id=1, source_target_pairs={{0,28},{4,0},{8,4},{12,8},{16,12},{20,16},{24,20},{28,24},{1,29},{... | collective-permute-start | bytes 491528 | tf_op jit(solution)/shard_map/ppermute | solution.py:519
  104.7 3.1 %collective-permute-start.16 = (f32[16,128]{1,0:T(8,128)S(1)}, f32[16,128]{1,0:T(8,128)S(1)}, u32[]{:S(2)}, u32[]{:S(2)}) collective-permute-start(f32[16,128]{1,0:T(8,128)S(1)} %get-tuple-element.66), channel_id=1, source_target_pairs={{0,1},{1,2},{2,3},{3,0},{4,5},{5,6},{6,7},{7,4},{8,9},{9,10},{10,1... | collective-permute-start | bytes 24584 | tf_op jit(solution)/shard_map/ppermute | solution.py:519
  104.8 3.1 %collective-permute-start.17 = (f32[16,128]{1,0:T(8,128)S(1)}, f32[16,128]{1,0:T(8,128)S(1)}, u32[]{:S(2)}, u32[]{:S(2)}) collective-permute-start(f32[16,128]{1,0:T(8,128)S(1)} %get-tuple-element.67), channel_id=1, source_target_pairs={{0,3},{1,0},{2,1},{3,2},{4,7},{5,4},{6,5},{7,6},{8,11},{9,8},{10,9... | collective-permute-start | bytes 24584 | tf_op jit(solution)/shard_map/ppermute | solution.py:519
  107.9 7.3 %collective-permute-start.18 = (f32[64,256]{1,0:T(8,128)S(1)}, f32[64,256]{1,0:T(8,128)S(1)}, u32[]{:S(2)}, u32[]{:S(2)}) collective-permute-start(f32[64,256]{1,0:T(8,128)S(1)} %get-tuple-element.106), channel_id=1, source_target_pairs={{0,4},{4,8},{8,12},{12,16},{16,20},{20,24},{24,28},{28,0},{1,5},{5... | collective-permute-start | bytes 196616 | tf_op jit(solution)/shard_map/ppermute | solution.py:519
  107.9 7.3 %collective-permute-start.19 = (f32[64,256]{1,0:T(8,128)S(1)}, f32[64,256]{1,0:T(8,128)S(1)}, u32[]{:S(2)}, u32[]{:S(2)}) collective-permute-start(f32[64,256]{1,0:T(8,128)S(1)} %get-tuple-element.105), channel_id=1, source_target_pairs={{0,28},{4,0},{8,4},{12,8},{16,12},{20,16},{24,20},{28,24},{1,29},{... | collective-permute-start | bytes 196616 | tf_op jit(solution)/shard_map/ppermute | solution.py:519
  117.0 3.6 %collective-permute-start.20 = (f32[8,128]{1,0:T(8,128)S(1)}, f32[8,128]{1,0:T(8,128)S(1)}, u32[]{:S(2)}, u32[]{:S(2)}) collective-permute-start(f32[8,128]{1,0:T(8,128)S(1)} %get-tuple-element.72), channel_id=1, source_target_pairs={{0,1},{1,2},{2,3},{3,0},{4,5},{5,6},{6,7},{7,4},{8,9},{9,10},{10,1... | collective-permute-start | bytes 12296 | tf_op jit(solution)/shard_map/ppermute | solution.py:519
  117.3 3.3 %collective-permute-start.21 = (f32[8,128]{1,0:T(8,128)S(1)}, f32[8,128]{1,0:T(8,128)S(1)}, u32[]{:S(2)}, u32[]{:S(2)}) collective-permute-start(f32[8,128]{1,0:T(8,128)S(1)} %get-tuple-element.73), channel_id=1, source_target_pairs={{0,3},{1,0},{2,1},{3,2},{4,7},{5,4},{6,5},{7,6},{8,11},{9,8},{10,9... | collective-permute-start | bytes 12296 | tf_op jit(solution)/shard_map/ppermute | solution.py:519
  120.7 10.3 %collective-permute-start.22 = (f32[80,256]{1,0:T(8,128)S(1)}, f32[80,256]{1,0:T(8,128)S(1)}, u32[]{:S(2)}, u32[]{:S(2)}) collective-permute-start(f32[80,256]{1,0:T(8,128)S(1)} %get-tuple-element.110), channel_id=1, source_target_pairs={{0,4},{4,8},{8,12},{12,16},{16,20},{20,24},{24,28},{28,0},{1,5},{5... | collective-permute-start | bytes 245768 | tf_op jit(solution)/shard_map/ppermute | solution.py:519
  120.9 10.1 %collective-permute-start.23 = (f32[80,256]{1,0:T(8,128)S(1)}, f32[80,256]{1,0:T(8,128)S(1)}, u32[]{:S(2)}, u32[]{:S(2)}) collective-permute-start(f32[80,256]{1,0:T(8,128)S(1)} %get-tuple-element.109), channel_id=1, source_target_pairs={{0,28},{4,0},{8,4},{12,8},{16,12},{20,16},{24,20},{28,24},{1,29},{... | collective-permute-start | bytes 245768 | tf_op jit(solution)/shard_map/ppermute | solution.py:519
  (5 other events, 13.3 us)

commit v3 on v2

--- a/solution.py
+++ b/solution.py
@@ -29,9 +29,9 @@
     return pl.CostEstimate(flops=int(pairs * ops * 15), bytes_accessed=1 << 20, transcendentals=0)
 
 
-def pair_force(own, their, total):
-    xi, yi, zi, ui, vi, wi, qi, ci, ri = own
-    xj, yj, zj, uj, vj, wj, qj, cj, rj, mj = their
+def force_core(own, their):
+    xi, yi, zi, ui, vi, wi, qi, ci, ri = own[:9]
+    xj, yj, zj, uj, vj, wj, qj, cj, rj = their[:9]
     dx, dy, dz = xi - xj, yi - yj, zi - zj
     squared = dx * dx + dy * dy + dz * dz
     radius = squared * lax.rsqrt(jnp.maximum(squared, 1e-30))
@@ -39,19 +39,42 @@
     approach = dx * (ui - uj) + dy * (vi - vj) + dz * (wi - wj)
     closing = jnp.minimum(approach, 0.0) * pl.reciprocal(squared + SOFTEN, approx=True)
     viscous = closing * (closing - (ci + cj)) * pl.reciprocal(ri + rj, approx=True)
-    strength = (qi + qj + viscous) * ((remain * remain) * (remain * mj))
-    return (total[0] + strength * dx, total[1] + strength * dy, total[2] + strength * dz)
-
-
-def pair_density(own, their, total):
-    xi, yi, zi = own
-    xj, yj, zj, mj = their
+    return (dx, dy, dz), (qi + qj + viscous), remain
+
+
+def density_core(own, their):
+    xi, yi, zi = own[:3]
+    xj, yj, zj = their[:3]
     dx, dy, dz = xi - xj, yi - yj, zi - zj
     squared = dx * dx + dy * dy + dz * dz
     radius = squared * lax.rsqrt(jnp.maximum(squared, 1e-30))
-    remain = jnp.maximum(1.0 - radius, 0.0)
+    return jnp.maximum(1.0 - radius, 0.0)
+
+
+def pair_force(own, their, total):
+    delta, pressure, remain = force_core(own, their)
+    strength = pressure * ((remain * remain) * (remain * their[-1]))
+    return tuple(t + strength * d for t, d in zip(total, delta))
+
+
+def pair_density(own, their, total):
+    remain = density_core(own, their)
     square = remain * remain
-    return (total[0] + (square * square) * ((5.0 - 4.0 * remain) * mj),)
+    return (total[0] + (square * square) * ((5.0 - 4.0 * remain) * their[-1]),)
+
+
+def both_force(own, their, total):
+    delta, pressure, remain = force_core(own, their)
+    strength = pressure * ((remain * remain) * remain)
+    on_own, on_their = strength * their[-1], strength * own[-1]
+    return tuple(t + on_own * d for t, d in zip(total, delta)), tuple(on_their * d for d in delta)
+
+
+def both_density(own, their, total):
+    remain = density_core(own, their)
+    square = remain * remain
+    weight = (square * square) * (5.0 - 4.0 * remain)
+    return (total[0] + weight * their[-1],), (weight * own[-1],)
 
 
 DENSITY = ((0, 1.0), (1, 1.0), (2, 1.0)), (), ((6, KERNEL_NORM),), pair_density, 1
@@ -197,6 +220,7 @@
     columns, _, slots, width = motion.shape
     moved, pressed, massed, _, outs = kind
     inner = shifts == (0,)
+    mutual = limit == slots
     if inner:
         ends_m = ends_p = []
     flat_m = [e for pair in ends_m for e in pair]
@@ -213,6 +237,9 @@
         pressure_ref = refs.pop(0) if pressed else None
         m_refs = refs[: len(flat_m)]
         p_refs = refs[len(flat_m) : len(flat_m) + len(flat_p)]
+        if mutual:
+            *refs, parts, reaction, packed = refs
+            mutual_refs = (parts, reaction, packed)
         partial_ref = None if partial is None else refs[-3]
         out_ref, shifted = refs[-2:]
 
@@ -241,18 +268,171 @@
             for k in range(outs):
                 out_ref[x, k, span, lanes] = total[k]
 
+        if not mutual:
+            for x in range(columns):
+                add_pairs(kind, motion_ref, pressure_ref, shifted, x, own_sources(x, columns), limit, first, last)
+            return
+        parts, reaction, packed = mutual_refs
+        if inner:
+            for x in range(columns):
+                add_pairs(kind, motion_ref, pressure_ref, shifted, x, [(x, 0)], limit, first, last)
+        else:
+            out_ref[...] = partial_ref[...]
+        edges = []
         for x in range(columns):
-            add_pairs(kind, motion_ref, pressure_ref, shifted, x, own_sources(x, columns), limit, first, last)
+            for col in (x, x + 1):
+                for shift in shifts:
+                    if col == columns or (col == x and shift != 1):
+                        continue
+                    both_ways(kind, motion_ref, pressure_ref, shifted, x, col, shifts.index(shift), out_ref, parts, reaction)
+                    take_reaction(out_ref, reaction, col, shift, outs)
+                    if shift:
+                        edges.append((col, x, -shift))
+        if edges:
+            edge_pairs(kind, motion_ref, pressure_ref, shifted, shifts, edges, out_ref, packed)
 
     return pl.pallas_call(
         kernel,
         out_shape=jax.ShapeDtypeStruct((columns, outs, limit, width), jnp.float32),
         in_specs=[VMEM] * len(inputs),
         out_specs=VMEM,
-        scratch_shapes=[pltpu.VMEM((columns, len(shifts), width // LANES, rows, slots, LANES), jnp.float32)],
+        scratch_shapes=[pltpu.VMEM((columns, len(shifts), width // LANES, rows, slots, LANES), jnp.float32)]
+        + (
+            [
+                pltpu.VMEM((outs, slots, ROWS, LANES), jnp.float32),
+                pltpu.VMEM((outs, width // LANES, slots, LANES), jnp.float32),
+                pltpu.VMEM((rows, slots, LANES), jnp.float32),
+            ]
+            if mutual
+            else []
+        ),
         compiler_params=PARAMS,
         cost_estimate=cost(limit * slots * len(shifts) * (3 * columns - 2) * width, 60 if outs == 3 else 30),
     )(*inputs)
+
+
+def sum_rows(values):
+    row = lax.broadcasted_iota(jnp.int32, (ROWS, LANES), 0)
+    step = 1
+    while len(values) > 1:
+        low = lax.bitwise_and(row, step) == 0
+        values = [
+            jnp.where(low, a, b) + pltpu.roll(jnp.where(low, b, a), step, 0) for a, b in zip(values[::2], values[1::2])
+        ]
+        step *= 2
+    return values[0]
+
+
+def own_rows(kind, motion_ref, pressure_ref, x, span, lanes):
+    moved, pressed, massed = kind[:3]
+    rows = [(motion_ref, f, s) for f, s in moved] + [(pressure_ref, f, s) for f, s in pressed] + [(motion_ref, f, s) for f, s in massed]
+    return [ref[x, f, span, lanes] * s if s != 1.0 else ref[x, f, span, lanes] for ref, f, s in rows]
+
+
+def both_ways(kind, motion_ref, pressure_ref, shifted, x, col, form, sums, parts, reaction):
+    outs = kind[4]
+    slots, blocks, rows = shifted.shape[-2], shifted.shape[2], shifted.shape[3]
+    both = both_force if outs == 3 else both_density
+    sign = -1.0 if outs == 3 else 1.0
+    group = 2 if outs == 3 else 4
+    unroll = 8
+
+    def lane_block(b, carry):
+        lanes = pl.ds(pl.multiple_of(b * LANES, LANES), LANES)
+        for part in range(slots // (ROWS * group)):
+            spans = [slice((part * group + v) * ROWS, (part * group + v + 1) * ROWS) for v in range(group)]
+            mine = []
+            for span in spans:
+                values = own_rows(kind, motion_ref, pressure_ref, x, span, lanes)
+                mine.append([values[0] - float(col - x)] + values[1:])
+
+            def step(outer, totals):
+                totals = list(totals)
+                for inner in range(unroll):
+                    slot = outer * unroll + inner
+                    their = [jnp.broadcast_to(shifted[col, form, b, r, pl.ds(slot, 1), :], (ROWS, LANES)) for r in range(rows)]
+                    back = None
+                    for v in range(group):
+                        totals[v], given = both(mine[v], their, totals[v])
+                        back = given if back is None else tuple(p + q for p, q in zip(back, given))
+                    for k in range(outs):
+                        parts[k, slot] = back[k] if part == 0 else parts[k, slot] + back[k]
+                return tuple(totals)
+
+            totals = tuple(tuple(sums[x, k, span, lanes] for k in range(outs)) for span in spans)
+            totals = lax.fori_loop(0, slots // unroll, step, totals)
+            for span, total in zip(spans, totals):
+                for k in range(outs):
+                    sums[x, k, span, lanes] = total[k]
+        for k in range(outs):
+            for lo in range(0, slots, ROWS):
+                reaction[k, b, lo : lo + ROWS, :] = sign * sum_rows([parts[k, lo + r] for r in range(ROWS)])
+        return carry
+
+    lax.fori_loop(0, blocks, lane_block, 0)
+
+
+def take_reaction(sums, reaction, col, shift, outs):
+    blocks, slots = reaction.shape[1], reaction.shape[2]
+    lane = lane_of((slots, LANES))
+    for k in range(outs):
+        values = [reaction[k, b] for b in range(blocks)]
+        if shift == 1:
+            turned = [jnp.zeros((slots, LANES), jnp.float32)] + [pltpu.roll(v, 1, 1) for v in values]
+            values = [jnp.where(lane == 0, turned[b], turned[b + 1]) for b in range(blocks)]
+        elif shift == -1:
+            turned = [pltpu.roll(v, LANES - 1, 1) for v in values] + [jnp.zeros((slots, LANES), jnp.float32)]
+            values = [jnp.where(lane == LANES - 1, turned[b + 1], turned[b]) for b in range(blocks)]
+        for b in range(blocks):
+            lanes = slice(b * LANES, (b + 1) * LANES)
+            sums[col, k, :, lanes] = sums[col, k, :, lanes] + values[b]
+
+
+def edge_pairs(kind, motion_ref, pressure_ref, shifted, forms, edges, sums, packed):
+    pair, outs = kind[3], kind[4]
+    slots, blocks, rows = shifted.shape[-2], shifted.shape[2], shifted.shape[3]
+    lane = lane_of((ROWS, LANES))
+    width = blocks * LANES
+    tall = lane_of((slots, LANES))
+    for r in range(rows):
+        value = jnp.zeros((slots, LANES), jnp.float32)
+        for q, (x, col, shift) in enumerate(edges):
+            block, turn = (0, q) if shift == -1 else (blocks - 1, q + 1)
+            value = jnp.where(tall == q, pltpu.roll(shifted[col, forms.index(shift), block, r], turn, 1), value)
+        packed[r] = value
+    spans = [slice(lo, lo + ROWS) for lo in range(0, slots, ROWS)]
+    group = 2 if outs == 3 else 4
+    unroll = 8
+    for part in range(len(spans) // group):
+        mine = []
+        for span in spans[part * group : (part + 1) * group]:
+            values = None
+            for q, (x, col, shift) in enumerate(edges):
+                lanes, turn = (slice(0, LANES), q) if shift == -1 else (slice(width - LANES, width), q + 1)
+                cell = own_rows(kind, motion_ref, pressure_ref, x, span, lanes)
+                cell = [pltpu.roll(v, turn, 1) if turn else v for v in cell]
+                cell[0] = cell[0] - float(col - x)
+                values = cell if values is None else [jnp.where(lane == q, c, v) for c, v in zip(cell, values)]
+            mine.append(values)
+
+        def step(outer, totals):
+            totals = list(totals)
+            for inner in range(unroll):
+                slot = outer * unroll + inner
+                their = [jnp.broadcast_to(packed[r, pl.ds(slot, 1), :], (ROWS, LANES)) for r in range(rows)]
+                for v in range(group):
+                    totals[v] = pair(mine[v], their, totals[v])
+            return tuple(totals)
+
+        zero = jnp.zeros((ROWS, LANES), jnp.float32)
+        totals = lax.fori_loop(0, slots // unroll, step, tuple((zero,) * outs for _ in range(group)))
+        for v, span in enumerate(spans[part * group : (part + 1) * group]):
+            for k in range(outs):
+                for q, (x, col, shift) in enumerate(edges):
+                    at = 0 if shift == -1 else LANES - 1
+                    lanes = slice(0, LANES) if shift == -1 else slice(width - LANES, width)
+                    back = pltpu.roll(totals[v][k], (at - q) % LANES, 1) if at != q else totals[v][k]
+                    sums[x, k, span, lanes] = sums[x, k, span, lanes] + jnp.where(lane == at, back, 0.0)
 
 
 def halo_sums(kind, refs, columns, slots, limit, first, last, motion_ref, pressure_ref, shifted, sizes_m, sizes_p):

time: 154 us -> 148 us (0.961)
  Pallas kernels: 93.2 us -> 85.6 us
  waiting for transfers between devices: 1.68 us -> 3.93 us
    pallas_call x12, Pallas kernels: 56.5 us -> 48.9 us  [own_part(): pl.pallas_call(kernel, out_shape=jax.ShapeDtypeStruct((columns, outs, lim...]
    ppermute x24, waiting for transfers between devices: 1.68 us -> 3.93 us  [pass_on(): lax.ppermute(value, axis, [(i, (i + step) % count) for i in range(count)])]
  transfers between devices with their start and end apart: 24 -> 24, of which waited for: 3 -> 6; matrix products, arithmetic and copies ran while one was open for 0% -> 0% of each run, Pallas kernels for 37% -> 34%
where the time goes in v3:
time: 148 us
  Pallas kernels  85.6 us (58%)
  starting transfers between devices  40.8 us (28%)
  blocking collectives  14.1 us (10%)
  waiting for transfers between devices  3.93 us (3%)
  local copies, waits for them, and re-layouts  2.95 us (2%)
    pallas_call x12, Pallas kernels, own_part(): pl.pallas_call(kernel, out_shape=jax.ShapeDtypeStruct((columns, outs, lim...  48.9 us
    ppermute x24, starting transfers between devices, pass_on(): lax.ppermute(value, axis, [(i, (i + step) % count) for i in range(count)])  40.8 us
    pallas_call x3, Pallas kernels, force_rest(): pl.pallas_call(kernel, out_shape=outs, in_specs=[VMEM] * n_in, out_specs=...  21.2 us
    all_to_all x1, blocking collectives, shards(): lax.all_to_all(lists, 'sub', split_axis=0, concat_axis=0, tiled=True)  14.1 us
    pallas_call x3, Pallas kernels, density_rest(): pl.pallas_call(kernel, out_shape=(jax.ShapeDtypeStruct((columns, PRESSURE...  9.93 us
    pallas_call x1, Pallas kernels, compact(): pl.pallas_call(kernel, out_shape=jax.ShapeDtypeStruct((parts, 8, capacity...  4.57 us
    ppermute x24, waiting for transfers between devices, pass_on(): lax.ppermute(value, axis, [(i, (i + step) % count) for i in range(count)])  3.93 us
  transfers between devices with their start and end apart: 24, of which 6 were waited for; matrix products, arithmetic and copies ran while one was open for 0% of the time, Pallas kernels for 34%

profile of v3, /device:TPU:0, one launch (start us, length us, event | category | flops | bytes accessed | tf_op | source)
XLA Modules:
  0.0 148.0 jit_solution(6214391924806542676)
XLA Ops:
  2.6 2.0 %collective-permute-start.1 = (f32[32,128]{1,0:T(8,128)S(1)}, f32[32,128]{1,0:T(8,128)S(1)}, u32[]{:S(2)}, u32[]{:S(2)}) collective-permute-start(f32[32,128]{1,0:T(8,128)S(1)} %get-tuple-element.43), channel_id=1, source_target_pairs={{0,3},{1,0},{2,1},{3,2},{4,7},{5,4},{6,5},{7,6},{8,11},{9,8},{10,9... | collective-permute-start | bytes 49160 | tf_op jit(solution)/shard_map/ppermute | solution.py:699
  4.7 2.5 %shard_map.65.refs_3_ = f32[2,1,32,256]{3,2,1,0:T(8,128)S(1)} custom-call(f32[2,7,32,256]{3,2,1,0:T(8,128)S(1)} %maximum_bitcast_fusion.motion_ref.refs_0_), custom_call_target="tpu_custom_call" | custom-call | flops 471859200 | bytes 1048576 | tf_op jit(solution)/shard_map/pallas_call | solution.py:294
  7.2 2.3 %collective-permute-start.2 = (f32[160,256]{1,0:T(8,128)S(1)}, f32[160,256]{1,0:T(8,128)S(1)}, u32[]{:S(2)}, u32[]{:S(2)}) collective-permute-start(f32[160,256]{1,0:T(8,128)S(1)} %get-tuple-element.104), channel_id=1, source_target_pairs={{0,4},{4,8},{8,12},{12,16},{16,20},{20,24},{24,28},{28,0},{1,5},{5... | collective-permute-start | bytes 491528 | tf_op jit(solution)/shard_map/ppermute | solution.py:699
  9.5 3.1 %collective-permute-start.3 = (f32[160,256]{1,0:T(8,128)S(1)}, f32[160,256]{1,0:T(8,128)S(1)}, u32[]{:S(2)}, u32[]{:S(2)}) collective-permute-start(f32[160,256]{1,0:T(8,128)S(1)} %get-tuple-element.103), channel_id=1, source_target_pairs={{0,28},{4,0},{8,4},{12,8},{16,12},{20,16},{24,20},{28,24},{1,29},{... | collective-permute-start | bytes 491528 | tf_op jit(solution)/shard_map/ppermute | solution.py:699
  12.6 4.8 %shard_map.66.refs_1_ = f32[2,1,32,256]{3,2,1,0:T(8,128)S(1)} custom-call(f32[2,7,32,256]{3,2,1,0:T(8,128)S(1)} %maximum_bitcast_fusion.motion_ref.refs_0_, f32[32,128]{1,0:T(8,128)S(1)} %collective-permute-done.refs_1_.refs_2_.refs_3_.refs_4_.refs_5_.refs_6_, f32[32,128]{1,0:T(8,128)S(1)} %collective-permute-done.1.refs_2_.refs_3_.refs_4_.refs_5_.refs_6_.refs_7_, ...), custom_call_target="tpu_custom_call" | custom-call | flops 943718400 | bytes 1048576 | tf_op jit(solution)/shard_map/pallas_call | solution.py:294
  19.3 5.2 %shard_map.67 = (f32[2,3,32,256]{3,2,1,0:T(8,128)S(1)}, f32[32,128]{1,0:T(8,128)S(1)}, f32[32,128]{1,0:T(8,128)S(1)}) custom-call(f32[2,7,32,256]{3,2,1,0:T(8,128)S(1)} %maximum_bitcast_fusion.motion_ref.refs_0_, f32[2,1,32,256]{3,2,1,0:T(8,128)S(1)} %shard_map.66.refs_1_, f32[2,32,256]{2,1,0:T(8,128)S(1)} %bitcast.37, s32[3,2,256]{2,1,0:T(2,128)S(1)} %copy-done, ...), custom_call_target="tpu_custom_call" | custom-call | flops 707788800 | bytes 1048576 | tf_op jit(solution)/shard_map/pallas_call | solution.py:518
  26.4 5.8 %shard_map.68.refs_6_ = f32[2,3,32,256]{3,2,1,0:T(8,128)S(1)} custom-call(f32[2,7,32,256]{3,2,1,0:T(8,128)S(1)} %maximum_bitcast_fusion.motion_ref.refs_0_, f32[2,3,32,256]{3,2,1,0:T(8,128)S(1)} %get-tuple-element.47.refs_1_.refs_4_), custom_call_target="tpu_custom_call" | custom-call | flops 943718400 | bytes 1048576 | tf_op jit(solution)/shard_map/pallas_call | solution.py:294
  32.6 4.4 %collective-permute-start.7 = (f32[224,256]{1,0:T(8,128)S(1)}, f32[224,256]{1,0:T(8,128)S(1)}, u32[]{:S(2)}, u32[]{:S(2)}) collective-permute-start(f32[224,256]{1,0:T(8,128)S(1)} %get-tuple-element.101), channel_id=1, source_target_pairs={{0,28},{4,0},{8,4},{12,8},{16,12},{20,16},{24,20},{28,24},{1,29},{... | collective-permute-start | bytes 688136 | tf_op jit(solution)/shard_map/ppermute | solution.py:699
  37.0 10.9 %shard_map.69.refs_2_ = f32[2,3,32,256]{3,2,1,0:T(8,128)S(1)} custom-call(f32[2,7,32,256]{3,2,1,0:T(8,128)S(1)} %maximum_bitcast_fusion.motion_ref.refs_0_, f32[2,3,32,256]{3,2,1,0:T(8,128)S(1)} %get-tuple-element.47.refs_1_.refs_4_, f32[32,128]{1,0:T(8,128)S(1)} %collective-permute-done.refs_1_.refs_2_.refs_3_.refs_4_.refs_5_.refs_6_, ...), custom_call_target="tpu_custom_call" | custom-call | flops 1887436800 | bytes 1048576 | tf_op jit(solution)/shard_map/pallas_call | solution.py:294
  48.0 11.6 %shard_map.70 = (f32[2,7,32,256]{3,2,1,0:T(8,128)S(1)}, f32[32,128]{1,0:T(8,128)S(1)}, f32[32,128]{1,0:T(8,128)S(1)}) custom-call(f32[2,7,32,256]{3,2,1,0:T(8,128)S(1)} %maximum_bitcast_fusion.motion_ref.refs_0_, f32[2,3,32,256]{3,2,1,0:T(8,128)S(1)} %get-tuple-element.47.refs_1_.refs_4_, f32[2,3,32,256]{3,2,1,0:T(8,128)S(1)} %shard_map.69.refs_2_, ...), custom_call_target="tpu_custom_call" | custom-call | flops 1415577600 | bytes 1048576 | tf_op jit(solution)/shard_map/pallas_call | solution.py:579
  63.1 4.7 %collective-permute-start.11 = (f32[128,256]{1,0:T(8,128)S(1)}, f32[128,256]{1,0:T(8,128)S(1)}, u32[]{:S(2)}, u32[]{:S(2)}) collective-permute-start(f32[128,256]{1,0:T(8,128)S(1)} %get-tuple-element.99), channel_id=1, source_target_pairs={{0,28},{4,0},{8,4},{12,8},{16,12},{20,16},{24,20},{28,24},{1,29},{... | collective-permute-start | bytes 393224 | tf_op jit(solution)/shard_map/ppermute | solution.py:699
  67.8 3.4 %shard_map.72.refs_1_ = f32[2,1,16,256]{3,2,1,0:T(8,128)S(1)} custom-call(f32[2,7,32,256]{3,2,1,0:T(8,128)S(1)} %get-tuple-element.53.refs_0_, f32[32,128]{1,0:T(8,128)S(1)} %collective-permute-done.8.refs_1_.refs_2_.refs_3_.refs_4_, f32[32,128]{1,0:T(8,128)S(1)} %collective-permute-done.9.refs_2_.refs_3_.refs_4_.refs_5_, ...), custom_call_target="tpu_custom_call" | custom-call | flops 471859200 | bytes 1048576 | tf_op jit(solution)/shard_map/pallas_call | solution.py:294
  71.8 3.0 %shard_map.73 = (f32[2,3,32,256]{3,2,1,0:T(8,128)S(1)}, f32[16,128]{1,0:T(8,128)S(1)}, f32[16,128]{1,0:T(8,128)S(1)}) custom-call(f32[2,7,32,256]{3,2,1,0:T(8,128)S(1)} %get-tuple-element.53.refs_0_, f32[2,1,16,256]{3,2,1,0:T(8,128)S(1)} %shard_map.72.refs_1_, f32[2,32,256]{2,1,0:T(8,128)S(1)} %bitcast.38, s32[3,2,256]{2,1,0:T(2,128)S(1)} %copy-done, ...), custom_call_target="tpu_custom_call" | custom-call | flops 353894400 | bytes 1048576 | tf_op jit(solution)/shard_map/pallas_call | solution.py:518
  76.6 3.6 %shard_map.74.refs_10_ = f32[2,3,16,256]{3,2,1,0:T(8,128)S(1)} custom-call(f32[2,7,32,256]{3,2,1,0:T(8,128)S(1)} %get-tuple-element.53.refs_0_, f32[2,3,32,256]{3,2,1,0:T(8,128)S(1)} %get-tuple-element.59.refs_1_.refs_4_), custom_call_target="tpu_custom_call" | custom-call | flops 471859200 | bytes 1048576 | tf_op jit(solution)/shard_map/pallas_call | solution.py:294
  80.5 4.5 %collective-permute-start.15 = (f32[160,256]{1,0:T(8,128)S(1)}, f32[160,256]{1,0:T(8,128)S(1)}, u32[]{:S(2)}, u32[]{:S(2)}) collective-permute-start(f32[160,256]{1,0:T(8,128)S(1)} %get-tuple-element.107), channel_id=1, source_target_pairs={{0,28},{4,0},{8,4},{12,8},{16,12},{20,16},{24,20},{28,24},{1,29},{... | collective-permute-start | bytes 491528 | tf_op jit(solution)/shard_map/ppermute | solution.py:699
  85.0 7.7 %shard_map.75.refs_2_ = f32[2,3,16,256]{3,2,1,0:T(8,128)S(1)} custom-call(f32[2,7,32,256]{3,2,1,0:T(8,128)S(1)} %get-tuple-element.53.refs_0_, f32[2,3,32,256]{3,2,1,0:T(8,128)S(1)} %get-tuple-element.59.refs_1_.refs_4_, f32[32,128]{1,0:T(8,128)S(1)} %collective-permute-done.8.refs_1_.refs_2_.refs_3_.refs_4_, ...), custom_call_target="tpu_custom_call" | custom-call | flops 943718400 | bytes 1048576 | tf_op jit(solution)/shard_map/pallas_call | solution.py:294
  92.7 6.1 %shard_map.76 = (f32[2,7,32,256]{3,2,1,0:T(8,128)S(1)}, f32[16,128]{1,0:T(8,128)S(1)}, f32[16,128]{1,0:T(8,128)S(1)}) custom-call(f32[2,7,32,256]{3,2,1,0:T(8,128)S(1)} %get-tuple-element.53.refs_0_, f32[2,3,32,256]{3,2,1,0:T(8,128)S(1)} %get-tuple-element.59.refs_1_.refs_4_, f32[2,3,16,256]{3,2,1,0:T(8,128)S(1)} %shard_map.75.refs_2_, ...), custom_call_target="tpu_custom_call" | custom-call | flops 707788800 | bytes 1048576 | tf_op jit(solution)/shard_map/pallas_call | solution.py:579
  102.1 4.7 %collective-permute-start.19 = (f32[64,256]{1,0:T(8,128)S(1)}, f32[64,256]{1,0:T(8,128)S(1)}, u32[]{:S(2)}, u32[]{:S(2)}) collective-permute-start(f32[64,256]{1,0:T(8,128)S(1)} %get-tuple-element.105), channel_id=1, source_target_pairs={{0,28},{4,0},{8,4},{12,8},{16,12},{20,16},{24,20},{28,24},{1,29},{... | collective-permute-start | bytes 196616 | tf_op jit(solution)/shard_map/ppermute | solution.py:699
  106.8 2.0 %shard_map.78.refs_1_ = f32[2,1,8,256]{3,2,1,0:T(8,128)S(1)} custom-call(f32[2,7,32,256]{3,2,1,0:T(8,128)S(1)} %get-tuple-element.65.refs_0_, f32[16,128]{1,0:T(8,128)S(1)} %collective-permute-done.16.refs_1_.refs_2_, f32[16,128]{1,0:T(8,128)S(1)} %collective-permute-done.17.refs_2_.refs_3_, ...), custom_call_target="tpu_custom_call" | custom-call | flops 235929600 | bytes 1048576 | tf_op jit(solution)/shard_map/pallas_call | solution.py:294
  115.2 4.7 %collective-permute-start.23 = (f32[80,256]{1,0:T(8,128)S(1)}, f32[80,256]{1,0:T(8,128)S(1)}, u32[]{:S(2)}, u32[]{:S(2)}) collective-permute-start(f32[80,256]{1,0:T(8,128)S(1)} %get-tuple-element.109), channel_id=1, source_target_pairs={{0,28},{4,0},{8,4},{12,8},{16,12},{20,16},{24,20},{28,24},{1,29},{... | collective-permute-start | bytes 245768 | tf_op jit(solution)/shard_map/ppermute | solution.py:699
  120.9 4.2 %shard_map.81.refs_2_ = f32[2,3,8,256]{3,2,1,0:T(8,128)S(1)} custom-call(f32[2,7,32,256]{3,2,1,0:T(8,128)S(1)} %get-tuple-element.65.refs_0_, f32[2,3,32,256]{3,2,1,0:T(8,128)S(1)} %get-tuple-element.71.refs_1_.pressure_ref, f32[16,128]{1,0:T(8,128)S(1)} %collective-permute-done.16.refs_1_.refs_2_, f32[16,128]{1,0:T(8,128)S(1)} %collective-permute-done.17.refs_2_.refs_3_, ...), custom_call_target="tpu_custom_call" | custom-call | flops 471859200 | bytes 1048576 | tf_op jit(solution)/shard_map/pallas_call | solution.py:294
  125.1 3.4 %shard_map.82.motion_ref = f32[2,7,32,256]{3,2,1,0:T(8,128)S(1)} custom-call(f32[2,7,32,256]{3,2,1,0:T(8,128)S(1)} %get-tuple-element.65.refs_0_, f32[2,3,32,256]{3,2,1,0:T(8,128)S(1)} %get-tuple-element.71.refs_1_.pressure_ref, f32[2,3,8,256]{3,2,1,0:T(8,128)S(1)} %shard_map.81.refs_2_, s32[3,2,256]{2,1,0:T(2,128)S(1)} %copy-done, ...), custom_call_target="tpu_custom_call" | custom-call | flops 353894400 | bytes 1048576 | tf_op jit(solution)/shard_map/pallas_call | solution.py:579
  128.5 4.6 %shard_map.84 = f32[4,8,6144]{2,1,0:T(8,128)S(1)} custom-call(f32[2,7,32,256]{3,2,1,0:T(8,128)S(1)} %shard_map.82.motion_ref, f32[2,3,32,256]{3,2,1,0:T(8,128)S(1)} %get-tuple-element.71.refs_1_.pressure_ref, s32[64,256]{1,0:T(8,128)S(1)} %get-tuple-element.77.place_ref, s32[64,12]{1,0:T(8,128)S(1)} %bitcast.40), custom_call_target="tpu_custom_call" | custom-call | tf_op jit(solution)/shard_map/pallas_call | solution.py:684
  133.1 14.1 %all_to_all.5 = f32[4,8,6144]{2,1,0:T(8,128)S(1)} all-to-all(f32[4,8,6144]{2,1,0:T(8,128)S(1)} %shard_map.84), channel_id=1, replica_groups=mesh['tile'=8,'sub'=4] {'sub'}, dimensions={0} | all-to-all | bytes 1572864 | tf_op jit(solution)/shard_map/all_to_all | solution.py:764
  (89 shorter events, 24.3 us)
Async XLA Ops:
  2.1 5.0 %collective-permute-start = (f32[32,128]{1,0:T(8,128)S(1)}, f32[32,128]{1,0:T(8,128)S(1)}, u32[]{:S(2)}, u32[]{:S(2)}) collective-permute-start(f32[32,128]{1,0:T(8,128)S(1)} %get-tuple-element.42), channel_id=1, source_target_pairs={{0,1},{1,2},{2,3},{3,0},{4,5},{5,6},{6,7},{7,4},{8,9},{9,10},{10,1... | collective-permute-start | bytes 49160 | tf_op jit(solution)/shard_map/ppermute | solution.py:699
  2.6 4.5 %collective-permute-start.1 = (f32[32,128]{1,0:T(8,128)S(1)}, f32[32,128]{1,0:T(8,128)S(1)}, u32[]{:S(2)}, u32[]{:S(2)}) collective-permute-start(f32[32,128]{1,0:T(8,128)S(1)} %get-tuple-element.43), channel_id=1, source_target_pairs={{0,3},{1,0},{2,1},{3,2},{4,7},{5,4},{6,5},{7,6},{8,11},{9,8},{10,9... | collective-permute-start | bytes 49160 | tf_op jit(solution)/shard_map/ppermute | solution.py:699
  7.2 10.3 %collective-permute-start.2 = (f32[160,256]{1,0:T(8,128)S(1)}, f32[160,256]{1,0:T(8,128)S(1)}, u32[]{:S(2)}, u32[]{:S(2)}) collective-permute-start(f32[160,256]{1,0:T(8,128)S(1)} %get-tuple-element.104), channel_id=1, source_target_pairs={{0,4},{4,8},{8,12},{12,16},{16,20},{20,24},{24,28},{28,0},{1,5},{5... | collective-permute-start | bytes 491528 | tf_op jit(solution)/shard_map/ppermute | solution.py:699
  9.5 9.8 %collective-permute-start.3 = (f32[160,256]{1,0:T(8,128)S(1)}, f32[160,256]{1,0:T(8,128)S(1)}, u32[]{:S(2)}, u32[]{:S(2)}) collective-permute-start(f32[160,256]{1,0:T(8,128)S(1)} %get-tuple-element.103), channel_id=1, source_target_pairs={{0,28},{4,0},{8,4},{12,8},{16,12},{20,16},{24,20},{28,24},{1,29},{... | collective-permute-start | bytes 491528 | tf_op jit(solution)/shard_map/ppermute | solution.py:699
  24.6 7.6 %collective-permute-start.4 = (f32[32,128]{1,0:T(8,128)S(1)}, f32[32,128]{1,0:T(8,128)S(1)}, u32[]{:S(2)}, u32[]{:S(2)}) collective-permute-start(f32[32,128]{1,0:T(8,128)S(1)} %get-tuple-element.48), channel_id=1, source_target_pairs={{0,1},{1,2},{2,3},{3,0},{4,5},{5,6},{6,7},{7,4},{8,9},{9,10},{10,1... | collective-permute-start | bytes 49160 | tf_op jit(solution)/shard_map/ppermute | solution.py:699
  24.6 7.5 %collective-permute-start.5 = (f32[32,128]{1,0:T(8,128)S(1)}, f32[32,128]{1,0:T(8,128)S(1)}, u32[]{:S(2)}, u32[]{:S(2)}) collective-permute-start(f32[32,128]{1,0:T(8,128)S(1)} %get-tuple-element.49), channel_id=1, source_target_pairs={{0,3},{1,0},{2,1},{3,2},{4,7},{5,4},{6,5},{7,6},{8,11},{9,8},{10,9... | collective-permute-start | bytes 49160 | tf_op jit(solution)/shard_map/ppermute | solution.py:699
  32.2 15.7 %collective-permute-start.6 = (f32[224,256]{1,0:T(8,128)S(1)}, f32[224,256]{1,0:T(8,128)S(1)}, u32[]{:S(2)}, u32[]{:S(2)}) collective-permute-start(f32[224,256]{1,0:T(8,128)S(1)} %get-tuple-element.102), channel_id=1, source_target_pairs={{0,4},{4,8},{8,12},{12,16},{16,20},{20,24},{24,28},{28,0},{1,5},{5... | collective-permute-start | bytes 688136 | tf_op jit(solution)/shard_map/ppermute | solution.py:699
  32.6 15.4 %collective-permute-start.7 = (f32[224,256]{1,0:T(8,128)S(1)}, f32[224,256]{1,0:T(8,128)S(1)}, u32[]{:S(2)}, u32[]{:S(2)}) collective-permute-start(f32[224,256]{1,0:T(8,128)S(1)} %get-tuple-element.101), channel_id=1, source_target_pairs={{0,28},{4,0},{8,4},{12,8},{16,12},{20,16},{24,20},{28,24},{1,29},{... | collective-permute-start | bytes 688136 | tf_op jit(solution)/shard_map/ppermute | solution.py:699
  59.6 3.4 %collective-permute-start.8 = (f32[32,128]{1,0:T(8,128)S(1)}, f32[32,128]{1,0:T(8,128)S(1)}, u32[]{:S(2)}, u32[]{:S(2)}) collective-permute-start(f32[32,128]{1,0:T(8,128)S(1)} %get-tuple-element.54), channel_id=1, source_target_pairs={{0,1},{1,2},{2,3},{3,0},{4,5},{5,6},{6,7},{7,4},{8,9},{9,10},{10,1... | collective-permute-start | bytes 49160 | tf_op jit(solution)/shard_map/ppermute | solution.py:699
  59.6 3.3 %collective-permute-start.9 = (f32[32,128]{1,0:T(8,128)S(1)}, f32[32,128]{1,0:T(8,128)S(1)}, u32[]{:S(2)}, u32[]{:S(2)}) collective-permute-start(f32[32,128]{1,0:T(8,128)S(1)} %get-tuple-element.55), channel_id=1, source_target_pairs={{0,3},{1,0},{2,1},{3,2},{4,7},{5,4},{6,5},{7,6},{8,11},{9,8},{10,9... | collective-permute-start | bytes 49160 | tf_op jit(solution)/shard_map/ppermute | solution.py:699
  63.0 8.7 %collective-permute-start.10 = (f32[128,256]{1,0:T(8,128)S(1)}, f32[128,256]{1,0:T(8,128)S(1)}, u32[]{:S(2)}, u32[]{:S(2)}) collective-permute-start(f32[128,256]{1,0:T(8,128)S(1)} %get-tuple-element.100), channel_id=1, source_target_pairs={{0,4},{4,8},{8,12},{12,16},{16,20},{20,24},{24,28},{28,0},{1,5},{5... | collective-permute-start | bytes 393224 | tf_op jit(solution)/shard_map/ppermute | solution.py:699
  63.1 8.7 %collective-permute-start.11 = (f32[128,256]{1,0:T(8,128)S(1)}, f32[128,256]{1,0:T(8,128)S(1)}, u32[]{:S(2)}, u32[]{:S(2)}) collective-permute-start(f32[128,256]{1,0:T(8,128)S(1)} %get-tuple-element.99), channel_id=1, source_target_pairs={{0,28},{4,0},{8,4},{12,8},{16,12},{20,16},{24,20},{28,24},{1,29},{... | collective-permute-start | bytes 393224 | tf_op jit(solution)/shard_map/ppermute | solution.py:699
  74.8 5.4 %collective-permute-start.12 = (f32[16,128]{1,0:T(8,128)S(1)}, f32[16,128]{1,0:T(8,128)S(1)}, u32[]{:S(2)}, u32[]{:S(2)}) collective-permute-start(f32[16,128]{1,0:T(8,128)S(1)} %get-tuple-element.60), channel_id=1, source_target_pairs={{0,1},{1,2},{2,3},{3,0},{4,5},{5,6},{6,7},{7,4},{8,9},{9,10},{10,1... | collective-permute-start | bytes 24584 | tf_op jit(solution)/shard_map/ppermute | solution.py:699
  74.8 5.3 %collective-permute-start.13 = (f32[16,128]{1,0:T(8,128)S(1)}, f32[16,128]{1,0:T(8,128)S(1)}, u32[]{:S(2)}, u32[]{:S(2)}) collective-permute-start(f32[16,128]{1,0:T(8,128)S(1)} %get-tuple-element.61), channel_id=1, source_target_pairs={{0,3},{1,0},{2,1},{3,2},{4,7},{5,4},{6,5},{7,6},{8,11},{9,8},{10,9... | collective-permute-start | bytes 24584 | tf_op jit(solution)/shard_map/ppermute | solution.py:699
  80.2 12.5 %collective-permute-start.14 = (f32[160,256]{1,0:T(8,128)S(1)}, f32[160,256]{1,0:T(8,128)S(1)}, u32[]{:S(2)}, u32[]{:S(2)}) collective-permute-start(f32[160,256]{1,0:T(8,128)S(1)} %get-tuple-element.108), channel_id=1, source_target_pairs={{0,4},{4,8},{8,12},{12,16},{16,20},{20,24},{24,28},{28,0},{1,5},{5... | collective-permute-start | bytes 491528 | tf_op jit(solution)/shard_map/ppermute | solution.py:699
  80.5 12.2 %collective-permute-start.15 = (f32[160,256]{1,0:T(8,128)S(1)}, f32[160,256]{1,0:T(8,128)S(1)}, u32[]{:S(2)}, u32[]{:S(2)}) collective-permute-start(f32[160,256]{1,0:T(8,128)S(1)} %get-tuple-element.107), channel_id=1, source_target_pairs={{0,28},{4,0},{8,4},{12,8},{16,12},{20,16},{24,20},{28,24},{1,29},{... | collective-permute-start | bytes 491528 | tf_op jit(solution)/shard_map/ppermute | solution.py:699
  98.9 3.1 %collective-permute-start.16 = (f32[16,128]{1,0:T(8,128)S(1)}, f32[16,128]{1,0:T(8,128)S(1)}, u32[]{:S(2)}, u32[]{:S(2)}) collective-permute-start(f32[16,128]{1,0:T(8,128)S(1)} %get-tuple-element.66), channel_id=1, source_target_pairs={{0,1},{1,2},{2,3},{3,0},{4,5},{5,6},{6,7},{7,4},{8,9},{9,10},{10,1... | collective-permute-start | bytes 24584 | tf_op jit(solution)/shard_map/ppermute | solution.py:699
  98.9 3.1 %collective-permute-start.17 = (f32[16,128]{1,0:T(8,128)S(1)}, f32[16,128]{1,0:T(8,128)S(1)}, u32[]{:S(2)}, u32[]{:S(2)}) collective-permute-start(f32[16,128]{1,0:T(8,128)S(1)} %get-tuple-element.67), channel_id=1, source_target_pairs={{0,3},{1,0},{2,1},{3,2},{4,7},{5,4},{6,5},{7,6},{8,11},{9,8},{10,9... | collective-permute-start | bytes 24584 | tf_op jit(solution)/shard_map/ppermute | solution.py:699
  102.0 7.7 %collective-permute-start.18 = (f32[64,256]{1,0:T(8,128)S(1)}, f32[64,256]{1,0:T(8,128)S(1)}, u32[]{:S(2)}, u32[]{:S(2)}) collective-permute-start(f32[64,256]{1,0:T(8,128)S(1)} %get-tuple-element.106), channel_id=1, source_target_pairs={{0,4},{4,8},{8,12},{12,16},{16,20},{20,24},{24,28},{28,0},{1,5},{5... | collective-permute-start | bytes 196616 | tf_op jit(solution)/shard_map/ppermute | solution.py:699
  102.1 7.6 %collective-permute-start.19 = (f32[64,256]{1,0:T(8,128)S(1)}, f32[64,256]{1,0:T(8,128)S(1)}, u32[]{:S(2)}, u32[]{:S(2)}) collective-permute-start(f32[64,256]{1,0:T(8,128)S(1)} %get-tuple-element.105), channel_id=1, source_target_pairs={{0,28},{4,0},{8,4},{12,8},{16,12},{20,16},{24,20},{28,24},{1,29},{... | collective-permute-start | bytes 196616 | tf_op jit(solution)/shard_map/ppermute | solution.py:699
  111.4 3.6 %collective-permute-start.20 = (f32[8,128]{1,0:T(8,128)S(1)}, f32[8,128]{1,0:T(8,128)S(1)}, u32[]{:S(2)}, u32[]{:S(2)}) collective-permute-start(f32[8,128]{1,0:T(8,128)S(1)} %get-tuple-element.72), channel_id=1, source_target_pairs={{0,1},{1,2},{2,3},{3,0},{4,5},{5,6},{6,7},{7,4},{8,9},{9,10},{10,1... | collective-permute-start | bytes 12296 | tf_op jit(solution)/shard_map/ppermute | solution.py:699
  111.6 3.5 %collective-permute-start.21 = (f32[8,128]{1,0:T(8,128)S(1)}, f32[8,128]{1,0:T(8,128)S(1)}, u32[]{:S(2)}, u32[]{:S(2)}) collective-permute-start(f32[8,128]{1,0:T(8,128)S(1)} %get-tuple-element.73), channel_id=1, source_target_pairs={{0,3},{1,0},{2,1},{3,2},{4,7},{5,4},{6,5},{7,6},{8,11},{9,8},{10,9... | collective-permute-start | bytes 12296 | tf_op jit(solution)/shard_map/ppermute | solution.py:699
  115.1 9.9 %collective-permute-start.22 = (f32[80,256]{1,0:T(8,128)S(1)}, f32[80,256]{1,0:T(8,128)S(1)}, u32[]{:S(2)}, u32[]{:S(2)}) collective-permute-start(f32[80,256]{1,0:T(8,128)S(1)} %get-tuple-element.110), channel_id=1, source_target_pairs={{0,4},{4,8},{8,12},{12,16},{16,20},{20,24},{24,28},{28,0},{1,5},{5... | collective-permute-start | bytes 245768 | tf_op jit(solution)/shard_map/ppermute | solution.py:699
  115.2 9.8 %collective-permute-start.23 = (f32[80,256]{1,0:T(8,128)S(1)}, f32[80,256]{1,0:T(8,128)S(1)}, u32[]{:S(2)}, u32[]{:S(2)}) collective-permute-start(f32[80,256]{1,0:T(8,128)S(1)} %get-tuple-element.109), channel_id=1, source_target_pairs={{0,28},{4,0},{8,4},{12,8},{16,12},{20,16},{24,20},{28,24},{1,29},{... | collective-permute-start | bytes 245768 | tf_op jit(solution)/shard_map/ppermute | solution.py:699
  (5 other events, 12.9 us)

commit v4 on v3

--- a/solution.py
+++ b/solution.py
@@ -122,13 +122,13 @@
             row += 1
 
 
-def add_pairs(kind, motion_ref, pressure_ref, shifted, x, sources, limit, first, last):
+def add_pairs(kind, motion_ref, pressure_ref, shifted, x, sources, limit, first, last, start=0):
     moved, pressed, _, pair, width = kind
     slots = shifted.shape[-2]
     blocks = shifted.shape[2]
     rows = shifted.shape[3]
     group = min(limit // ROWS, 2 if width == 3 else 4)
-    unroll = min(slots, 16 // group if width == 3 else 32 // group)
+    unroll = min(slots - start, 16 // group if width == 3 else 32 // group)
     forms = shifted.shape[1]
     low_col, low_shift = sources[0]
 
@@ -160,7 +160,7 @@
                             totals[v] = pair(mine[v], their, totals[v])
                     return tuple(totals)
 
-                return lax.fori_loop(0, slots // unroll, step, totals)
+                return lax.fori_loop(start // unroll, slots // unroll, step, totals)
 
             totals = tuple(first(x, span, lanes) for span in spans)
             totals = lax.fori_loop(0, forms * len(sources), source, totals)
@@ -220,7 +220,7 @@
     columns, _, slots, width = motion.shape
     moved, pressed, massed, _, outs = kind
     inner = shifts == (0,)
-    mutual = limit == slots
+    mutual = 2 * limit >= slots
     if inner:
         ends_m = ends_p = []
     flat_m = [e for pair in ends_m for e in pair]
@@ -273,23 +273,28 @@
                 add_pairs(kind, motion_ref, pressure_ref, shifted, x, own_sources(x, columns), limit, first, last)
             return
         parts, reaction, packed = mutual_refs
-        if inner:
-            for x in range(columns):
-                add_pairs(kind, motion_ref, pressure_ref, shifted, x, [(x, 0)], limit, first, last)
-        else:
-            out_ref[...] = partial_ref[...]
+
+        def so_far(x, span, lanes):
+            return tuple(out_ref[x, k, span, lanes] for k in range(outs))
+
+        out_ref[...] = jnp.zeros(out_ref.shape, jnp.float32) if partial is None else partial_ref[...]
+        for x in range(columns):
+            for at in own_sources(x, columns):
+                start = 0 if inner and at[0] == x else limit
+                if start < slots:
+                    add_pairs(kind, motion_ref, pressure_ref, shifted, x, [at], limit, so_far, last, start)
         edges = []
         for x in range(columns):
             for col in (x, x + 1):
                 for shift in shifts:
                     if col == columns or (col == x and shift != 1):
                         continue
-                    both_ways(kind, motion_ref, pressure_ref, shifted, x, col, shifts.index(shift), out_ref, parts, reaction)
+                    both_ways(kind, motion_ref, pressure_ref, shifted, x, col, shifts.index(shift), out_ref, parts, reaction, limit)
                     take_reaction(out_ref, reaction, col, shift, outs)
                     if shift:
                         edges.append((col, x, -shift))
         if edges:
-            edge_pairs(kind, motion_ref, pressure_ref, shifted, shifts, edges, out_ref, packed)
+            edge_pairs(kind, motion_ref, pressure_ref, shifted, shifts, edges, out_ref, packed, limit)
 
     return pl.pallas_call(
         kernel,
@@ -299,9 +304,9 @@
         scratch_shapes=[pltpu.VMEM((columns, len(shifts), width // LANES, rows, slots, LANES), jnp.float32)]
         + (
             [
-                pltpu.VMEM((outs, slots, ROWS, LANES), jnp.float32),
-                pltpu.VMEM((outs, width // LANES, slots, LANES), jnp.float32),
-                pltpu.VMEM((rows, slots, LANES), jnp.float32),
+                pltpu.VMEM((outs, limit, ROWS, LANES), jnp.float32),
+                pltpu.VMEM((outs, width // LANES, limit, LANES), jnp.float32),
+                pltpu.VMEM((rows, limit, LANES), jnp.float32),
             ]
             if mutual
             else []
@@ -329,17 +334,17 @@
     return [ref[x, f, span, lanes] * s if s != 1.0 else ref[x, f, span, lanes] for ref, f, s in rows]
 
 
-def both_ways(kind, motion_ref, pressure_ref, shifted, x, col, form, sums, parts, reaction):
+def both_ways(kind, motion_ref, pressure_ref, shifted, x, col, form, sums, parts, reaction, limit):
     outs = kind[4]
-    slots, blocks, rows = shifted.shape[-2], shifted.shape[2], shifted.shape[3]
+    blocks, rows = shifted.shape[2], shifted.shape[3]
     both = both_force if outs == 3 else both_density
     sign = -1.0 if outs == 3 else 1.0
-    group = 2 if outs == 3 else 4
+    group = min(limit // ROWS, 2 if outs == 3 else 4)
     unroll = 8
 
     def lane_block(b, carry):
         lanes = pl.ds(pl.multiple_of(b * LANES, LANES), LANES)
-        for part in range(slots // (ROWS * group)):
+        for part in range(limit // (ROWS * group)):
             spans = [slice((part * group + v) * ROWS, (part * group + v + 1) * ROWS) for v in range(group)]
             mine = []
             for span in spans:
@@ -360,12 +365,12 @@
                 return tuple(totals)
 
             totals = tuple(tuple(sums[x, k, span, lanes] for k in range(outs)) for span in spans)
-            totals = lax.fori_loop(0, slots // unroll, step, totals)
+            totals = lax.fori_loop(0, limit // unroll, step, totals)
             for span, total in zip(spans, totals):
                 for k in range(outs):
                     sums[x, k, span, lanes] = total[k]
         for k in range(outs):
-            for lo in range(0, slots, ROWS):
+            for lo in range(0, limit, ROWS):
                 reaction[k, b, lo : lo + ROWS, :] = sign * sum_rows([parts[k, lo + r] for r in range(ROWS)])
         return carry
 
@@ -388,20 +393,20 @@
             sums[col, k, :, lanes] = sums[col, k, :, lanes] + values[b]
 
 
-def edge_pairs(kind, motion_ref, pressure_ref, shifted, forms, edges, sums, packed):
+def edge_pairs(kind, motion_ref, pressure_ref, shifted, forms, edges, sums, packed, limit):
     pair, outs = kind[3], kind[4]
-    slots, blocks, rows = shifted.shape[-2], shifted.shape[2], shifted.shape[3]
+    blocks, rows = shifted.shape[2], shifted.shape[3]
     lane = lane_of((ROWS, LANES))
     width = blocks * LANES
-    tall = lane_of((slots, LANES))
+    tall = lane_of((limit, LANES))
     for r in range(rows):
-        value = jnp.zeros((slots, LANES), jnp.float32)
+        value = jnp.zeros((limit, LANES), jnp.float32)
         for q, (x, col, shift) in enumerate(edges):
             block, turn = (0, q) if shift == -1 else (blocks - 1, q + 1)
-            value = jnp.where(tall == q, pltpu.roll(shifted[col, forms.index(shift), block, r], turn, 1), value)
+            value = jnp.where(tall == q, pltpu.roll(shifted[col, forms.index(shift), block, r, :limit, :], turn, 1), value)
         packed[r] = value
-    spans = [slice(lo, lo + ROWS) for lo in range(0, slots, ROWS)]
-    group = 2 if outs == 3 else 4
+    spans = [slice(lo, lo + ROWS) for lo in range(0, limit, ROWS)]
+    group = min(limit // ROWS, 2 if outs == 3 else 4)
     unroll = 8
     for part in range(len(spans) // group):
         mine = []
@@ -425,7 +430,7 @@
             return tuple(totals)
 
         zero = jnp.zeros((ROWS, LANES), jnp.float32)
-        totals = lax.fori_loop(0, slots // unroll, step, tuple((zero,) * outs for _ in range(group)))
+        totals = lax.fori_loop(0, limit // unroll, step, tuple((zero,) * outs for _ in range(group)))
         for v, span in enumerate(spans[part * group : (part + 1) * group]):
             for k in range(outs):
                 for q, (x, col, shift) in enumerate(edges):
@@ -627,12 +632,14 @@
     )(destination)
 
 
-def compact(motion, pressure, place, meta, parts, capacity):
+def compact(motion, pressure, place, meta, here, parts, capacity):
     columns, _, slots, width = motion.shape
     chunks = width // LANES
     total = -(-capacity // LANES)
 
-    def kernel(motion_ref, pressure_ref, place_ref, meta_ref, out_ref, local, lists):
+    def kernel(motion_ref, pressure_ref, place_ref, meta_ref, here_ref, *refs):
+        out_refs, (local, lists) = refs[:parts], refs[parts:]
+        target = [lax.rem(here_ref[0] + k, parts) for k in range(parts)]
         lane = lane_of((ROWS, LANES))
 
         def do_group(group, carry):
@@ -660,8 +667,8 @@
                     for c in range(chunks):
                         local[buffer, c + 1] = moved[:, c * LANES : (c + 1) * LANES]
                     for d in range(parts):
-                        base = meta_ref[row, d]
-                        begin = meta_ref[row, parts + d]
+                        base = meta_ref[row, target[d]]
+                        begin = meta_ref[row, parts + target[d]]
                         chunk = lax.shift_right_logical(base, 7)
                         off = lax.bitwise_and(base, LANES - 1)
                         turn = lax.bitwise_and(off - begin, LANES - 1)
@@ -677,21 +684,46 @@
 
         lax.fori_loop(0, slots // ROWS, do_group, 0)
         for d in range(parts):
-            count = meta_ref[slots * columns - 1, 2 * parts + d]
+            count = meta_ref[slots * columns - 1, 2 * parts + target[d]]
             for c in range(total):
-                out_ref[d, :, c * LANES : (c + 1) * LANES] = jnp.where(lane + c * LANES < count, lists[d, c], 0.0)
+                out_refs[d][:, c * LANES : (c + 1) * LANES] = jnp.where(lane + c * LANES < count, lists[d, c], 0.0)
 
     return pl.pallas_call(
         kernel,
-        out_shape=jax.ShapeDtypeStruct((parts, 8, capacity), jnp.float32),
-        in_specs=[VMEM, VMEM, VMEM, SMEM],
-        out_specs=VMEM,
+        out_shape=(jax.ShapeDtypeStruct((8, capacity), jnp.float32),) * parts,
+        in_specs=[VMEM, VMEM, VMEM, SMEM, SMEM],
+        out_specs=(VMEM,) * parts,
         scratch_shapes=[
             pltpu.VMEM((4, 2 * chunks + 4, ROWS, LANES), jnp.float32),
             pltpu.VMEM((parts, total + chunks + 2, ROWS, LANES), jnp.float32),
         ],
         compiler_params=PARAMS,
-    )(motion, pressure, place, meta)
+    )(motion, pressure, place, meta, here)
+
+
+def in_order(here, received):
+    parts = len(received)
+    rows, capacity = received[0].shape
+
+    def kernel(here_ref, *refs):
+        out_ref = refs[parts]
+        for k in range(parts):
+
+            @pl.when(pl.program_id(0) == k)
+            def _():
+                out_ref[...] = refs[k][...]
+
+    return pl.pallas_call(
+        kernel,
+        out_shape=jax.ShapeDtypeStruct((rows, parts * capacity), jnp.float32),
+        grid_spec=pltpu.PrefetchScalarGridSpec(
+            num_scalar_prefetch=1,
+            grid=(parts,),
+            in_specs=[VMEM] * parts,
+            out_specs=pl.BlockSpec((rows, capacity), lambda k, here_ref: (0, lax.rem(here_ref[0] - k + parts, parts))),
+        ),
+        compiler_params=PARAMS,
+    )(here, *received)
 
 
 def pass_on(value, axis, step):
@@ -760,9 +792,12 @@
             motion, pressure, partial, (left_m, right_m), (left_p, right_p), sizes_m, sizes_p, active_counts, level, limit, more
         )
     capacity = 3 * slots * columns * width // 8
-    lists = compact(motion, pressure, place, meta[:, : 3 * parts], parts, capacity)
-    arrived = lax.all_to_all(lists, "sub", split_axis=0, concat_axis=0, tiled=True)
-    return arrived.transpose(1, 0, 2).reshape(8, parts * capacity)
+    here = lax.axis_index("sub").astype(jnp.int32).reshape(1)
+    lists = compact(motion, pressure, place, meta[:, : 3 * parts], here, parts, capacity)
+    received = {0: lists[0]}
+    for k in sorted(range(1, parts), key=lambda k: -min(k, parts - k)):
+        received[k] = pass_on(lists[k], "sub", k)
+    return in_order(here, [received[k] for k in range(parts)])
 
 
 def solution(mesh):

time: 148 us -> 145 us (0.980)
  blocking collectives: 14.1 us -> 0 us
  waiting for transfers between devices: 3.93 us -> 11.4 us
  starting transfers between devices: 40.8 us -> 43.1 us
    all_to_all x1 -> x0, blocking collectives: 14.1 us -> none  [shards(): lax.all_to_all(lists, 'sub', split_axis=0, concat_axis=0, tiled=True)]
    ppermute x24 -> x27, waiting for transfers between devices: 3.93 us -> 11.4 us  [pass_on(): lax.ppermute(value, axis, [(i, (i + step) % count) for i in range(count)])]
    ppermute x24 -> x27, starting transfers between devices: 40.8 us -> 43.1 us  [pass_on(): lax.ppermute(value, axis, [(i, (i + step) % count) for i in range(count)])]
    pallas_call x1 -> x2, Pallas kernels: 4.57 us -> 6.1 us  [the longest x1 4.63 us: compact(): pl.pallas_call(kernel, out_shape=(jax.ShapeDtypeStruct((8, capacity), jnp...]
  transfers between devices with their start and end apart: 24 -> 27, of which waited for: 6 -> 9; matrix products, arithmetic and copies ran while one was open for 0% -> 0% of each run, Pallas kernels for 34% -> 34%
where the time goes in v4:
time: 145 us; the launch traced here: 144 us
  Pallas kernels  86.4 us (60%)
  starting transfers between devices  43.1 us (30%)
  waiting for transfers between devices  11.4 us (8%)
  local copies, waits for them, and re-layouts  2.07 us (1%)
    pallas_call x12, Pallas kernels, own_part(): pl.pallas_call(kernel, out_shape=jax.ShapeDtypeStruct((columns, outs, lim...  48.2 us
    ppermute x27, starting transfers between devices, pass_on(): lax.ppermute(value, axis, [(i, (i + step) % count) for i in range(count)])  43.1 us
    pallas_call x3, Pallas kernels, force_rest(): pl.pallas_call(kernel, out_shape=outs, in_specs=[VMEM] * n_in, out_specs=...  21.2 us
    ppermute x27, waiting for transfers between devices, pass_on(): lax.ppermute(value, axis, [(i, (i + step) % count) for i in range(count)])  11.4 us
    pallas_call x3, Pallas kernels, density_rest(): pl.pallas_call(kernel, out_shape=(jax.ShapeDtypeStruct((columns, PRESSURE...  9.93 us
    pallas_call x1, Pallas kernels, compact(): pl.pallas_call(kernel, out_shape=(jax.ShapeDtypeStruct((8, capacity), jnp...  4.63 us
  transfers between devices with their start and end apart: 27, of which 9 were waited for; matrix products, arithmetic and copies ran while one was open for 0% of the time, Pallas kernels for 34%

profile of v4, /device:TPU:0, one launch (start us, length us, event | category | flops | bytes accessed | tf_op | source)
XLA Modules:
  0.0 143.7 jit_solution(9413528995883727915)
XLA Ops:
  2.6 2.0 %collective-permute-start.1 = (f32[32,128]{1,0:T(8,128)S(1)}, f32[32,128]{1,0:T(8,128)S(1)}, u32[]{:S(2)}, u32[]{:S(2)}) collective-permute-start(f32[32,128]{1,0:T(8,128)S(1)} %get-tuple-element.47), channel_id=1, source_target_pairs={{0,3},{1,0},{2,1},{3,2},{4,7},{5,4},{6,5},{7,6},{8,11},{9,8},{10,9... | collective-permute-start | bytes 49160 | tf_op jit(solution)/shard_map/ppermute | solution.py:731
  4.7 2.5 %shard_map.65.refs_3_ = f32[2,1,32,256]{3,2,1,0:T(8,128)S(1)} custom-call(f32[2,7,32,256]{3,2,1,0:T(8,128)S(1)} %maximum_bitcast_fusion.motion_ref.refs_0_), custom_call_target="tpu_custom_call" | custom-call | flops 471859200 | bytes 1048576 | tf_op jit(solution)/shard_map/pallas_call | solution.py:299
  7.2 2.3 %collective-permute-start.2 = (f32[160,256]{1,0:T(8,128)S(1)}, f32[160,256]{1,0:T(8,128)S(1)}, u32[]{:S(2)}, u32[]{:S(2)}) collective-permute-start(f32[160,256]{1,0:T(8,128)S(1)} %get-tuple-element.112), channel_id=1, source_target_pairs={{0,4},{4,8},{8,12},{12,16},{16,20},{20,24},{24,28},{28,0},{1,5},{5... | collective-permute-start | bytes 491528 | tf_op jit(solution)/shard_map/ppermute | solution.py:731
  9.5 3.1 %collective-permute-start.3 = (f32[160,256]{1,0:T(8,128)S(1)}, f32[160,256]{1,0:T(8,128)S(1)}, u32[]{:S(2)}, u32[]{:S(2)}) collective-permute-start(f32[160,256]{1,0:T(8,128)S(1)} %get-tuple-element.111), channel_id=1, source_target_pairs={{0,28},{4,0},{8,4},{12,8},{16,12},{20,16},{24,20},{28,24},{1,29},{... | collective-permute-start | bytes 491528 | tf_op jit(solution)/shard_map/ppermute | solution.py:731
  12.7 4.8 %shard_map.66.refs_1_ = f32[2,1,32,256]{3,2,1,0:T(8,128)S(1)} custom-call(f32[2,7,32,256]{3,2,1,0:T(8,128)S(1)} %maximum_bitcast_fusion.motion_ref.refs_0_, f32[32,128]{1,0:T(8,128)S(1)} %collective-permute-done.refs_1_.refs_2_.refs_3_.refs_4_.refs_5_.refs_6_, f32[32,128]{1,0:T(8,128)S(1)} %collective-permute-done.1.refs_2_.refs_3_.refs_4_.refs_5_.refs_6_.refs_7_, ...), custom_call_target="tpu_custom_call" | custom-call | flops 943718400 | bytes 1048576 | tf_op jit(solution)/shard_map/pallas_call | solution.py:299
  19.3 5.2 %shard_map.67 = (f32[2,3,32,256]{3,2,1,0:T(8,128)S(1)}, f32[32,128]{1,0:T(8,128)S(1)}, f32[32,128]{1,0:T(8,128)S(1)}) custom-call(f32[2,7,32,256]{3,2,1,0:T(8,128)S(1)} %maximum_bitcast_fusion.motion_ref.refs_0_, f32[2,1,32,256]{3,2,1,0:T(8,128)S(1)} %shard_map.66.refs_1_, f32[2,32,256]{2,1,0:T(8,128)S(1)} %bitcast.35, s32[3,2,256]{2,1,0:T(2,128)S(1)} %copy-done, ...), custom_call_target="tpu_custom_call" | custom-call | flops 707788800 | bytes 1048576 | tf_op jit(solution)/shard_map/pallas_call | solution.py:523
  26.4 5.8 %shard_map.68.refs_6_ = f32[2,3,32,256]{3,2,1,0:T(8,128)S(1)} custom-call(f32[2,7,32,256]{3,2,1,0:T(8,128)S(1)} %maximum_bitcast_fusion.motion_ref.refs_0_, f32[2,3,32,256]{3,2,1,0:T(8,128)S(1)} %get-tuple-element.51.refs_1_.refs_4_), custom_call_target="tpu_custom_call" | custom-call | flops 943718400 | bytes 1048576 | tf_op jit(solution)/shard_map/pallas_call | solution.py:299
  32.6 4.4 %collective-permute-start.7 = (f32[224,256]{1,0:T(8,128)S(1)}, f32[224,256]{1,0:T(8,128)S(1)}, u32[]{:S(2)}, u32[]{:S(2)}) collective-permute-start(f32[224,256]{1,0:T(8,128)S(1)} %get-tuple-element.109), channel_id=1, source_target_pairs={{0,28},{4,0},{8,4},{12,8},{16,12},{20,16},{24,20},{28,24},{1,29},{... | collective-permute-start | bytes 688136 | tf_op jit(solution)/shard_map/ppermute | solution.py:731
  37.0 10.9 %shard_map.69.refs_2_ = f32[2,3,32,256]{3,2,1,0:T(8,128)S(1)} custom-call(f32[2,7,32,256]{3,2,1,0:T(8,128)S(1)} %maximum_bitcast_fusion.motion_ref.refs_0_, f32[2,3,32,256]{3,2,1,0:T(8,128)S(1)} %get-tuple-element.51.refs_1_.refs_4_, f32[32,128]{1,0:T(8,128)S(1)} %collective-permute-done.refs_1_.refs_2_.refs_3_.refs_4_.refs_5_.refs_6_, ...), custom_call_target="tpu_custom_call" | custom-call | flops 1887436800 | bytes 1048576 | tf_op jit(solution)/shard_map/pallas_call | solution.py:299
  48.0 11.6 %shard_map.70 = (f32[2,7,32,256]{3,2,1,0:T(8,128)S(1)}, f32[32,128]{1,0:T(8,128)S(1)}, f32[32,128]{1,0:T(8,128)S(1)}) custom-call(f32[2,7,32,256]{3,2,1,0:T(8,128)S(1)} %maximum_bitcast_fusion.motion_ref.refs_0_, f32[2,3,32,256]{3,2,1,0:T(8,128)S(1)} %get-tuple-element.51.refs_1_.refs_4_, f32[2,3,32,256]{3,2,1,0:T(8,128)S(1)} %shard_map.69.refs_2_, ...), custom_call_target="tpu_custom_call" | custom-call | flops 1415577600 | bytes 1048576 | tf_op jit(solution)/shard_map/pallas_call | solution.py:584
  63.0 4.7 %collective-permute-start.11 = (f32[128,256]{1,0:T(8,128)S(1)}, f32[128,256]{1,0:T(8,128)S(1)}, u32[]{:S(2)}, u32[]{:S(2)}) collective-permute-start(f32[128,256]{1,0:T(8,128)S(1)} %get-tuple-element.107), channel_id=1, source_target_pairs={{0,28},{4,0},{8,4},{12,8},{16,12},{20,16},{24,20},{28,24},{1,29},{... | collective-permute-start | bytes 393224 | tf_op jit(solution)/shard_map/ppermute | solution.py:731
  67.7 3.5 %shard_map.72.refs_1_ = f32[2,1,16,256]{3,2,1,0:T(8,128)S(1)} custom-call(f32[2,7,32,256]{3,2,1,0:T(8,128)S(1)} %get-tuple-element.57.refs_0_, f32[32,128]{1,0:T(8,128)S(1)} %collective-permute-done.8.refs_1_.refs_2_.refs_3_.refs_4_, f32[32,128]{1,0:T(8,128)S(1)} %collective-permute-done.9.refs_2_.refs_3_.refs_4_.refs_5_, ...), custom_call_target="tpu_custom_call" | custom-call | flops 471859200 | bytes 1048576 | tf_op jit(solution)/shard_map/pallas_call | solution.py:299
  71.8 3.0 %shard_map.73 = (f32[2,3,32,256]{3,2,1,0:T(8,128)S(1)}, f32[16,128]{1,0:T(8,128)S(1)}, f32[16,128]{1,0:T(8,128)S(1)}) custom-call(f32[2,7,32,256]{3,2,1,0:T(8,128)S(1)} %get-tuple-element.57.refs_0_, f32[2,1,16,256]{3,2,1,0:T(8,128)S(1)} %shard_map.72.refs_1_, f32[2,32,256]{2,1,0:T(8,128)S(1)} %bitcast.36, s32[3,2,256]{2,1,0:T(2,128)S(1)} %copy-done, ...), custom_call_target="tpu_custom_call" | custom-call | flops 353894400 | bytes 1048576 | tf_op jit(solution)/shard_map/pallas_call | solution.py:523
  76.6 3.3 %shard_map.74.refs_10_ = f32[2,3,16,256]{3,2,1,0:T(8,128)S(1)} custom-call(f32[2,7,32,256]{3,2,1,0:T(8,128)S(1)} %get-tuple-element.57.refs_0_, f32[2,3,32,256]{3,2,1,0:T(8,128)S(1)} %get-tuple-element.63.refs_1_.refs_4_), custom_call_target="tpu_custom_call" | custom-call | flops 471859200 | bytes 1048576 | tf_op jit(solution)/shard_map/pallas_call | solution.py:299
  80.2 4.5 %collective-permute-start.15 = (f32[160,256]{1,0:T(8,128)S(1)}, f32[160,256]{1,0:T(8,128)S(1)}, u32[]{:S(2)}, u32[]{:S(2)}) collective-permute-start(f32[160,256]{1,0:T(8,128)S(1)} %get-tuple-element.115), channel_id=1, source_target_pairs={{0,28},{4,0},{8,4},{12,8},{16,12},{20,16},{24,20},{28,24},{1,29},{... | collective-permute-start | bytes 491528 | tf_op jit(solution)/shard_map/ppermute | solution.py:731
  84.7 7.3 %shard_map.75.refs_2_ = f32[2,3,16,256]{3,2,1,0:T(8,128)S(1)} custom-call(f32[2,7,32,256]{3,2,1,0:T(8,128)S(1)} %get-tuple-element.57.refs_0_, f32[2,3,32,256]{3,2,1,0:T(8,128)S(1)} %get-tuple-element.63.refs_1_.refs_4_, f32[32,128]{1,0:T(8,128)S(1)} %collective-permute-done.8.refs_1_.refs_2_.refs_3_.refs_4_, ...), custom_call_target="tpu_custom_call" | custom-call | flops 943718400 | bytes 1048576 | tf_op jit(solution)/shard_map/pallas_call | solution.py:299
  92.1 6.1 %shard_map.76 = (f32[2,7,32,256]{3,2,1,0:T(8,128)S(1)}, f32[16,128]{1,0:T(8,128)S(1)}, f32[16,128]{1,0:T(8,128)S(1)}) custom-call(f32[2,7,32,256]{3,2,1,0:T(8,128)S(1)} %get-tuple-element.57.refs_0_, f32[2,3,32,256]{3,2,1,0:T(8,128)S(1)} %get-tuple-element.63.refs_1_.refs_4_, f32[2,3,16,256]{3,2,1,0:T(8,128)S(1)} %shard_map.75.refs_2_, ...), custom_call_target="tpu_custom_call" | custom-call | flops 707788800 | bytes 1048576 | tf_op jit(solution)/shard_map/pallas_call | solution.py:584
  101.5 4.7 %collective-permute-start.19 = (f32[64,256]{1,0:T(8,128)S(1)}, f32[64,256]{1,0:T(8,128)S(1)}, u32[]{:S(2)}, u32[]{:S(2)}) collective-permute-start(f32[64,256]{1,0:T(8,128)S(1)} %get-tuple-element.113), channel_id=1, source_target_pairs={{0,28},{4,0},{8,4},{12,8},{16,12},{20,16},{24,20},{28,24},{1,29},{... | collective-permute-start | bytes 196616 | tf_op jit(solution)/shard_map/ppermute | solution.py:731
  106.2 2.0 %shard_map.78.refs_1_ = f32[2,1,8,256]{3,2,1,0:T(8,128)S(1)} custom-call(f32[2,7,32,256]{3,2,1,0:T(8,128)S(1)} %get-tuple-element.69.refs_0_, f32[16,128]{1,0:T(8,128)S(1)} %collective-permute-done.16.refs_1_.refs_2_, f32[16,128]{1,0:T(8,128)S(1)} %collective-permute-done.17.refs_2_.refs_3_, ...), custom_call_target="tpu_custom_call" | custom-call | flops 235929600 | bytes 1048576 | tf_op jit(solution)/shard_map/pallas_call | solution.py:299
  114.5 4.7 %collective-permute-start.23 = (f32[80,256]{1,0:T(8,128)S(1)}, f32[80,256]{1,0:T(8,128)S(1)}, u32[]{:S(2)}, u32[]{:S(2)}) collective-permute-start(f32[80,256]{1,0:T(8,128)S(1)} %get-tuple-element.117), channel_id=1, source_target_pairs={{0,28},{4,0},{8,4},{12,8},{16,12},{20,16},{24,20},{28,24},{1,29},{... | collective-permute-start | bytes 245768 | tf_op jit(solution)/shard_map/ppermute | solution.py:731
  120.1 4.2 %shard_map.81.refs_2_ = f32[2,3,8,256]{3,2,1,0:T(8,128)S(1)} custom-call(f32[2,7,32,256]{3,2,1,0:T(8,128)S(1)} %get-tuple-element.69.refs_0_, f32[2,3,32,256]{3,2,1,0:T(8,128)S(1)} %get-tuple-element.75.refs_1_.pressure_ref, f32[16,128]{1,0:T(8,128)S(1)} %collective-permute-done.16.refs_1_.refs_2_, f32[16,128]{1,0:T(8,128)S(1)} %collective-permute-done.17.refs_2_.refs_3_, ...), custom_call_target="tpu_custom_call" | custom-call | flops 471859200 | bytes 1048576 | tf_op jit(solution)/shard_map/pallas_call | solution.py:299
  124.3 3.4 %shard_map.82.motion_ref = f32[2,7,32,256]{3,2,1,0:T(8,128)S(1)} custom-call(f32[2,7,32,256]{3,2,1,0:T(8,128)S(1)} %get-tuple-element.69.refs_0_, f32[2,3,32,256]{3,2,1,0:T(8,128)S(1)} %get-tuple-element.75.refs_1_.pressure_ref, f32[2,3,8,256]{3,2,1,0:T(8,128)S(1)} %shard_map.81.refs_2_, s32[3,2,256]{2,1,0:T(2,128)S(1)} %copy-done, ...), custom_call_target="tpu_custom_call" | custom-call | flops 353894400 | bytes 1048576 | tf_op jit(solution)/shard_map/pallas_call | solution.py:584
  127.8 4.6 %shard_map.84 = (f32[8,6144]{1,0:T(8,128)S(1)}, f32[8,6144]{1,0:T(8,128)S(1)}, f32[8,6144]{1,0:T(8,128)S(1)}, f32[8,6144]{1,0:T(8,128)S(1)}) custom-call(f32[2,7,32,256]{3,2,1,0:T(8,128)S(1)} %shard_map.82.motion_ref, f32[2,3,32,256]{3,2,1,0:T(8,128)S(1)} %get-tuple-element.75.refs_1_.pressure_ref, s32[64,256]{1,0:T(8,128)S(1)} %get-tuple-element.81.place_ref, ...), custom_call_target="tpu_custom_call" | custom-call | tf_op jit(solution)/shard_map/pallas_call | solution.py:691
  134.7 4.3 %collective-permute-done.24.refs_1_ = f32[8,6144]{1,0:T(8,128)S(1)} collective-permute-done((f32[8,6144]{1,0:T(8,128)S(1)}, f32[8,6144]{1,0:T(8,128)S(1)}, u32[]{:S(2)}, u32[]{:S(2)}) %collective-permute-start.24) | collective-permute-done | bytes 196640 | tf_op jit(solution)/shard_map/ppermute | solution.py:731
  (94 shorter events, 30.2 us)
Async XLA Ops:
  2.1 5.0 %collective-permute-start = (f32[32,128]{1,0:T(8,128)S(1)}, f32[32,128]{1,0:T(8,128)S(1)}, u32[]{:S(2)}, u32[]{:S(2)}) collective-permute-start(f32[32,128]{1,0:T(8,128)S(1)} %get-tuple-element.46), channel_id=1, source_target_pairs={{0,1},{1,2},{2,3},{3,0},{4,5},{5,6},{6,7},{7,4},{8,9},{9,10},{10,1... | collective-permute-start | bytes 49160 | tf_op jit(solution)/shard_map/ppermute | solution.py:731
  2.6 4.5 %collective-permute-start.1 = (f32[32,128]{1,0:T(8,128)S(1)}, f32[32,128]{1,0:T(8,128)S(1)}, u32[]{:S(2)}, u32[]{:S(2)}) collective-permute-start(f32[32,128]{1,0:T(8,128)S(1)} %get-tuple-element.47), channel_id=1, source_target_pairs={{0,3},{1,0},{2,1},{3,2},{4,7},{5,4},{6,5},{7,6},{8,11},{9,8},{10,9... | collective-permute-start | bytes 49160 | tf_op jit(solution)/shard_map/ppermute | solution.py:731
  7.2 10.3 %collective-permute-start.2 = (f32[160,256]{1,0:T(8,128)S(1)}, f32[160,256]{1,0:T(8,128)S(1)}, u32[]{:S(2)}, u32[]{:S(2)}) collective-permute-start(f32[160,256]{1,0:T(8,128)S(1)} %get-tuple-element.112), channel_id=1, source_target_pairs={{0,4},{4,8},{8,12},{12,16},{16,20},{20,24},{24,28},{28,0},{1,5},{5... | collective-permute-start | bytes 491528 | tf_op jit(solution)/shard_map/ppermute | solution.py:731
  9.5 9.8 %collective-permute-start.3 = (f32[160,256]{1,0:T(8,128)S(1)}, f32[160,256]{1,0:T(8,128)S(1)}, u32[]{:S(2)}, u32[]{:S(2)}) collective-permute-start(f32[160,256]{1,0:T(8,128)S(1)} %get-tuple-element.111), channel_id=1, source_target_pairs={{0,28},{4,0},{8,4},{12,8},{16,12},{20,16},{24,20},{28,24},{1,29},{... | collective-permute-start | bytes 491528 | tf_op jit(solution)/shard_map/ppermute | solution.py:731
  24.6 7.6 %collective-permute-start.4 = (f32[32,128]{1,0:T(8,128)S(1)}, f32[32,128]{1,0:T(8,128)S(1)}, u32[]{:S(2)}, u32[]{:S(2)}) collective-permute-start(f32[32,128]{1,0:T(8,128)S(1)} %get-tuple-element.52), channel_id=1, source_target_pairs={{0,1},{1,2},{2,3},{3,0},{4,5},{5,6},{6,7},{7,4},{8,9},{9,10},{10,1... | collective-permute-start | bytes 49160 | tf_op jit(solution)/shard_map/ppermute | solution.py:731
  24.6 7.5 %collective-permute-start.5 = (f32[32,128]{1,0:T(8,128)S(1)}, f32[32,128]{1,0:T(8,128)S(1)}, u32[]{:S(2)}, u32[]{:S(2)}) collective-permute-start(f32[32,128]{1,0:T(8,128)S(1)} %get-tuple-element.53), channel_id=1, source_target_pairs={{0,3},{1,0},{2,1},{3,2},{4,7},{5,4},{6,5},{7,6},{8,11},{9,8},{10,9... | collective-permute-start | bytes 49160 | tf_op jit(solution)/shard_map/ppermute | solution.py:731
  32.2 15.7 %collective-permute-start.6 = (f32[224,256]{1,0:T(8,128)S(1)}, f32[224,256]{1,0:T(8,128)S(1)}, u32[]{:S(2)}, u32[]{:S(2)}) collective-permute-start(f32[224,256]{1,0:T(8,128)S(1)} %get-tuple-element.110), channel_id=1, source_target_pairs={{0,4},{4,8},{8,12},{12,16},{16,20},{20,24},{24,28},{28,0},{1,5},{5... | collective-permute-start | bytes 688136 | tf_op jit(solution)/shard_map/ppermute | solution.py:731
  32.6 15.4 %collective-permute-start.7 = (f32[224,256]{1,0:T(8,128)S(1)}, f32[224,256]{1,0:T(8,128)S(1)}, u32[]{:S(2)}, u32[]{:S(2)}) collective-permute-start(f32[224,256]{1,0:T(8,128)S(1)} %get-tuple-element.109), channel_id=1, source_target_pairs={{0,28},{4,0},{8,4},{12,8},{16,12},{20,16},{24,20},{28,24},{1,29},{... | collective-permute-start | bytes 688136 | tf_op jit(solution)/shard_map/ppermute | solution.py:731
  59.6 3.2 %collective-permute-start.8 = (f32[32,128]{1,0:T(8,128)S(1)}, f32[32,128]{1,0:T(8,128)S(1)}, u32[]{:S(2)}, u32[]{:S(2)}) collective-permute-start(f32[32,128]{1,0:T(8,128)S(1)} %get-tuple-element.58), channel_id=1, source_target_pairs={{0,1},{1,2},{2,3},{3,0},{4,5},{5,6},{6,7},{7,4},{8,9},{9,10},{10,1... | collective-permute-start | bytes 49160 | tf_op jit(solution)/shard_map/ppermute | solution.py:731
  62.9 8.8 %collective-permute-start.10 = (f32[128,256]{1,0:T(8,128)S(1)}, f32[128,256]{1,0:T(8,128)S(1)}, u32[]{:S(2)}, u32[]{:S(2)}) collective-permute-start(f32[128,256]{1,0:T(8,128)S(1)} %get-tuple-element.108), channel_id=1, source_target_pairs={{0,4},{4,8},{8,12},{12,16},{16,20},{20,24},{24,28},{28,0},{1,5},{5... | collective-permute-start | bytes 393224 | tf_op jit(solution)/shard_map/ppermute | solution.py:731
  63.0 8.8 %collective-permute-start.11 = (f32[128,256]{1,0:T(8,128)S(1)}, f32[128,256]{1,0:T(8,128)S(1)}, u32[]{:S(2)}, u32[]{:S(2)}) collective-permute-start(f32[128,256]{1,0:T(8,128)S(1)} %get-tuple-element.107), channel_id=1, source_target_pairs={{0,28},{4,0},{8,4},{12,8},{16,12},{20,16},{24,20},{28,24},{1,29},{... | collective-permute-start | bytes 393224 | tf_op jit(solution)/shard_map/ppermute | solution.py:731
  74.8 5.1 %collective-permute-start.12 = (f32[16,128]{1,0:T(8,128)S(1)}, f32[16,128]{1,0:T(8,128)S(1)}, u32[]{:S(2)}, u32[]{:S(2)}) collective-permute-start(f32[16,128]{1,0:T(8,128)S(1)} %get-tuple-element.64), channel_id=1, source_target_pairs={{0,1},{1,2},{2,3},{3,0},{4,5},{5,6},{6,7},{7,4},{8,9},{9,10},{10,1... | collective-permute-start | bytes 24584 | tf_op jit(solution)/shard_map/ppermute | solution.py:731
  74.8 5.1 %collective-permute-start.13 = (f32[16,128]{1,0:T(8,128)S(1)}, f32[16,128]{1,0:T(8,128)S(1)}, u32[]{:S(2)}, u32[]{:S(2)}) collective-permute-start(f32[16,128]{1,0:T(8,128)S(1)} %get-tuple-element.65), channel_id=1, source_target_pairs={{0,3},{1,0},{2,1},{3,2},{4,7},{5,4},{6,5},{7,6},{8,11},{9,8},{10,9... | collective-permute-start | bytes 24584 | tf_op jit(solution)/shard_map/ppermute | solution.py:731
  80.0 12.1 %collective-permute-start.14 = (f32[160,256]{1,0:T(8,128)S(1)}, f32[160,256]{1,0:T(8,128)S(1)}, u32[]{:S(2)}, u32[]{:S(2)}) collective-permute-start(f32[160,256]{1,0:T(8,128)S(1)} %get-tuple-element.116), channel_id=1, source_target_pairs={{0,4},{4,8},{8,12},{12,16},{16,20},{20,24},{24,28},{28,0},{1,5},{5... | collective-permute-start | bytes 491528 | tf_op jit(solution)/shard_map/ppermute | solution.py:731
  80.2 11.8 %collective-permute-start.15 = (f32[160,256]{1,0:T(8,128)S(1)}, f32[160,256]{1,0:T(8,128)S(1)}, u32[]{:S(2)}, u32[]{:S(2)}) collective-permute-start(f32[160,256]{1,0:T(8,128)S(1)} %get-tuple-element.115), channel_id=1, source_target_pairs={{0,28},{4,0},{8,4},{12,8},{16,12},{20,16},{24,20},{28,24},{1,29},{... | collective-permute-start | bytes 491528 | tf_op jit(solution)/shard_map/ppermute | solution.py:731
  101.4 7.5 %collective-permute-start.18 = (f32[64,256]{1,0:T(8,128)S(1)}, f32[64,256]{1,0:T(8,128)S(1)}, u32[]{:S(2)}, u32[]{:S(2)}) collective-permute-start(f32[64,256]{1,0:T(8,128)S(1)} %get-tuple-element.114), channel_id=1, source_target_pairs={{0,4},{4,8},{8,12},{12,16},{16,20},{20,24},{24,28},{28,0},{1,5},{5... | collective-permute-start | bytes 196616 | tf_op jit(solution)/shard_map/ppermute | solution.py:731
  101.5 7.5 %collective-permute-start.19 = (f32[64,256]{1,0:T(8,128)S(1)}, f32[64,256]{1,0:T(8,128)S(1)}, u32[]{:S(2)}, u32[]{:S(2)}) collective-permute-start(f32[64,256]{1,0:T(8,128)S(1)} %get-tuple-element.113), channel_id=1, source_target_pairs={{0,28},{4,0},{8,4},{12,8},{16,12},{20,16},{24,20},{28,24},{1,29},{... | collective-permute-start | bytes 196616 | tf_op jit(solution)/shard_map/ppermute | solution.py:731
  110.7 3.6 %collective-permute-start.20 = (f32[8,128]{1,0:T(8,128)S(1)}, f32[8,128]{1,0:T(8,128)S(1)}, u32[]{:S(2)}, u32[]{:S(2)}) collective-permute-start(f32[8,128]{1,0:T(8,128)S(1)} %get-tuple-element.76), channel_id=1, source_target_pairs={{0,1},{1,2},{2,3},{3,0},{4,5},{5,6},{6,7},{7,4},{8,9},{9,10},{10,1... | collective-permute-start | bytes 12296 | tf_op jit(solution)/shard_map/ppermute | solution.py:731
  110.8 3.6 %collective-permute-start.21 = (f32[8,128]{1,0:T(8,128)S(1)}, f32[8,128]{1,0:T(8,128)S(1)}, u32[]{:S(2)}, u32[]{:S(2)}) collective-permute-start(f32[8,128]{1,0:T(8,128)S(1)} %get-tuple-element.77), channel_id=1, source_target_pairs={{0,3},{1,0},{2,1},{3,2},{4,7},{5,4},{6,5},{7,6},{8,11},{9,8},{10,9... | collective-permute-start | bytes 12296 | tf_op jit(solution)/shard_map/ppermute | solution.py:731
  114.4 9.9 %collective-permute-start.22 = (f32[80,256]{1,0:T(8,128)S(1)}, f32[80,256]{1,0:T(8,128)S(1)}, u32[]{:S(2)}, u32[]{:S(2)}) collective-permute-start(f32[80,256]{1,0:T(8,128)S(1)} %get-tuple-element.118), channel_id=1, source_target_pairs={{0,4},{4,8},{8,12},{12,16},{16,20},{20,24},{24,28},{28,0},{1,5},{5... | collective-permute-start | bytes 245768 | tf_op jit(solution)/shard_map/ppermute | solution.py:731
  114.5 9.8 %collective-permute-start.23 = (f32[80,256]{1,0:T(8,128)S(1)}, f32[80,256]{1,0:T(8,128)S(1)}, u32[]{:S(2)}, u32[]{:S(2)}) collective-permute-start(f32[80,256]{1,0:T(8,128)S(1)} %get-tuple-element.117), channel_id=1, source_target_pairs={{0,28},{4,0},{8,4},{12,8},{16,12},{20,16},{24,20},{28,24},{1,29},{... | collective-permute-start | bytes 245768 | tf_op jit(solution)/shard_map/ppermute | solution.py:731
  132.4 6.6 %collective-permute-start.24 = (f32[8,6144]{1,0:T(8,128)S(1)}, f32[8,6144]{1,0:T(8,128)S(1)}, u32[]{:S(2)}, u32[]{:S(2)}) collective-permute-start(f32[8,6144]{1,0:T(8,128)S(1)} %get-tuple-element.84), channel_id=1, source_target_pairs={{0,1},{1,2},{2,3},{3,0},{4,5},{5,6},{6,7},{7,4},{8,9},{9,10},{10,1... | collective-permute-start | bytes 589832 | tf_op jit(solution)/shard_map/ppermute | solution.py:731
  132.5 7.8 %collective-permute-start.25 = (f32[8,6144]{1,0:T(8,128)S(1)}, f32[8,6144]{1,0:T(8,128)S(1)}, u32[]{:S(2)}, u32[]{:S(2)}) collective-permute-start(f32[8,6144]{1,0:T(8,128)S(1)} %get-tuple-element.85), channel_id=1, source_target_pairs={{0,2},{1,3},{2,0},{3,1},{4,6},{5,7},{6,4},{7,5},{8,10},{9,11},{10,... | collective-permute-start | bytes 589832 | tf_op jit(solution)/shard_map/ppermute | solution.py:731
  133.5 8.7 %collective-permute-start.26 = (f32[8,6144]{1,0:T(8,128)S(1)}, f32[8,6144]{1,0:T(8,128)S(1)}, u32[]{:S(2)}, u32[]{:S(2)}) collective-permute-start(f32[8,6144]{1,0:T(8,128)S(1)} %get-tuple-element.86), channel_id=1, source_target_pairs={{0,3},{1,0},{2,1},{3,2},{4,7},{5,4},{6,5},{7,6},{8,11},{9,8},{10,9... | collective-permute-start | bytes 589832 | tf_op jit(solution)/shard_map/ppermute | solution.py:731
  (8 other events, 22.3 us)

commit v5 on v4

--- a/solution.py
+++ b/solution.py
@@ -16,9 +16,10 @@
 ROWS = 8
 VMEM = pl.BlockSpec(memory_space=pltpu.VMEM)
 SMEM = pl.BlockSpec(memory_space=pltpu.SMEM)
-PARAMS = pltpu.CompilerParams(vmem_limit_bytes=40 << 20)
+PARAMS = pltpu.CompilerParams(vmem_limit_bytes=24 << 20)
 MOTION, PRESSURE = 7, 3
 SHIFTS = (-1, 0, 1)
+KEEP = ((True, True, True), (True, True, True), (False, False, False))
 
 
 def lane_of(shape):
@@ -29,52 +30,59 @@
     return pl.CostEstimate(flops=int(pairs * ops * 15), bytes_accessed=1 << 20, transcendentals=0)
 
 
-def force_core(own, their):
-    xi, yi, zi, ui, vi, wi, qi, ci, ri = own[:9]
-    xj, yj, zj, uj, vj, wj, qj, cj, rj = their[:9]
-    dx, dy, dz = xi - xj, yi - yj, zi - zj
-    squared = dx * dx + dy * dy + dz * dz
-    radius = squared * lax.rsqrt(jnp.maximum(squared, 1e-30))
-    remain = jnp.maximum(1.0 - radius, 0.0)
-    approach = dx * (ui - uj) + dy * (vi - vj) + dz * (wi - wj)
-    closing = jnp.minimum(approach, 0.0) * pl.reciprocal(squared + SOFTEN, approx=True)
-    viscous = closing * (closing - (ci + cj)) * pl.reciprocal(ri + rj, approx=True)
-    return (dx, dy, dz), (qi + qj + viscous), remain
-
-
-def density_core(own, their):
-    xi, yi, zi = own[:3]
-    xj, yj, zj = their[:3]
-    dx, dy, dz = xi - xj, yi - yj, zi - zj
+def closeness(delta):
+    dx, dy, dz = delta
     squared = dx * dx + dy * dy + dz * dz
     radius = squared * lax.rsqrt(jnp.maximum(squared, 1e-30))
     return jnp.maximum(1.0 - radius, 0.0)
 
 
-def pair_force(own, their, total):
-    delta, pressure, remain = force_core(own, their)
+def displacement(own, their):
+    return tuple(i - j for i, j in zip(own[:3], their[:3]))
+
+
+def force_core(own, their, remain):
+    ui, vi, wi, qi, ci, ri = own[3:9]
+    uj, vj, wj, qj, cj, rj = their[3:9]
+    dx, dy, dz = displacement(own, their)
+    radius = 1.0 - remain
+    approach = dx * (ui - uj) + dy * (vi - vj) + dz * (wi - wj)
+    closing = jnp.minimum(approach, 0.0) * pl.reciprocal(radius * radius + SOFTEN, approx=True)
+    viscous = closing * (closing - (ci + cj)) * pl.reciprocal(ri + rj, approx=True)
+    return (dx, dy, dz), qi + qj + viscous
+
+
+def pair_force(own, their, total, remain):
+    delta, pressure = force_core(own, their, remain)
     strength = pressure * ((remain * remain) * (remain * their[-1]))
     return tuple(t + strength * d for t, d in zip(total, delta))
 
 
-def pair_density(own, their, total):
-    remain = density_core(own, their)
+def pair_density(own, their, total, remain):
     square = remain * remain
     return (total[0] + (square * square) * ((5.0 - 4.0 * remain) * their[-1]),)
 
 
-def both_force(own, their, total):
-    delta, pressure, remain = force_core(own, their)
+def both_force(own, their, total, remain):
+    delta, pressure = force_core(own, their, remain)
     strength = pressure * ((remain * remain) * remain)
     on_own, on_their = strength * their[-1], strength * own[-1]
     return tuple(t + on_own * d for t, d in zip(total, delta)), tuple(on_their * d for d in delta)
 
 
-def both_density(own, their, total):
-    remain = density_core(own, their)
+def both_density(own, their, total, remain):
     square = remain * remain
     weight = (square * square) * (5.0 - 4.0 * remain)
     return (total[0] + weight * their[-1],), (weight * own[-1],)
+
+
+def kept(kept_ref, at, own, their, first):
+    if kept_ref is not None and not first:
+        return kept_ref[at]
+    value = closeness(displacement(own, their))
+    if kept_ref is not None:
+        kept_ref[at] = value
+    return value
 
 
 DENSITY = ((0, 1.0), (1, 1.0), (2, 1.0)), (), ((6, KERNEL_NORM),), pair_density, 1
@@ -122,7 +130,7 @@
             row += 1
 
 
-def add_pairs(kind, motion_ref, pressure_ref, shifted, x, sources, limit, first, last, start=0):
+def add_pairs(kind, motion_ref, pressure_ref, shifted, x, sources, limit, first, last, kept_ref, unit, start=0):
     moved, pressed, _, pair, width = kind
     slots = shifted.shape[-2]
     blocks = shifted.shape[2]
@@ -157,7 +165,9 @@
                             for r in range(rows)
                         ]
                         for v in range(group):
-                            totals[v] = pair(mine[v], their, totals[v])
+                            place = (unit + at, b, slot, part * group + v)
+                            remain = kept(kept_ref, place, mine[v], their, width == 1)
+                            totals[v] = pair(mine[v], their, totals[v], remain)
                     return tuple(totals)
 
                 return lax.fori_loop(start // unroll, slots // unroll, step, totals)
@@ -216,7 +226,7 @@
     return spans
 
 
-def own_part(kind, motion, pressure, ends_m, ends_p, limit, shifts, partial=None):
+def own_part(kind, motion, pressure, ends_m, ends_p, limit, shifts, partial=None, closeness_kept=None, keep=False):
     columns, _, slots, width = motion.shape
     moved, pressed, massed, _, outs = kind
     inner = shifts == (0,)
@@ -229,19 +239,39 @@
     spans_m = whole if inner else bounds_of([e[0].shape[0] for e in ends_m])
     spans_p = whole if inner else bounds_of([e[0].shape[0] for e in ends_p])
     inputs = [motion] + ([pressure] if pressed else []) + flat_m + flat_p + ([] if partial is None else [partial])
+    n_in = len(inputs)
+    calls = []
+    for x in range(columns):
+        for col, _ in own_sources(x, columns):
+            start = limit if mutual and not (inner and col == x) else 0
+            if start < slots:
+                calls.append((x, col, start, None))
+    if mutual:
+        for x in range(columns):
+            for col in (x, x + 1):
+                for form, shift in enumerate(shifts):
+                    if col < columns and (col != x or shift == 1):
+                        calls.append((x, col, 0, form))
+    units = sum(len(shifts) if form is None else 1 for *_, form in calls)
+    kept_shape = jax.ShapeDtypeStruct((units, width // LANES, slots, limit // ROWS, ROWS, LANES), jnp.float32)
+    keep = keep and not pressed
+    if closeness_kept is not None:
+        inputs.append(closeness_kept)
     rows = len(moved) + len(pressed) + len(massed)
 
-    def kernel(*refs):
-        refs = list(refs)
+    def kernel(*own_refs):
+        refs = list(own_refs)
         motion_ref = refs.pop(0)
         pressure_ref = refs.pop(0) if pressed else None
         m_refs = refs[: len(flat_m)]
         p_refs = refs[len(flat_m) : len(flat_m) + len(flat_p)]
-        if mutual:
-            *refs, parts, reaction, packed = refs
-            mutual_refs = (parts, reaction, packed)
-        partial_ref = None if partial is None else refs[-3]
-        out_ref, shifted = refs[-2:]
+        partial_ref = None if partial is None else own_refs[n_in - 1]
+        left = list(own_refs[n_in:])
+        kept_ref = None if closeness_kept is None else left.pop(0)
+        out_ref = left.pop(0)
+        if keep:
+            kept_ref = left.pop(0)
+        shifted, *mutual_refs = left
 
         def pieces(cells, ends, spans):
             if inner:
@@ -257,50 +287,40 @@
                 return pieces(pressure_ref.at[c, field], p_refs, spans_p)
 
             fill_column(shifted, c, kind, motion_pieces, pressure_pieces, lambda f: f * columns + c, shifts)
-        zero = jnp.zeros((ROWS, LANES), jnp.float32)
 
         def first(x, span, lanes):
-            if partial is None:
-                return (zero,) * outs
-            return tuple(partial_ref[x, k, span, lanes] for k in range(outs))
+            return tuple(out_ref[x, k, span, lanes] for k in range(outs))
 
         def last(x, span, lanes, total):
             for k in range(outs):
                 out_ref[x, k, span, lanes] = total[k]
 
-        if not mutual:
-            for x in range(columns):
-                add_pairs(kind, motion_ref, pressure_ref, shifted, x, own_sources(x, columns), limit, first, last)
-            return
-        parts, reaction, packed = mutual_refs
-
-        def so_far(x, span, lanes):
-            return tuple(out_ref[x, k, span, lanes] for k in range(outs))
-
         out_ref[...] = jnp.zeros(out_ref.shape, jnp.float32) if partial is None else partial_ref[...]
-        for x in range(columns):
-            for at in own_sources(x, columns):
-                start = 0 if inner and at[0] == x else limit
-                if start < slots:
-                    add_pairs(kind, motion_ref, pressure_ref, shifted, x, [at], limit, so_far, last, start)
-        edges = []
-        for x in range(columns):
-            for col in (x, x + 1):
-                for shift in shifts:
-                    if col == columns or (col == x and shift != 1):
-                        continue
-                    both_ways(kind, motion_ref, pressure_ref, shifted, x, col, shifts.index(shift), out_ref, parts, reaction, limit)
-                    take_reaction(out_ref, reaction, col, shift, outs)
-                    if shift:
-                        edges.append((col, x, -shift))
+        edges, unit = [], 0
+        for x, col, start, form in calls:
+            if form is None:
+                add_pairs(
+                    kind, motion_ref, pressure_ref, shifted, x, [(col, col - x)], limit, first, last, kept_ref, unit, start
+                )
+                unit += len(shifts)
+                continue
+            parts, reaction, packed = mutual_refs
+            both_ways(
+                kind, motion_ref, pressure_ref, shifted, x, col, form, out_ref, parts, reaction, limit, kept_ref, unit
+            )
+            take_reaction(out_ref, reaction, col, shifts[form], outs)
+            unit += 1
+            if shifts[form]:
+                edges.append((col, x, -shifts[form]))
         if edges:
             edge_pairs(kind, motion_ref, pressure_ref, shifted, shifts, edges, out_ref, packed, limit)
 
+    sums_shape = jax.ShapeDtypeStruct((columns, outs, limit, width), jnp.float32)
     return pl.pallas_call(
         kernel,
-        out_shape=jax.ShapeDtypeStruct((columns, outs, limit, width), jnp.float32),
+        out_shape=(sums_shape, kept_shape) if keep else (sums_shape,),
         in_specs=[VMEM] * len(inputs),
-        out_specs=VMEM,
+        out_specs=(VMEM, VMEM) if keep else (VMEM,),
         scratch_shapes=[pltpu.VMEM((columns, len(shifts), width // LANES, rows, slots, LANES), jnp.float32)]
         + (
             [
@@ -334,7 +354,7 @@
     return [ref[x, f, span, lanes] * s if s != 1.0 else ref[x, f, span, lanes] for ref, f, s in rows]
 
 
-def both_ways(kind, motion_ref, pressure_ref, shifted, x, col, form, sums, parts, reaction, limit):
+def both_ways(kind, motion_ref, pressure_ref, shifted, x, col, form, sums, parts, reaction, limit, kept_ref, unit):
     outs = kind[4]
     blocks, rows = shifted.shape[2], shifted.shape[3]
     both = both_force if outs == 3 else both_density
@@ -358,7 +378,9 @@
                     their = [jnp.broadcast_to(shifted[col, form, b, r, pl.ds(slot, 1), :], (ROWS, LANES)) for r in range(rows)]
                     back = None
                     for v in range(group):
-                        totals[v], given = both(mine[v], their, totals[v])
+                        place = (unit, b, slot, part * group + v)
+                        remain = kept(kept_ref, place, mine[v], their, outs == 1)
+                        totals[v], given = both(mine[v], their, totals[v], remain)
                         back = given if back is None else tuple(p + q for p, q in zip(back, given))
                     for k in range(outs):
                         parts[k, slot] = back[k] if part == 0 else parts[k, slot] + back[k]
@@ -426,7 +448,7 @@
                 slot = outer * unroll + inner
                 their = [jnp.broadcast_to(packed[r, pl.ds(slot, 1), :], (ROWS, LANES)) for r in range(rows)]
                 for v in range(group):
-                    totals[v] = pair(mine[v], their, totals[v])
+                    totals[v] = pair(mine[v], their, totals[v], closeness(displacement(mine[v], their)))
             return tuple(totals)
 
         zero = jnp.zeros((ROWS, LANES), jnp.float32)
@@ -440,7 +462,7 @@
                     sums[x, k, span, lanes] = sums[x, k, span, lanes] + jnp.where(lane == at, back, 0.0)
 
 
-def halo_sums(kind, refs, columns, slots, limit, first, last, motion_ref, pressure_ref, shifted, sizes_m, sizes_p):
+def halo_sums(kind, refs, columns, slots, limit, first, last, motion_ref, pressure_ref, shifted, sizes_m, sizes_p, kept_ref):
     spans_m, spans_p = bounds_of(sizes_m), bounds_of(sizes_p)
     for side in range(2):
         m_refs, p_refs = refs[side]
@@ -472,22 +494,27 @@
 
         fill_column(shifted, side, kind, motion_pieces, pressure_pieces, lambda f: f * columns + column, SHIFTS)
         x, shift = (0, -1) if side == 0 else (columns - 1, 1)
-        add_pairs(kind, motion_ref, pressure_ref, shifted, x, [(side, shift)], limit, first, last)
-
-
-def density_rest(motion, partial, messages, sizes, density, entropy, counts, level, limit, slots_sent):
+        add_pairs(
+            kind, motion_ref, pressure_ref, shifted, x, [(side, shift)], limit, first, last, kept_ref, side * len(SHIFTS)
+        )
+
+
+def density_rest(motion, partial, messages, sizes, density, entropy, counts, level, limit, slots_sent, keep):
     columns, _, slots, width = motion.shape
     (m_left, m_right) = messages
     first = density is None
     inputs = [motion, partial, entropy, counts] + ([] if first else [density]) + m_left + m_right
     n_in, n_m = len(inputs), len(m_left)
     rows = 4
+    kept_shape = jax.ShapeDtypeStruct((2 * len(SHIFTS), width // LANES, slots, limit // ROWS, ROWS, LANES), jnp.float32)
 
     def kernel(*refs):
         motion_ref, partial_ref, entropy_ref, counts_ref = refs[:4]
         old_ref = None if first else refs[4]
         m_refs = refs[n_in - 2 * n_m : n_in]
-        press_ref, left_ref, right_ref, shifted, sums = refs[n_in:]
+        press_ref, left_ref, right_ref, *left = refs[n_in:]
+        kept_ref = left[0] if keep else None
+        shifted, sums = left[-2:]
         sums[...] = partial_ref[...]
 
         def start(x, span, lanes):
@@ -497,7 +524,7 @@
             sums[x, 0, span, lanes] = total[0]
 
         sides = ((m_refs[:n_m], []), (m_refs[n_m:], []))
-        halo_sums(DENSITY, sides, columns, slots, limit, start, end, motion_ref, None, shifted, sizes, [])
+        halo_sums(DENSITY, sides, columns, slots, limit, start, end, motion_ref, None, shifted, sizes, [], kept_ref)
         for x in range(columns):
             count = counts_ref[level, x : x + 1, :]
             for lo in range(0, slots, ROWS):
@@ -522,9 +549,14 @@
     ends = jax.ShapeDtypeStruct((slots_sent, LANES), jnp.float32)
     return pl.pallas_call(
         kernel,
-        out_shape=(jax.ShapeDtypeStruct((columns, PRESSURE, slots, width), jnp.float32), ends, ends),
+        out_shape=(
+            jax.ShapeDtypeStruct((columns, PRESSURE, slots, width), jnp.float32),
+            ends,
+            ends,
+        )
+        + ((kept_shape,) if keep else ()),
         in_specs=[VMEM] * n_in,
-        out_specs=(VMEM,) * 3,
+        out_specs=(VMEM,) * (4 if keep else 3),
         scratch_shapes=[
             pltpu.VMEM((2, 3, width // LANES, rows, slots, LANES), jnp.float32),
             pltpu.VMEM((columns, 1, limit, width), jnp.float32),
@@ -534,10 +566,11 @@
     )(*inputs)
 
 
-def force_rest(motion, pressure, partial, messages_m, messages_p, sizes_m, sizes_p, counts, level, limit, slots_sent):
+def force_rest(motion, pressure, partial, messages_m, messages_p, sizes_m, sizes_p, counts, level, limit, slots_sent, closeness_kept):
     columns, _, slots, width = motion.shape
     n_m, n_p = len(messages_m[0]), len(messages_p[0])
     inputs = [motion, pressure, partial, counts] + messages_m[0] + messages_p[0] + messages_m[1] + messages_p[1]
+    inputs += [] if closeness_kept is None else [closeness_kept]
     n_in = len(inputs)
     rows = 10
     ends = jax.ShapeDtypeStruct((slots_sent, LANES), jnp.float32)
@@ -561,7 +594,8 @@
                 sums[x, k, span, lanes] = total[k]
 
         halo_sums(
-            FORCE, sides, columns, slots, limit, start, end, motion_ref, pressure_ref, shifted, sizes_m, sizes_p
+            FORCE, sides, columns, slots, limit, start, end, motion_ref, pressure_ref, shifted, sizes_m, sizes_p,
+            None if closeness_kept is None else refs[n_in - 1],
         )
         for x in range(columns):
             count = counts_ref[level, x : x + 1, :]
@@ -768,7 +802,7 @@
         limit = limits[level]
         sent = limits[max(level - 1, 0)]
         ends_m.insert(0, swap_ends(*made))
-        partial = own_part(DENSITY, motion, None, ends_m, [], limit, (0,))
+        partial, *inner_kept = own_part(DENSITY, motion, None, ends_m, [], limit, (0,), keep=KEEP[level][0])
         ends_m[0], partial = lax.optimization_barrier((ends_m[0], partial))
         plane = beside(ends_m[0], width)
         masses = (lambda c: [motion[c, 6]]) if level == 0 else (lambda c: [])
@@ -776,20 +810,21 @@
         sizes_m.insert(0, sent)
         left_m.insert(0, cells[0])
         right_m.insert(0, cells[1])
-        partial = own_part(DENSITY, motion, None, ends_m, [], limit, (-1, 1), partial)
-        pressure, *made = density_rest(motion, partial, (left_m, right_m), sizes_m, pressure, entropy, active_counts, level, limit, limit)
+        partial, *outer_kept = own_part(DENSITY, motion, None, ends_m, [], limit, (-1, 1), partial, keep=KEEP[level][1])
+        pressure, *made = density_rest(motion, partial, (left_m, right_m), sizes_m, pressure, entropy, active_counts, level, limit, limit, KEEP[level][2])
+        rest_kept = made.pop() if KEEP[level][2] else None
         ends_p.insert(0, swap_ends(*made))
-        partial = own_part(FORCE, motion, pressure, ends_m, ends_p, limit, (0,))
+        (partial,) = own_part(FORCE, motion, pressure, ends_m, ends_p, limit, (0,), None, *inner_kept)
         ends_p[0], partial = lax.optimization_barrier((ends_p[0], partial))
         plane = beside(ends_p[0], width)
         cells = swap_columns(lambda c: [rows_of(pressure[c, :, :limit]), plane, rows_of(motion[c, 3:6, :sent])])
         sizes_p.insert(0, limit)
         left_p.insert(0, cells[0])
         right_p.insert(0, cells[1])
-        partial = own_part(FORCE, motion, pressure, ends_m, ends_p, limit, (-1, 1), partial)
+        (partial,) = own_part(FORCE, motion, pressure, ends_m, ends_p, limit, (-1, 1), partial, *outer_kept)
         more = limit if level < levels - 1 else 0
         motion, *made = force_rest(
-            motion, pressure, partial, (left_m, right_m), (left_p, right_p), sizes_m, sizes_p, active_counts, level, limit, more
+            motion, pressure, partial, (left_m, right_m), (left_p, right_p), sizes_m, sizes_p, active_counts, level, limit, more, rest_kept
         )
     capacity = 3 * slots * columns * width // 8
     here = lax.axis_index("sub").astype(jnp.int32).reshape(1)

time: 145 us -> 143 us (0.986)
  Pallas kernels: 86.4 us -> 83.2 us
    pallas_call x12, Pallas kernels: 48.2 us -> 46.3 us  [own_part(): pl.pallas_call(kernel, out_shape=(sums_shape, kept_shape) if keep else (s...]
    pallas_call x3, Pallas kernels: 21.2 us -> 19.7 us  [force_rest(): pl.pallas_call(kernel, out_shape=outs, in_specs=[VMEM] * n_in, out_specs=...]
  transfers between devices with their start and end apart: 27 -> 27, of which waited for: 9 -> 8; matrix products, arithmetic and copies ran while one was open for 0% -> 0% of each run, Pallas kernels for 34% -> 33%
where the time goes in v5:
time: 143 us; the launch traced here: 142 us
  Pallas kernels  83.2 us (58%)
  starting transfers between devices  43.1 us (30%)
  waiting for transfers between devices  11.4 us (8%)
  local copies, waits for them, and re-layouts  2.8 us (2%)
    pallas_call x12, Pallas kernels, own_part(): pl.pallas_call(kernel, out_shape=(sums_shape, kept_shape) if keep else (s...  46.3 us
    ppermute x27, starting transfers between devices, pass_on(): lax.ppermute(value, axis, [(i, (i + step) % count) for i in range(count)])  43.1 us
    pallas_call x3, Pallas kernels, force_rest(): pl.pallas_call(kernel, out_shape=outs, in_specs=[VMEM] * n_in, out_specs=...  19.7 us
    ppermute x27, waiting for transfers between devices, pass_on(): lax.ppermute(value, axis, [(i, (i + step) % count) for i in range(count)])  11.4 us
    pallas_call x3, Pallas kernels, density_rest(): pl.pallas_call(kernel, out_shape=(jax.ShapeDtypeStruct((columns, PRESSURE...  10.1 us
    pallas_call x1, Pallas kernels, compact(): pl.pallas_call(kernel, out_shape=(jax.ShapeDtypeStruct((8, capacity), jnp...  4.64 us
  transfers between devices with their start and end apart: 27, of which 8 were waited for; matrix products, arithmetic and copies ran while one was open for 0% of the time, Pallas kernels for 33%

profile of v5, /device:TPU:0, one launch (start us, length us, event | category | flops | bytes accessed | tf_op | source)
XLA Modules:
  0.0 142.0 jit_solution(4843205721281470869)
XLA Ops:
  4.2 2.0 %collective-permute-start.1 = (f32[32,128]{1,0:T(8,128)S(1)}, f32[32,128]{1,0:T(8,128)S(1)}, u32[]{:S(2)}, u32[]{:S(2)}) collective-permute-start(f32[32,128]{1,0:T(8,128)S(1)} %get-tuple-element.57), channel_id=1, source_target_pairs={{0,3},{1,0},{2,1},{3,2},{4,7},{5,4},{6,5},{7,6},{8,11},{9,8},{10,9... | collective-permute-start | bytes 49160 | tf_op jit(solution)/shard_map/ppermute | solution.py:765
  6.2 2.5 %shard_map.65 = (f32[2,1,32,256]{3,2,1,0:T(8,128)S(1)}, f32[3,2,32,4,8,128]{5,4,3,2,1,0:T(8,128)S(1)}) custom-call(f32[2,7,32,256]{3,2,1,0:T(8,128)S(1)} %maximum_bitcast_fusion.motion_ref.own_refs_0_.refs_0_), custom_call_target="tpu_custom_call" | custom-call | flops 471859200 | bytes 1048576 | tf_op jit(solution)/shard_map/pallas_call | solution.py:319
  8.8 2.3 %collective-permute-start.2 = (f32[160,256]{1,0:T(8,128)S(1)}, f32[160,256]{1,0:T(8,128)S(1)}, u32[]{:S(2)}, u32[]{:S(2)}) collective-permute-start(f32[160,256]{1,0:T(8,128)S(1)} %get-tuple-element.132), channel_id=1, source_target_pairs={{0,4},{4,8},{8,12},{12,16},{16,20},{20,24},{24,28},{28,0},{1,5},{5... | collective-permute-start | bytes 491528 | tf_op jit(solution)/shard_map/ppermute | solution.py:765
  11.2 3.1 %collective-permute-start.3 = (f32[160,256]{1,0:T(8,128)S(1)}, f32[160,256]{1,0:T(8,128)S(1)}, u32[]{:S(2)}, u32[]{:S(2)}) collective-permute-start(f32[160,256]{1,0:T(8,128)S(1)} %get-tuple-element.131), channel_id=1, source_target_pairs={{0,28},{4,0},{8,4},{12,8},{16,12},{20,16},{24,20},{28,24},{1,29},{... | collective-permute-start | bytes 491528 | tf_op jit(solution)/shard_map/ppermute | solution.py:765
  14.3 4.7 %shard_map.66 = (f32[2,1,32,256]{3,2,1,0:T(8,128)S(1)}, f32[4,2,32,4,8,128]{5,4,3,2,1,0:T(8,128)S(1)}) custom-call(f32[2,7,32,256]{3,2,1,0:T(8,128)S(1)} %maximum_bitcast_fusion.motion_ref.own_refs_0_.refs_0_, f32[32,128]{1,0:T(8,128)S(1)} %collective-permute-done.own_refs_1_.own_refs_2_.own_refs_3_.own_refs_4_.own_refs_5_.own_refs_6_, ...), custom_call_target="tpu_custom_call" | custom-call | flops 943718400 | bytes 1048576 | tf_op jit(solution)/shard_map/pallas_call | solution.py:319
  20.9 5.4 %shard_map.67 = (f32[2,3,32,256]{3,2,1,0:T(8,128)S(1)}, f32[32,128]{1,0:T(8,128)S(1)}, f32[32,128]{1,0:T(8,128)S(1)}, f32[6,2,32,4,8,128]{5,4,3,2,1,0:T(8,128)S(1)}) custom-call(f32[2,7,32,256]{3,2,1,0:T(8,128)S(1)} %maximum_bitcast_fusion.motion_ref.own_refs_0_.refs_0_, f32[2,1,32,256]{3,2,1,0:T(8,128)S(1)} %get-tuple-element.62.refs_1_, ...), custom_call_target="tpu_custom_call" | custom-call | flops 707788800 | bytes 1048576 | tf_op jit(solution)/shard_map/pallas_call | solution.py:550
  28.2 5.1 %shard_map.68.own_refs_6_ = f32[2,3,32,256]{3,2,1,0:T(8,128)S(1)} custom-call(f32[2,7,32,256]{3,2,1,0:T(8,128)S(1)} %maximum_bitcast_fusion.motion_ref.own_refs_0_.refs_0_, f32[2,3,32,256]{3,2,1,0:T(8,128)S(1)} %get-tuple-element.63.own_refs_1_.refs_1_.refs_4_, f32[3,2,32,4,8,128]{5,4,3,2,1,0:T(8,128)S(1)} %get-tuple-element.66.own_refs_2_), custom_call_target="tpu_custom_call" | custom-call | flops 943718400 | bytes 1048576 | tf_op jit(solution)/shard_map/pallas_call | solution.py:319
  33.7 4.4 %collective-permute-start.7 = (f32[224,256]{1,0:T(8,128)S(1)}, f32[224,256]{1,0:T(8,128)S(1)}, u32[]{:S(2)}, u32[]{:S(2)}) collective-permute-start(f32[224,256]{1,0:T(8,128)S(1)} %get-tuple-element.129), channel_id=1, source_target_pairs={{0,28},{4,0},{8,4},{12,8},{16,12},{20,16},{24,20},{28,24},{1,29},{... | collective-permute-start | bytes 688136 | tf_op jit(solution)/shard_map/ppermute | solution.py:765
  38.1 9.9 %shard_map.69.refs_2_ = f32[2,3,32,256]{3,2,1,0:T(8,128)S(1)} custom-call(f32[2,7,32,256]{3,2,1,0:T(8,128)S(1)} %maximum_bitcast_fusion.motion_ref.own_refs_0_.refs_0_, f32[2,3,32,256]{3,2,1,0:T(8,128)S(1)} %get-tuple-element.63.own_refs_1_.refs_1_.refs_4_, ...), custom_call_target="tpu_custom_call" | custom-call | flops 1887436800 | bytes 1048576 | tf_op jit(solution)/shard_map/pallas_call | solution.py:319
  48.1 10.4 %shard_map.70 = (f32[2,7,32,256]{3,2,1,0:T(8,128)S(1)}, f32[32,128]{1,0:T(8,128)S(1)}, f32[32,128]{1,0:T(8,128)S(1)}) custom-call(f32[2,7,32,256]{3,2,1,0:T(8,128)S(1)} %maximum_bitcast_fusion.motion_ref.own_refs_0_.refs_0_, f32[2,3,32,256]{3,2,1,0:T(8,128)S(1)} %get-tuple-element.63.own_refs_1_.refs_1_.refs_4_, f32[2,3,32,256]{3,2,1,0:T(8,128)S(1)} %shard_map.69.refs_2_, ...), custom_call_target="tpu_custom_call" | custom-call | flops 1415577600 | bytes 1048576 | tf_op jit(solution)/shard_map/pallas_call | solution.py:618
  61.9 4.7 %collective-permute-start.11 = (f32[128,256]{1,0:T(8,128)S(1)}, f32[128,256]{1,0:T(8,128)S(1)}, u32[]{:S(2)}, u32[]{:S(2)}) collective-permute-start(f32[128,256]{1,0:T(8,128)S(1)} %get-tuple-element.127), channel_id=1, source_target_pairs={{0,28},{4,0},{8,4},{12,8},{16,12},{20,16},{24,20},{28,24},{1,29},{... | collective-permute-start | bytes 393224 | tf_op jit(solution)/shard_map/ppermute | solution.py:765
  66.6 3.5 %shard_map.72 = (f32[2,1,16,256]{3,2,1,0:T(8,128)S(1)}, f32[12,2,32,2,8,128]{5,4,3,2,1,0:T(8,128)S(1)}) custom-call(f32[2,7,32,256]{3,2,1,0:T(8,128)S(1)} %get-tuple-element.72.own_refs_0_.refs_0_, f32[32,128]{1,0:T(8,128)S(1)} %collective-permute-done.8.own_refs_1_.own_refs_2_.own_refs_3_.own_refs_4_, ...), custom_call_target="tpu_custom_call" | custom-call | flops 471859200 | bytes 1048576 | tf_op jit(solution)/shard_map/pallas_call | solution.py:319
  70.7 3.0 %shard_map.73 = (f32[2,3,32,256]{3,2,1,0:T(8,128)S(1)}, f32[16,128]{1,0:T(8,128)S(1)}, f32[16,128]{1,0:T(8,128)S(1)}, f32[6,2,32,2,8,128]{5,4,3,2,1,0:T(8,128)S(1)}) custom-call(f32[2,7,32,256]{3,2,1,0:T(8,128)S(1)} %get-tuple-element.72.own_refs_0_.refs_0_, f32[2,1,16,256]{3,2,1,0:T(8,128)S(1)} %get-tuple-element.79.refs_1_, f32[2,32,256]{2,1,0:T(8,128)S(1)} %bitcast.36, ...), custom_call_target="tpu_custom_call" | custom-call | flops 353894400 | bytes 1048576 | tf_op jit(solution)/shard_map/pallas_call | solution.py:550
  75.4 3.0 %shard_map.74.own_refs_10_ = f32[2,3,16,256]{3,2,1,0:T(8,128)S(1)} custom-call(f32[2,7,32,256]{3,2,1,0:T(8,128)S(1)} %get-tuple-element.72.own_refs_0_.refs_0_, f32[2,3,32,256]{3,2,1,0:T(8,128)S(1)} %get-tuple-element.80.own_refs_1_.refs_1_.refs_4_, f32[5,2,32,2,8,128]{5,4,3,2,1,0:T(8,128)S(1)} %get-tuple-element.83.own_refs_2_), custom_call_target="tpu_custom_call" | custom-call | flops 471859200 | bytes 1048576 | tf_op jit(solution)/shard_map/pallas_call | solution.py:319
  78.8 4.5 %collective-permute-start.15 = (f32[160,256]{1,0:T(8,128)S(1)}, f32[160,256]{1,0:T(8,128)S(1)}, u32[]{:S(2)}, u32[]{:S(2)}) collective-permute-start(f32[160,256]{1,0:T(8,128)S(1)} %get-tuple-element.135), channel_id=1, source_target_pairs={{0,28},{4,0},{8,4},{12,8},{16,12},{20,16},{24,20},{28,24},{1,29},{... | collective-permute-start | bytes 491528 | tf_op jit(solution)/shard_map/ppermute | solution.py:765
  83.3 6.7 %shard_map.75.refs_2_ = f32[2,3,16,256]{3,2,1,0:T(8,128)S(1)} custom-call(f32[2,7,32,256]{3,2,1,0:T(8,128)S(1)} %get-tuple-element.72.own_refs_0_.refs_0_, f32[2,3,32,256]{3,2,1,0:T(8,128)S(1)} %get-tuple-element.80.own_refs_1_.refs_1_.refs_4_, f32[32,128]{1,0:T(8,128)S(1)} %collective-permute-done.8.own_refs_1_.own_refs_2_.own_refs_3_.own_refs_4_, ...), custom_call_target="tpu_custom_call" | custom-call | flops 943718400 | bytes 1048576 | tf_op jit(solution)/shard_map/pallas_call | solution.py:319
  90.0 5.6 %shard_map.76 = (f32[2,7,32,256]{3,2,1,0:T(8,128)S(1)}, f32[16,128]{1,0:T(8,128)S(1)}, f32[16,128]{1,0:T(8,128)S(1)}) custom-call(f32[2,7,32,256]{3,2,1,0:T(8,128)S(1)} %get-tuple-element.72.own_refs_0_.refs_0_, f32[2,3,32,256]{3,2,1,0:T(8,128)S(1)} %get-tuple-element.80.own_refs_1_.refs_1_.refs_4_, f32[2,3,16,256]{3,2,1,0:T(8,128)S(1)} %shard_map.75.refs_2_, ...), custom_call_target="tpu_custom_call" | custom-call | flops 707788800 | bytes 1048576 | tf_op jit(solution)/shard_map/pallas_call | solution.py:618
  98.9 4.7 %collective-permute-start.19 = (f32[64,256]{1,0:T(8,128)S(1)}, f32[64,256]{1,0:T(8,128)S(1)}, u32[]{:S(2)}, u32[]{:S(2)}) collective-permute-start(f32[64,256]{1,0:T(8,128)S(1)} %get-tuple-element.133), channel_id=1, source_target_pairs={{0,28},{4,0},{8,4},{12,8},{16,12},{20,16},{24,20},{28,24},{1,29},{... | collective-permute-start | bytes 196616 | tf_op jit(solution)/shard_map/ppermute | solution.py:765
  110.0 2.0 %shard_map.80.own_refs_14_ = f32[2,3,8,256]{3,2,1,0:T(8,128)S(1)} custom-call(f32[2,7,32,256]{3,2,1,0:T(8,128)S(1)} %get-tuple-element.89.own_refs_0_.refs_0_, f32[2,3,32,256]{3,2,1,0:T(8,128)S(1)} %get-tuple-element.95.own_refs_1_.refs_1_.pressure_ref), custom_call_target="tpu_custom_call" | custom-call | flops 235929600 | bytes 1048576 | tf_op jit(solution)/shard_map/pallas_call | solution.py:319
  112.1 4.7 %collective-permute-start.23 = (f32[80,256]{1,0:T(8,128)S(1)}, f32[80,256]{1,0:T(8,128)S(1)}, u32[]{:S(2)}, u32[]{:S(2)}) collective-permute-start(f32[80,256]{1,0:T(8,128)S(1)} %get-tuple-element.137), channel_id=1, source_target_pairs={{0,28},{4,0},{8,4},{12,8},{16,12},{20,16},{24,20},{28,24},{1,29},{... | collective-permute-start | bytes 245768 | tf_op jit(solution)/shard_map/ppermute | solution.py:765
  117.7 4.6 %shard_map.81.refs_2_ = f32[2,3,8,256]{3,2,1,0:T(8,128)S(1)} custom-call(f32[2,7,32,256]{3,2,1,0:T(8,128)S(1)} %get-tuple-element.89.own_refs_0_.refs_0_, f32[2,3,32,256]{3,2,1,0:T(8,128)S(1)} %get-tuple-element.95.own_refs_1_.refs_1_.pressure_ref, f32[16,128]{1,0:T(8,128)S(1)} %collective-permute-done.16.own_refs_1_.own_refs_2_, ...), custom_call_target="tpu_custom_call" | custom-call | flops 471859200 | bytes 1048576 | tf_op jit(solution)/shard_map/pallas_call | solution.py:319
  122.3 3.7 %shard_map.82.motion_ref = f32[2,7,32,256]{3,2,1,0:T(8,128)S(1)} custom-call(f32[2,7,32,256]{3,2,1,0:T(8,128)S(1)} %get-tuple-element.89.own_refs_0_.refs_0_, f32[2,3,32,256]{3,2,1,0:T(8,128)S(1)} %get-tuple-element.95.own_refs_1_.refs_1_.pressure_ref, f32[2,3,8,256]{3,2,1,0:T(8,128)S(1)} %shard_map.81.refs_2_, s32[3,2,256]{2,1,0:T(2,128)S(1)} %copy-done, ...), custom_call_target="tpu_custom_call" | custom-call | flops 353894400 | bytes 1048576 | tf_op jit(solution)/shard_map/pallas_call | solution.py:618
  126.0 4.6 %shard_map.84 = (f32[8,6144]{1,0:T(8,128)S(1)}, f32[8,6144]{1,0:T(8,128)S(1)}, f32[8,6144]{1,0:T(8,128)S(1)}, f32[8,6144]{1,0:T(8,128)S(1)}) custom-call(f32[2,7,32,256]{3,2,1,0:T(8,128)S(1)} %shard_map.82.motion_ref, f32[2,3,32,256]{3,2,1,0:T(8,128)S(1)} %get-tuple-element.95.own_refs_1_.refs_1_.pressure_ref, s32[64,256]{1,0:T(8,128)S(1)} %get-tuple-element.101.place_ref, ...), custom_call_target="tpu_custom_call" | custom-call | tf_op jit(solution)/shard_map/pallas_call | solution.py:725
  133.0 4.3 %collective-permute-done.24.refs_1_ = f32[8,6144]{1,0:T(8,128)S(1)} collective-permute-done((f32[8,6144]{1,0:T(8,128)S(1)}, f32[8,6144]{1,0:T(8,128)S(1)}, u32[]{:S(2)}, u32[]{:S(2)}) %collective-permute-start.24) | collective-permute-done | bytes 196640 | tf_op jit(solution)/shard_map/ppermute | solution.py:765
  (90 shorter events, 32.0 us)
Async XLA Ops:
  3.7 5.1 %collective-permute-start = (f32[32,128]{1,0:T(8,128)S(1)}, f32[32,128]{1,0:T(8,128)S(1)}, u32[]{:S(2)}, u32[]{:S(2)}) collective-permute-start(f32[32,128]{1,0:T(8,128)S(1)} %get-tuple-element.56), channel_id=1, source_target_pairs={{0,1},{1,2},{2,3},{3,0},{4,5},{5,6},{6,7},{7,4},{8,9},{9,10},{10,1... | collective-permute-start | bytes 49160 | tf_op jit(solution)/shard_map/ppermute | solution.py:765
  4.2 4.6 %collective-permute-start.1 = (f32[32,128]{1,0:T(8,128)S(1)}, f32[32,128]{1,0:T(8,128)S(1)}, u32[]{:S(2)}, u32[]{:S(2)}) collective-permute-start(f32[32,128]{1,0:T(8,128)S(1)} %get-tuple-element.57), channel_id=1, source_target_pairs={{0,3},{1,0},{2,1},{3,2},{4,7},{5,4},{6,5},{7,6},{8,11},{9,8},{10,9... | collective-permute-start | bytes 49160 | tf_op jit(solution)/shard_map/ppermute | solution.py:765
  8.8 10.2 %collective-permute-start.2 = (f32[160,256]{1,0:T(8,128)S(1)}, f32[160,256]{1,0:T(8,128)S(1)}, u32[]{:S(2)}, u32[]{:S(2)}) collective-permute-start(f32[160,256]{1,0:T(8,128)S(1)} %get-tuple-element.132), channel_id=1, source_target_pairs={{0,4},{4,8},{8,12},{12,16},{16,20},{20,24},{24,28},{28,0},{1,5},{5... | collective-permute-start | bytes 491528 | tf_op jit(solution)/shard_map/ppermute | solution.py:765
  11.2 9.8 %collective-permute-start.3 = (f32[160,256]{1,0:T(8,128)S(1)}, f32[160,256]{1,0:T(8,128)S(1)}, u32[]{:S(2)}, u32[]{:S(2)}) collective-permute-start(f32[160,256]{1,0:T(8,128)S(1)} %get-tuple-element.131), channel_id=1, source_target_pairs={{0,28},{4,0},{8,4},{12,8},{16,12},{20,16},{24,20},{28,24},{1,29},{... | collective-permute-start | bytes 491528 | tf_op jit(solution)/shard_map/ppermute | solution.py:765
  26.4 6.9 %collective-permute-start.4 = (f32[32,128]{1,0:T(8,128)S(1)}, f32[32,128]{1,0:T(8,128)S(1)}, u32[]{:S(2)}, u32[]{:S(2)}) collective-permute-start(f32[32,128]{1,0:T(8,128)S(1)} %get-tuple-element.64), channel_id=1, source_target_pairs={{0,1},{1,2},{2,3},{3,0},{4,5},{5,6},{6,7},{7,4},{8,9},{9,10},{10,1... | collective-permute-start | bytes 49160 | tf_op jit(solution)/shard_map/ppermute | solution.py:765
  26.4 6.9 %collective-permute-start.5 = (f32[32,128]{1,0:T(8,128)S(1)}, f32[32,128]{1,0:T(8,128)S(1)}, u32[]{:S(2)}, u32[]{:S(2)}) collective-permute-start(f32[32,128]{1,0:T(8,128)S(1)} %get-tuple-element.65), channel_id=1, source_target_pairs={{0,3},{1,0},{2,1},{3,2},{4,7},{5,4},{6,5},{7,6},{8,11},{9,8},{10,9... | collective-permute-start | bytes 49160 | tf_op jit(solution)/shard_map/ppermute | solution.py:765
  33.4 14.7 %collective-permute-start.6 = (f32[224,256]{1,0:T(8,128)S(1)}, f32[224,256]{1,0:T(8,128)S(1)}, u32[]{:S(2)}, u32[]{:S(2)}) collective-permute-start(f32[224,256]{1,0:T(8,128)S(1)} %get-tuple-element.130), channel_id=1, source_target_pairs={{0,4},{4,8},{8,12},{12,16},{16,20},{20,24},{24,28},{28,0},{1,5},{5... | collective-permute-start | bytes 688136 | tf_op jit(solution)/shard_map/ppermute | solution.py:765
  33.7 14.4 %collective-permute-start.7 = (f32[224,256]{1,0:T(8,128)S(1)}, f32[224,256]{1,0:T(8,128)S(1)}, u32[]{:S(2)}, u32[]{:S(2)}) collective-permute-start(f32[224,256]{1,0:T(8,128)S(1)} %get-tuple-element.129), channel_id=1, source_target_pairs={{0,28},{4,0},{8,4},{12,8},{16,12},{20,16},{24,20},{28,24},{1,29},{... | collective-permute-start | bytes 688136 | tf_op jit(solution)/shard_map/ppermute | solution.py:765
  58.5 3.3 %collective-permute-start.8 = (f32[32,128]{1,0:T(8,128)S(1)}, f32[32,128]{1,0:T(8,128)S(1)}, u32[]{:S(2)}, u32[]{:S(2)}) collective-permute-start(f32[32,128]{1,0:T(8,128)S(1)} %get-tuple-element.73), channel_id=1, source_target_pairs={{0,1},{1,2},{2,3},{3,0},{4,5},{5,6},{6,7},{7,4},{8,9},{9,10},{10,1... | collective-permute-start | bytes 49160 | tf_op jit(solution)/shard_map/ppermute | solution.py:765
  61.8 8.8 %collective-permute-start.10 = (f32[128,256]{1,0:T(8,128)S(1)}, f32[128,256]{1,0:T(8,128)S(1)}, u32[]{:S(2)}, u32[]{:S(2)}) collective-permute-start(f32[128,256]{1,0:T(8,128)S(1)} %get-tuple-element.128), channel_id=1, source_target_pairs={{0,4},{4,8},{8,12},{12,16},{16,20},{20,24},{24,28},{28,0},{1,5},{5... | collective-permute-start | bytes 393224 | tf_op jit(solution)/shard_map/ppermute | solution.py:765
  61.9 8.8 %collective-permute-start.11 = (f32[128,256]{1,0:T(8,128)S(1)}, f32[128,256]{1,0:T(8,128)S(1)}, u32[]{:S(2)}, u32[]{:S(2)}) collective-permute-start(f32[128,256]{1,0:T(8,128)S(1)} %get-tuple-element.127), channel_id=1, source_target_pairs={{0,28},{4,0},{8,4},{12,8},{16,12},{20,16},{24,20},{28,24},{1,29},{... | collective-permute-start | bytes 393224 | tf_op jit(solution)/shard_map/ppermute | solution.py:765
  73.6 4.8 %collective-permute-start.12 = (f32[16,128]{1,0:T(8,128)S(1)}, f32[16,128]{1,0:T(8,128)S(1)}, u32[]{:S(2)}, u32[]{:S(2)}) collective-permute-start(f32[16,128]{1,0:T(8,128)S(1)} %get-tuple-element.81), channel_id=1, source_target_pairs={{0,1},{1,2},{2,3},{3,0},{4,5},{5,6},{6,7},{7,4},{8,9},{9,10},{10,1... | collective-permute-start | bytes 24584 | tf_op jit(solution)/shard_map/ppermute | solution.py:765
  73.7 4.7 %collective-permute-start.13 = (f32[16,128]{1,0:T(8,128)S(1)}, f32[16,128]{1,0:T(8,128)S(1)}, u32[]{:S(2)}, u32[]{:S(2)}) collective-permute-start(f32[16,128]{1,0:T(8,128)S(1)} %get-tuple-element.82), channel_id=1, source_target_pairs={{0,3},{1,0},{2,1},{3,2},{4,7},{5,4},{6,5},{7,6},{8,11},{9,8},{10,9... | collective-permute-start | bytes 24584 | tf_op jit(solution)/shard_map/ppermute | solution.py:765
  78.5 11.5 %collective-permute-start.14 = (f32[160,256]{1,0:T(8,128)S(1)}, f32[160,256]{1,0:T(8,128)S(1)}, u32[]{:S(2)}, u32[]{:S(2)}) collective-permute-start(f32[160,256]{1,0:T(8,128)S(1)} %get-tuple-element.136), channel_id=1, source_target_pairs={{0,4},{4,8},{8,12},{12,16},{16,20},{20,24},{24,28},{28,0},{1,5},{5... | collective-permute-start | bytes 491528 | tf_op jit(solution)/shard_map/ppermute | solution.py:765
  78.8 11.2 %collective-permute-start.15 = (f32[160,256]{1,0:T(8,128)S(1)}, f32[160,256]{1,0:T(8,128)S(1)}, u32[]{:S(2)}, u32[]{:S(2)}) collective-permute-start(f32[160,256]{1,0:T(8,128)S(1)} %get-tuple-element.135), channel_id=1, source_target_pairs={{0,28},{4,0},{8,4},{12,8},{16,12},{20,16},{24,20},{28,24},{1,29},{... | collective-permute-start | bytes 491528 | tf_op jit(solution)/shard_map/ppermute | solution.py:765
  98.8 7.6 %collective-permute-start.18 = (f32[64,256]{1,0:T(8,128)S(1)}, f32[64,256]{1,0:T(8,128)S(1)}, u32[]{:S(2)}, u32[]{:S(2)}) collective-permute-start(f32[64,256]{1,0:T(8,128)S(1)} %get-tuple-element.134), channel_id=1, source_target_pairs={{0,4},{4,8},{8,12},{12,16},{16,20},{20,24},{24,28},{28,0},{1,5},{5... | collective-permute-start | bytes 196616 | tf_op jit(solution)/shard_map/ppermute | solution.py:765
  98.9 7.5 %collective-permute-start.19 = (f32[64,256]{1,0:T(8,128)S(1)}, f32[64,256]{1,0:T(8,128)S(1)}, u32[]{:S(2)}, u32[]{:S(2)}) collective-permute-start(f32[64,256]{1,0:T(8,128)S(1)} %get-tuple-element.133), channel_id=1, source_target_pairs={{0,28},{4,0},{8,4},{12,8},{16,12},{20,16},{24,20},{28,24},{1,29},{... | collective-permute-start | bytes 196616 | tf_op jit(solution)/shard_map/ppermute | solution.py:765
  108.1 3.8 %collective-permute-start.20 = (f32[8,128]{1,0:T(8,128)S(1)}, f32[8,128]{1,0:T(8,128)S(1)}, u32[]{:S(2)}, u32[]{:S(2)}) collective-permute-start(f32[8,128]{1,0:T(8,128)S(1)} %get-tuple-element.96), channel_id=1, source_target_pairs={{0,1},{1,2},{2,3},{3,0},{4,5},{5,6},{6,7},{7,4},{8,9},{9,10},{10,1... | collective-permute-start | bytes 12296 | tf_op jit(solution)/shard_map/ppermute | solution.py:765
  108.2 3.8 %collective-permute-start.21 = (f32[8,128]{1,0:T(8,128)S(1)}, f32[8,128]{1,0:T(8,128)S(1)}, u32[]{:S(2)}, u32[]{:S(2)}) collective-permute-start(f32[8,128]{1,0:T(8,128)S(1)} %get-tuple-element.97), channel_id=1, source_target_pairs={{0,3},{1,0},{2,1},{3,2},{4,7},{5,4},{6,5},{7,6},{8,11},{9,8},{10,9... | collective-permute-start | bytes 12296 | tf_op jit(solution)/shard_map/ppermute | solution.py:765
  112.0 10.3 %collective-permute-start.22 = (f32[80,256]{1,0:T(8,128)S(1)}, f32[80,256]{1,0:T(8,128)S(1)}, u32[]{:S(2)}, u32[]{:S(2)}) collective-permute-start(f32[80,256]{1,0:T(8,128)S(1)} %get-tuple-element.138), channel_id=1, source_target_pairs={{0,4},{4,8},{8,12},{12,16},{16,20},{20,24},{24,28},{28,0},{1,5},{5... | collective-permute-start | bytes 245768 | tf_op jit(solution)/shard_map/ppermute | solution.py:765
  112.1 10.2 %collective-permute-start.23 = (f32[80,256]{1,0:T(8,128)S(1)}, f32[80,256]{1,0:T(8,128)S(1)}, u32[]{:S(2)}, u32[]{:S(2)}) collective-permute-start(f32[80,256]{1,0:T(8,128)S(1)} %get-tuple-element.137), channel_id=1, source_target_pairs={{0,28},{4,0},{8,4},{12,8},{16,12},{20,16},{24,20},{28,24},{1,29},{... | collective-permute-start | bytes 245768 | tf_op jit(solution)/shard_map/ppermute | solution.py:765
  130.7 6.6 %collective-permute-start.24 = (f32[8,6144]{1,0:T(8,128)S(1)}, f32[8,6144]{1,0:T(8,128)S(1)}, u32[]{:S(2)}, u32[]{:S(2)}) collective-permute-start(f32[8,6144]{1,0:T(8,128)S(1)} %get-tuple-element.104), channel_id=1, source_target_pairs={{0,1},{1,2},{2,3},{3,0},{4,5},{5,6},{6,7},{7,4},{8,9},{9,10},{10,1... | collective-permute-start | bytes 589832 | tf_op jit(solution)/shard_map/ppermute | solution.py:765
  130.8 7.8 %collective-permute-start.25 = (f32[8,6144]{1,0:T(8,128)S(1)}, f32[8,6144]{1,0:T(8,128)S(1)}, u32[]{:S(2)}, u32[]{:S(2)}) collective-permute-start(f32[8,6144]{1,0:T(8,128)S(1)} %get-tuple-element.105), channel_id=1, source_target_pairs={{0,2},{1,3},{2,0},{3,1},{4,6},{5,7},{6,4},{7,5},{8,10},{9,11},{10,... | collective-permute-start | bytes 589832 | tf_op jit(solution)/shard_map/ppermute | solution.py:765
  131.7 8.9 %collective-permute-start.26 = (f32[8,6144]{1,0:T(8,128)S(1)}, f32[8,6144]{1,0:T(8,128)S(1)}, u32[]{:S(2)}, u32[]{:S(2)}) collective-permute-start(f32[8,6144]{1,0:T(8,128)S(1)} %get-tuple-element.106), channel_id=1, source_target_pairs={{0,3},{1,0},{2,1},{3,2},{4,7},{5,4},{6,5},{7,6},{8,11},{9,8},{10,9... | collective-permute-start | bytes 589832 | tf_op jit(solution)/shard_map/ppermute | solution.py:765
  (6 other events, 68.0 us)

commit v6 on v5

--- a/solution.py
+++ b/solution.py
@@ -34,43 +34,49 @@
     dx, dy, dz = delta
     squared = dx * dx + dy * dy + dz * dz
     radius = squared * lax.rsqrt(jnp.maximum(squared, 1e-30))
-    return jnp.maximum(1.0 - radius, 0.0)
+    return jnp.maximum(1.0 - radius, 0.0), squared
 
 
 def displacement(own, their):
     return tuple(i - j for i, j in zip(own[:3], their[:3]))
 
 
-def force_core(own, their, remain):
+def force_core(own, their, near):
+    remain, squared = near
+    if squared is None:
+        squared = (1.0 - remain) * (1.0 - remain)
     ui, vi, wi, qi, ci, ri = own[3:9]
     uj, vj, wj, qj, cj, rj = their[3:9]
     dx, dy, dz = displacement(own, their)
-    radius = 1.0 - remain
     approach = dx * (ui - uj) + dy * (vi - vj) + dz * (wi - wj)
-    closing = jnp.minimum(approach, 0.0) * pl.reciprocal(radius * radius + SOFTEN, approx=True)
+    closing = jnp.minimum(approach, 0.0) * pl.reciprocal(squared + SOFTEN, approx=True)
     viscous = closing * (closing - (ci + cj)) * pl.reciprocal(ri + rj, approx=True)
     return (dx, dy, dz), qi + qj + viscous
 
 
-def pair_force(own, their, total, remain):
-    delta, pressure = force_core(own, their, remain)
+def pair_force(own, their, total, near):
+    remain = near[0]
+    delta, pressure = force_core(own, their, near)
     strength = pressure * ((remain * remain) * (remain * their[-1]))
     return tuple(t + strength * d for t, d in zip(total, delta))
 
 
-def pair_density(own, their, total, remain):
+def pair_density(own, their, total, near):
+    remain = near[0]
     square = remain * remain
     return (total[0] + (square * square) * ((5.0 - 4.0 * remain) * their[-1]),)
 
 
-def both_force(own, their, total, remain):
-    delta, pressure = force_core(own, their, remain)
+def both_force(own, their, total, near):
+    remain = near[0]
+    delta, pressure = force_core(own, their, near)
     strength = pressure * ((remain * remain) * remain)
     on_own, on_their = strength * their[-1], strength * own[-1]
     return tuple(t + on_own * d for t, d in zip(total, delta)), tuple(on_their * d for d in delta)
 
 
-def both_density(own, their, total, remain):
+def both_density(own, their, total, near):
+    remain = near[0]
     square = remain * remain
     weight = (square * square) * (5.0 - 4.0 * remain)
     return (total[0] + weight * their[-1],), (weight * own[-1],)
@@ -78,11 +84,11 @@
 
 def kept(kept_ref, at, own, their, first):
     if kept_ref is not None and not first:
-        return kept_ref[at]
-    value = closeness(displacement(own, their))
+        return kept_ref[at], None
+    near = closeness(displacement(own, their))
     if kept_ref is not None:
-        kept_ref[at] = value
-    return value
+        kept_ref[at] = near[0]
+    return near
 
 
 DENSITY = ((0, 1.0), (1, 1.0), (2, 1.0)), (), ((6, KERNEL_NORM),), pair_density, 1
@@ -165,7 +171,7 @@
                             for r in range(rows)
                         ]
                         for v in range(group):
-                            place = (unit + at, b, slot, part * group + v)
+                            place = (unit + at, b, slot * (limit // ROWS) + part * group + v)
                             remain = kept(kept_ref, place, mine[v], their, width == 1)
                             totals[v] = pair(mine[v], their, totals[v], remain)
                     return tuple(totals)
@@ -253,7 +259,7 @@
                     if col < columns and (col != x or shift == 1):
                         calls.append((x, col, 0, form))
     units = sum(len(shifts) if form is None else 1 for *_, form in calls)
-    kept_shape = jax.ShapeDtypeStruct((units, width // LANES, slots, limit // ROWS, ROWS, LANES), jnp.float32)
+    kept_shape = jax.ShapeDtypeStruct((units, width // LANES, slots * limit // ROWS, ROWS, LANES), jnp.float32)
     keep = keep and not pressed
     if closeness_kept is not None:
         inputs.append(closeness_kept)
@@ -378,7 +384,7 @@
                     their = [jnp.broadcast_to(shifted[col, form, b, r, pl.ds(slot, 1), :], (ROWS, LANES)) for r in range(rows)]
                     back = None
                     for v in range(group):
-                        place = (unit, b, slot, part * group + v)
+                        place = (unit, b, slot * (limit // ROWS) + part * group + v)
                         remain = kept(kept_ref, place, mine[v], their, outs == 1)
                         totals[v], given = both(mine[v], their, totals[v], remain)
                         back = given if back is None else tuple(p + q for p, q in zip(back, given))
@@ -506,7 +512,7 @@
     inputs = [motion, partial, entropy, counts] + ([] if first else [density]) + m_left + m_right
     n_in, n_m = len(inputs), len(m_left)
     rows = 4
-    kept_shape = jax.ShapeDtypeStruct((2 * len(SHIFTS), width // LANES, slots, limit // ROWS, ROWS, LANES), jnp.float32)
+    kept_shape = jax.ShapeDtypeStruct((2 * len(SHIFTS), width // LANES, slots * limit // ROWS, ROWS, LANES), jnp.float32)
 
     def kernel(*refs):
         motion_ref, partial_ref, entropy_ref, counts_ref = refs[:4]

time: 143 us -> 142 us (level)
  no operation moved by 1% of the time
where the time goes in v6:
time: 142 us; the launch traced here: 141 us
  Pallas kernels  82.2 us (58%)
  starting transfers between devices  43.1 us (30%)
  waiting for transfers between devices  11.4 us (8%)
  local copies, waits for them, and re-layouts  2.8 us (2%)
    pallas_call x12, Pallas kernels, own_part(): pl.pallas_call(kernel, out_shape=(sums_shape, kept_shape) if keep else (s...  45.5 us
    ppermute x27, starting transfers between devices, pass_on(): lax.ppermute(value, axis, [(i, (i + step) % count) for i in range(count)])  43.1 us
    pallas_call x3, Pallas kernels, force_rest(): pl.pallas_call(kernel, out_shape=outs, in_specs=[VMEM] * n_in, out_specs=...  19.4 us
    ppermute x27, waiting for transfers between devices, pass_on(): lax.ppermute(value, axis, [(i, (i + step) % count) for i in range(count)])  11.4 us
    pallas_call x3, Pallas kernels, density_rest(): pl.pallas_call(kernel, out_shape=(jax.ShapeDtypeStruct((columns, PRESSURE...  10.1 us
    pallas_call x1, Pallas kernels, compact(): pl.pallas_call(kernel, out_shape=(jax.ShapeDtypeStruct((8, capacity), jnp...  4.64 us
  transfers between devices with their start and end apart: 27, of which 8 were waited for; matrix products, arithmetic and copies ran while one was open for 0% of the time, Pallas kernels for 33%

profile of v6, /device:TPU:0, one launch (start us, length us, event | category | flops | bytes accessed | tf_op | source)
XLA Modules:
  0.0 141.0 jit_solution(4588493309258991602)
XLA Ops:
  4.2 2.0 %collective-permute-start.1 = (f32[32,128]{1,0:T(8,128)S(1)}, f32[32,128]{1,0:T(8,128)S(1)}, u32[]{:S(2)}, u32[]{:S(2)}) collective-permute-start(f32[32,128]{1,0:T(8,128)S(1)} %get-tuple-element.57), channel_id=1, source_target_pairs={{0,3},{1,0},{2,1},{3,2},{4,7},{5,4},{6,5},{7,6},{8,11},{9,8},{10,9... | collective-permute-start | bytes 49160 | tf_op jit(solution)/shard_map/ppermute | solution.py:771
  6.2 2.5 %shard_map.65 = (f32[2,1,32,256]{3,2,1,0:T(8,128)S(1)}, f32[3,2,128,8,128]{4,3,2,1,0:T(8,128)S(1)}) custom-call(f32[2,7,32,256]{3,2,1,0:T(8,128)S(1)} %maximum_bitcast_fusion.motion_ref.own_refs_0_.refs_0_), custom_call_target="tpu_custom_call" | custom-call | flops 471859200 | bytes 1048576 | tf_op jit(solution)/shard_map/pallas_call | solution.py:325
  8.8 2.3 %collective-permute-start.2 = (f32[160,256]{1,0:T(8,128)S(1)}, f32[160,256]{1,0:T(8,128)S(1)}, u32[]{:S(2)}, u32[]{:S(2)}) collective-permute-start(f32[160,256]{1,0:T(8,128)S(1)} %get-tuple-element.132), channel_id=1, source_target_pairs={{0,4},{4,8},{8,12},{12,16},{16,20},{20,24},{24,28},{28,0},{1,5},{5... | collective-permute-start | bytes 491528 | tf_op jit(solution)/shard_map/ppermute | solution.py:771
  11.2 3.1 %collective-permute-start.3 = (f32[160,256]{1,0:T(8,128)S(1)}, f32[160,256]{1,0:T(8,128)S(1)}, u32[]{:S(2)}, u32[]{:S(2)}) collective-permute-start(f32[160,256]{1,0:T(8,128)S(1)} %get-tuple-element.131), channel_id=1, source_target_pairs={{0,28},{4,0},{8,4},{12,8},{16,12},{20,16},{24,20},{28,24},{1,29},{... | collective-permute-start | bytes 491528 | tf_op jit(solution)/shard_map/ppermute | solution.py:771
  14.3 4.7 %shard_map.66 = (f32[2,1,32,256]{3,2,1,0:T(8,128)S(1)}, f32[4,2,128,8,128]{4,3,2,1,0:T(8,128)S(1)}) custom-call(f32[2,7,32,256]{3,2,1,0:T(8,128)S(1)} %maximum_bitcast_fusion.motion_ref.own_refs_0_.refs_0_, f32[32,128]{1,0:T(8,128)S(1)} %collective-permute-done.own_refs_1_.own_refs_2_.own_refs_3_.own_refs_4_.own_refs_5_.own_refs_6_, ...), custom_call_target="tpu_custom_call" | custom-call | flops 943718400 | bytes 1048576 | tf_op jit(solution)/shard_map/pallas_call | solution.py:325
  20.9 5.4 %shard_map.67 = (f32[2,3,32,256]{3,2,1,0:T(8,128)S(1)}, f32[32,128]{1,0:T(8,128)S(1)}, f32[32,128]{1,0:T(8,128)S(1)}, f32[6,2,128,8,128]{4,3,2,1,0:T(8,128)S(1)}) custom-call(f32[2,7,32,256]{3,2,1,0:T(8,128)S(1)} %maximum_bitcast_fusion.motion_ref.own_refs_0_.refs_0_, f32[2,1,32,256]{3,2,1,0:T(8,128)S(1)} %get-tuple-element.62.refs_1_, ...), custom_call_target="tpu_custom_call" | custom-call | flops 707788800 | bytes 1048576 | tf_op jit(solution)/shard_map/pallas_call | solution.py:556
  28.2 5.1 %shard_map.68.own_refs_6_ = f32[2,3,32,256]{3,2,1,0:T(8,128)S(1)} custom-call(f32[2,7,32,256]{3,2,1,0:T(8,128)S(1)} %maximum_bitcast_fusion.motion_ref.own_refs_0_.refs_0_, f32[2,3,32,256]{3,2,1,0:T(8,128)S(1)} %get-tuple-element.63.own_refs_1_.refs_1_.refs_4_, f32[3,2,128,8,128]{4,3,2,1,0:T(8,128)S(1)} %get-tuple-element.66.own_refs_2_), custom_call_target="tpu_custom_call" | custom-call | flops 943718400 | bytes 1048576 | tf_op jit(solution)/shard_map/pallas_call | solution.py:325
  33.7 4.4 %collective-permute-start.7 = (f32[224,256]{1,0:T(8,128)S(1)}, f32[224,256]{1,0:T(8,128)S(1)}, u32[]{:S(2)}, u32[]{:S(2)}) collective-permute-start(f32[224,256]{1,0:T(8,128)S(1)} %get-tuple-element.129), channel_id=1, source_target_pairs={{0,28},{4,0},{8,4},{12,8},{16,12},{20,16},{24,20},{28,24},{1,29},{... | collective-permute-start | bytes 688136 | tf_op jit(solution)/shard_map/ppermute | solution.py:771
  38.1 9.8 %shard_map.69.refs_2_ = f32[2,3,32,256]{3,2,1,0:T(8,128)S(1)} custom-call(f32[2,7,32,256]{3,2,1,0:T(8,128)S(1)} %maximum_bitcast_fusion.motion_ref.own_refs_0_.refs_0_, f32[2,3,32,256]{3,2,1,0:T(8,128)S(1)} %get-tuple-element.63.own_refs_1_.refs_1_.refs_4_, ...), custom_call_target="tpu_custom_call" | custom-call | flops 1887436800 | bytes 1048576 | tf_op jit(solution)/shard_map/pallas_call | solution.py:325
  47.9 10.4 %shard_map.70 = (f32[2,7,32,256]{3,2,1,0:T(8,128)S(1)}, f32[32,128]{1,0:T(8,128)S(1)}, f32[32,128]{1,0:T(8,128)S(1)}) custom-call(f32[2,7,32,256]{3,2,1,0:T(8,128)S(1)} %maximum_bitcast_fusion.motion_ref.own_refs_0_.refs_0_, f32[2,3,32,256]{3,2,1,0:T(8,128)S(1)} %get-tuple-element.63.own_refs_1_.refs_1_.refs_4_, f32[2,3,32,256]{3,2,1,0:T(8,128)S(1)} %shard_map.69.refs_2_, ...), custom_call_target="tpu_custom_call" | custom-call | flops 1415577600 | bytes 1048576 | tf_op jit(solution)/shard_map/pallas_call | solution.py:624
  61.8 4.7 %collective-permute-start.11 = (f32[128,256]{1,0:T(8,128)S(1)}, f32[128,256]{1,0:T(8,128)S(1)}, u32[]{:S(2)}, u32[]{:S(2)}) collective-permute-start(f32[128,256]{1,0:T(8,128)S(1)} %get-tuple-element.127), channel_id=1, source_target_pairs={{0,28},{4,0},{8,4},{12,8},{16,12},{20,16},{24,20},{28,24},{1,29},{... | collective-permute-start | bytes 393224 | tf_op jit(solution)/shard_map/ppermute | solution.py:771
  66.5 3.5 %shard_map.72 = (f32[2,1,16,256]{3,2,1,0:T(8,128)S(1)}, f32[12,2,64,8,128]{4,3,2,1,0:T(8,128)S(1)}) custom-call(f32[2,7,32,256]{3,2,1,0:T(8,128)S(1)} %get-tuple-element.72.own_refs_0_.refs_0_, f32[32,128]{1,0:T(8,128)S(1)} %collective-permute-done.8.own_refs_1_.own_refs_2_.own_refs_3_.own_refs_4_, ...), custom_call_target="tpu_custom_call" | custom-call | flops 471859200 | bytes 1048576 | tf_op jit(solution)/shard_map/pallas_call | solution.py:325
  70.6 3.0 %shard_map.73 = (f32[2,3,32,256]{3,2,1,0:T(8,128)S(1)}, f32[16,128]{1,0:T(8,128)S(1)}, f32[16,128]{1,0:T(8,128)S(1)}, f32[6,2,64,8,128]{4,3,2,1,0:T(8,128)S(1)}) custom-call(f32[2,7,32,256]{3,2,1,0:T(8,128)S(1)} %get-tuple-element.72.own_refs_0_.refs_0_, f32[2,1,16,256]{3,2,1,0:T(8,128)S(1)} %get-tuple-element.79.refs_1_, f32[2,32,256]{2,1,0:T(8,128)S(1)} %bitcast.36, ...), custom_call_target="tpu_custom_call" | custom-call | flops 353894400 | bytes 1048576 | tf_op jit(solution)/shard_map/pallas_call | solution.py:556
  75.3 3.0 %shard_map.74.own_refs_10_ = f32[2,3,16,256]{3,2,1,0:T(8,128)S(1)} custom-call(f32[2,7,32,256]{3,2,1,0:T(8,128)S(1)} %get-tuple-element.72.own_refs_0_.refs_0_, f32[2,3,32,256]{3,2,1,0:T(8,128)S(1)} %get-tuple-element.80.own_refs_1_.refs_1_.refs_4_, f32[5,2,64,8,128]{4,3,2,1,0:T(8,128)S(1)} %get-tuple-element.83.own_refs_2_), custom_call_target="tpu_custom_call" | custom-call | flops 471859200 | bytes 1048576 | tf_op jit(solution)/shard_map/pallas_call | solution.py:325
  78.7 4.5 %collective-permute-start.15 = (f32[160,256]{1,0:T(8,128)S(1)}, f32[160,256]{1,0:T(8,128)S(1)}, u32[]{:S(2)}, u32[]{:S(2)}) collective-permute-start(f32[160,256]{1,0:T(8,128)S(1)} %get-tuple-element.135), channel_id=1, source_target_pairs={{0,28},{4,0},{8,4},{12,8},{16,12},{20,16},{24,20},{28,24},{1,29},{... | collective-permute-start | bytes 491528 | tf_op jit(solution)/shard_map/ppermute | solution.py:771
  83.2 6.7 %shard_map.75.refs_2_ = f32[2,3,16,256]{3,2,1,0:T(8,128)S(1)} custom-call(f32[2,7,32,256]{3,2,1,0:T(8,128)S(1)} %get-tuple-element.72.own_refs_0_.refs_0_, f32[2,3,32,256]{3,2,1,0:T(8,128)S(1)} %get-tuple-element.80.own_refs_1_.refs_1_.refs_4_, f32[32,128]{1,0:T(8,128)S(1)} %collective-permute-done.8.own_refs_1_.own_refs_2_.own_refs_3_.own_refs_4_, ...), custom_call_target="tpu_custom_call" | custom-call | flops 943718400 | bytes 1048576 | tf_op jit(solution)/shard_map/pallas_call | solution.py:325
  89.9 5.6 %shard_map.76 = (f32[2,7,32,256]{3,2,1,0:T(8,128)S(1)}, f32[16,128]{1,0:T(8,128)S(1)}, f32[16,128]{1,0:T(8,128)S(1)}) custom-call(f32[2,7,32,256]{3,2,1,0:T(8,128)S(1)} %get-tuple-element.72.own_refs_0_.refs_0_, f32[2,3,32,256]{3,2,1,0:T(8,128)S(1)} %get-tuple-element.80.own_refs_1_.refs_1_.refs_4_, f32[2,3,16,256]{3,2,1,0:T(8,128)S(1)} %shard_map.75.refs_2_, ...), custom_call_target="tpu_custom_call" | custom-call | flops 707788800 | bytes 1048576 | tf_op jit(solution)/shard_map/pallas_call | solution.py:624
  98.7 4.7 %collective-permute-start.19 = (f32[64,256]{1,0:T(8,128)S(1)}, f32[64,256]{1,0:T(8,128)S(1)}, u32[]{:S(2)}, u32[]{:S(2)}) collective-permute-start(f32[64,256]{1,0:T(8,128)S(1)} %get-tuple-element.133), channel_id=1, source_target_pairs={{0,28},{4,0},{8,4},{12,8},{16,12},{20,16},{24,20},{28,24},{1,29},{... | collective-permute-start | bytes 196616 | tf_op jit(solution)/shard_map/ppermute | solution.py:771
  103.4 2.0 %shard_map.78.refs_1_ = f32[2,1,8,256]{3,2,1,0:T(8,128)S(1)} custom-call(f32[2,7,32,256]{3,2,1,0:T(8,128)S(1)} %get-tuple-element.89.own_refs_0_.refs_0_, f32[16,128]{1,0:T(8,128)S(1)} %collective-permute-done.16.own_refs_1_.own_refs_2_, f32[16,128]{1,0:T(8,128)S(1)} %collective-permute-done.17.own_refs_2_.own_refs_3_, ...), custom_call_target="tpu_custom_call" | custom-call | flops 235929600 | bytes 1048576 | tf_op jit(solution)/shard_map/pallas_call | solution.py:325
  111.7 4.7 %collective-permute-start.23 = (f32[80,256]{1,0:T(8,128)S(1)}, f32[80,256]{1,0:T(8,128)S(1)}, u32[]{:S(2)}, u32[]{:S(2)}) collective-permute-start(f32[80,256]{1,0:T(8,128)S(1)} %get-tuple-element.137), channel_id=1, source_target_pairs={{0,28},{4,0},{8,4},{12,8},{16,12},{20,16},{24,20},{28,24},{1,29},{... | collective-permute-start | bytes 245768 | tf_op jit(solution)/shard_map/ppermute | solution.py:771
  117.4 4.2 %shard_map.81.refs_2_ = f32[2,3,8,256]{3,2,1,0:T(8,128)S(1)} custom-call(f32[2,7,32,256]{3,2,1,0:T(8,128)S(1)} %get-tuple-element.89.own_refs_0_.refs_0_, f32[2,3,32,256]{3,2,1,0:T(8,128)S(1)} %get-tuple-element.95.own_refs_1_.refs_1_.pressure_ref, f32[16,128]{1,0:T(8,128)S(1)} %collective-permute-done.16.own_refs_1_.own_refs_2_, ...), custom_call_target="tpu_custom_call" | custom-call | flops 471859200 | bytes 1048576 | tf_op jit(solution)/shard_map/pallas_call | solution.py:325
  121.6 3.4 %shard_map.82.motion_ref = f32[2,7,32,256]{3,2,1,0:T(8,128)S(1)} custom-call(f32[2,7,32,256]{3,2,1,0:T(8,128)S(1)} %get-tuple-element.89.own_refs_0_.refs_0_, f32[2,3,32,256]{3,2,1,0:T(8,128)S(1)} %get-tuple-element.95.own_refs_1_.refs_1_.pressure_ref, f32[2,3,8,256]{3,2,1,0:T(8,128)S(1)} %shard_map.81.refs_2_, s32[3,2,256]{2,1,0:T(2,128)S(1)} %copy-done, ...), custom_call_target="tpu_custom_call" | custom-call | flops 353894400 | bytes 1048576 | tf_op jit(solution)/shard_map/pallas_call | solution.py:624
  125.1 4.6 %shard_map.84 = (f32[8,6144]{1,0:T(8,128)S(1)}, f32[8,6144]{1,0:T(8,128)S(1)}, f32[8,6144]{1,0:T(8,128)S(1)}, f32[8,6144]{1,0:T(8,128)S(1)}) custom-call(f32[2,7,32,256]{3,2,1,0:T(8,128)S(1)} %shard_map.82.motion_ref, f32[2,3,32,256]{3,2,1,0:T(8,128)S(1)} %get-tuple-element.95.own_refs_1_.refs_1_.pressure_ref, s32[64,256]{1,0:T(8,128)S(1)} %get-tuple-element.101.place_ref, ...), custom_call_target="tpu_custom_call" | custom-call | tf_op jit(solution)/shard_map/pallas_call | solution.py:731
  132.0 4.3 %collective-permute-done.24.refs_1_ = f32[8,6144]{1,0:T(8,128)S(1)} collective-permute-done((f32[8,6144]{1,0:T(8,128)S(1)}, f32[8,6144]{1,0:T(8,128)S(1)}, u32[]{:S(2)}, u32[]{:S(2)}) %collective-permute-start.24) | collective-permute-done | bytes 196640 | tf_op jit(solution)/shard_map/ppermute | solution.py:771
  (90 shorter events, 31.7 us)
Async XLA Ops:
  3.7 5.1 %collective-permute-start = (f32[32,128]{1,0:T(8,128)S(1)}, f32[32,128]{1,0:T(8,128)S(1)}, u32[]{:S(2)}, u32[]{:S(2)}) collective-permute-start(f32[32,128]{1,0:T(8,128)S(1)} %get-tuple-element.56), channel_id=1, source_target_pairs={{0,1},{1,2},{2,3},{3,0},{4,5},{5,6},{6,7},{7,4},{8,9},{9,10},{10,1... | collective-permute-start | bytes 49160 | tf_op jit(solution)/shard_map/ppermute | solution.py:771
  4.2 4.6 %collective-permute-start.1 = (f32[32,128]{1,0:T(8,128)S(1)}, f32[32,128]{1,0:T(8,128)S(1)}, u32[]{:S(2)}, u32[]{:S(2)}) collective-permute-start(f32[32,128]{1,0:T(8,128)S(1)} %get-tuple-element.57), channel_id=1, source_target_pairs={{0,3},{1,0},{2,1},{3,2},{4,7},{5,4},{6,5},{7,6},{8,11},{9,8},{10,9... | collective-permute-start | bytes 49160 | tf_op jit(solution)/shard_map/ppermute | solution.py:771
  8.8 10.2 %collective-permute-start.2 = (f32[160,256]{1,0:T(8,128)S(1)}, f32[160,256]{1,0:T(8,128)S(1)}, u32[]{:S(2)}, u32[]{:S(2)}) collective-permute-start(f32[160,256]{1,0:T(8,128)S(1)} %get-tuple-element.132), channel_id=1, source_target_pairs={{0,4},{4,8},{8,12},{12,16},{16,20},{20,24},{24,28},{28,0},{1,5},{5... | collective-permute-start | bytes 491528 | tf_op jit(solution)/shard_map/ppermute | solution.py:771
  11.2 9.8 %collective-permute-start.3 = (f32[160,256]{1,0:T(8,128)S(1)}, f32[160,256]{1,0:T(8,128)S(1)}, u32[]{:S(2)}, u32[]{:S(2)}) collective-permute-start(f32[160,256]{1,0:T(8,128)S(1)} %get-tuple-element.131), channel_id=1, source_target_pairs={{0,28},{4,0},{8,4},{12,8},{16,12},{20,16},{24,20},{28,24},{1,29},{... | collective-permute-start | bytes 491528 | tf_op jit(solution)/shard_map/ppermute | solution.py:771
  26.4 6.9 %collective-permute-start.4 = (f32[32,128]{1,0:T(8,128)S(1)}, f32[32,128]{1,0:T(8,128)S(1)}, u32[]{:S(2)}, u32[]{:S(2)}) collective-permute-start(f32[32,128]{1,0:T(8,128)S(1)} %get-tuple-element.64), channel_id=1, source_target_pairs={{0,1},{1,2},{2,3},{3,0},{4,5},{5,6},{6,7},{7,4},{8,9},{9,10},{10,1... | collective-permute-start | bytes 49160 | tf_op jit(solution)/shard_map/ppermute | solution.py:771
  26.4 6.9 %collective-permute-start.5 = (f32[32,128]{1,0:T(8,128)S(1)}, f32[32,128]{1,0:T(8,128)S(1)}, u32[]{:S(2)}, u32[]{:S(2)}) collective-permute-start(f32[32,128]{1,0:T(8,128)S(1)} %get-tuple-element.65), channel_id=1, source_target_pairs={{0,3},{1,0},{2,1},{3,2},{4,7},{5,4},{6,5},{7,6},{8,11},{9,8},{10,9... | collective-permute-start | bytes 49160 | tf_op jit(solution)/shard_map/ppermute | solution.py:771
  33.4 14.6 %collective-permute-start.6 = (f32[224,256]{1,0:T(8,128)S(1)}, f32[224,256]{1,0:T(8,128)S(1)}, u32[]{:S(2)}, u32[]{:S(2)}) collective-permute-start(f32[224,256]{1,0:T(8,128)S(1)} %get-tuple-element.130), channel_id=1, source_target_pairs={{0,4},{4,8},{8,12},{12,16},{16,20},{20,24},{24,28},{28,0},{1,5},{5... | collective-permute-start | bytes 688136 | tf_op jit(solution)/shard_map/ppermute | solution.py:771
  33.7 14.2 %collective-permute-start.7 = (f32[224,256]{1,0:T(8,128)S(1)}, f32[224,256]{1,0:T(8,128)S(1)}, u32[]{:S(2)}, u32[]{:S(2)}) collective-permute-start(f32[224,256]{1,0:T(8,128)S(1)} %get-tuple-element.129), channel_id=1, source_target_pairs={{0,28},{4,0},{8,4},{12,8},{16,12},{20,16},{24,20},{28,24},{1,29},{... | collective-permute-start | bytes 688136 | tf_op jit(solution)/shard_map/ppermute | solution.py:771
  58.4 3.3 %collective-permute-start.8 = (f32[32,128]{1,0:T(8,128)S(1)}, f32[32,128]{1,0:T(8,128)S(1)}, u32[]{:S(2)}, u32[]{:S(2)}) collective-permute-start(f32[32,128]{1,0:T(8,128)S(1)} %get-tuple-element.73), channel_id=1, source_target_pairs={{0,1},{1,2},{2,3},{3,0},{4,5},{5,6},{6,7},{7,4},{8,9},{9,10},{10,1... | collective-permute-start | bytes 49160 | tf_op jit(solution)/shard_map/ppermute | solution.py:771
  61.7 8.8 %collective-permute-start.10 = (f32[128,256]{1,0:T(8,128)S(1)}, f32[128,256]{1,0:T(8,128)S(1)}, u32[]{:S(2)}, u32[]{:S(2)}) collective-permute-start(f32[128,256]{1,0:T(8,128)S(1)} %get-tuple-element.128), channel_id=1, source_target_pairs={{0,4},{4,8},{8,12},{12,16},{16,20},{20,24},{24,28},{28,0},{1,5},{5... | collective-permute-start | bytes 393224 | tf_op jit(solution)/shard_map/ppermute | solution.py:771
  61.8 8.8 %collective-permute-start.11 = (f32[128,256]{1,0:T(8,128)S(1)}, f32[128,256]{1,0:T(8,128)S(1)}, u32[]{:S(2)}, u32[]{:S(2)}) collective-permute-start(f32[128,256]{1,0:T(8,128)S(1)} %get-tuple-element.127), channel_id=1, source_target_pairs={{0,28},{4,0},{8,4},{12,8},{16,12},{20,16},{24,20},{28,24},{1,29},{... | collective-permute-start | bytes 393224 | tf_op jit(solution)/shard_map/ppermute | solution.py:771
  73.5 4.8 %collective-permute-start.12 = (f32[16,128]{1,0:T(8,128)S(1)}, f32[16,128]{1,0:T(8,128)S(1)}, u32[]{:S(2)}, u32[]{:S(2)}) collective-permute-start(f32[16,128]{1,0:T(8,128)S(1)} %get-tuple-element.81), channel_id=1, source_target_pairs={{0,1},{1,2},{2,3},{3,0},{4,5},{5,6},{6,7},{7,4},{8,9},{9,10},{10,1... | collective-permute-start | bytes 24584 | tf_op jit(solution)/shard_map/ppermute | solution.py:771
  73.6 4.7 %collective-permute-start.13 = (f32[16,128]{1,0:T(8,128)S(1)}, f32[16,128]{1,0:T(8,128)S(1)}, u32[]{:S(2)}, u32[]{:S(2)}) collective-permute-start(f32[16,128]{1,0:T(8,128)S(1)} %get-tuple-element.82), channel_id=1, source_target_pairs={{0,3},{1,0},{2,1},{3,2},{4,7},{5,4},{6,5},{7,6},{8,11},{9,8},{10,9... | collective-permute-start | bytes 24584 | tf_op jit(solution)/shard_map/ppermute | solution.py:771
  78.4 11.5 %collective-permute-start.14 = (f32[160,256]{1,0:T(8,128)S(1)}, f32[160,256]{1,0:T(8,128)S(1)}, u32[]{:S(2)}, u32[]{:S(2)}) collective-permute-start(f32[160,256]{1,0:T(8,128)S(1)} %get-tuple-element.136), channel_id=1, source_target_pairs={{0,4},{4,8},{8,12},{12,16},{16,20},{20,24},{24,28},{28,0},{1,5},{5... | collective-permute-start | bytes 491528 | tf_op jit(solution)/shard_map/ppermute | solution.py:771
  78.7 11.2 %collective-permute-start.15 = (f32[160,256]{1,0:T(8,128)S(1)}, f32[160,256]{1,0:T(8,128)S(1)}, u32[]{:S(2)}, u32[]{:S(2)}) collective-permute-start(f32[160,256]{1,0:T(8,128)S(1)} %get-tuple-element.135), channel_id=1, source_target_pairs={{0,28},{4,0},{8,4},{12,8},{16,12},{20,16},{24,20},{28,24},{1,29},{... | collective-permute-start | bytes 491528 | tf_op jit(solution)/shard_map/ppermute | solution.py:771
  98.7 7.6 %collective-permute-start.18 = (f32[64,256]{1,0:T(8,128)S(1)}, f32[64,256]{1,0:T(8,128)S(1)}, u32[]{:S(2)}, u32[]{:S(2)}) collective-permute-start(f32[64,256]{1,0:T(8,128)S(1)} %get-tuple-element.134), channel_id=1, source_target_pairs={{0,4},{4,8},{8,12},{12,16},{16,20},{20,24},{24,28},{28,0},{1,5},{5... | collective-permute-start | bytes 196616 | tf_op jit(solution)/shard_map/ppermute | solution.py:771
  98.7 7.5 %collective-permute-start.19 = (f32[64,256]{1,0:T(8,128)S(1)}, f32[64,256]{1,0:T(8,128)S(1)}, u32[]{:S(2)}, u32[]{:S(2)}) collective-permute-start(f32[64,256]{1,0:T(8,128)S(1)} %get-tuple-element.133), channel_id=1, source_target_pairs={{0,28},{4,0},{8,4},{12,8},{16,12},{20,16},{24,20},{28,24},{1,29},{... | collective-permute-start | bytes 196616 | tf_op jit(solution)/shard_map/ppermute | solution.py:771
  108.0 3.6 %collective-permute-start.20 = (f32[8,128]{1,0:T(8,128)S(1)}, f32[8,128]{1,0:T(8,128)S(1)}, u32[]{:S(2)}, u32[]{:S(2)}) collective-permute-start(f32[8,128]{1,0:T(8,128)S(1)} %get-tuple-element.96), channel_id=1, source_target_pairs={{0,1},{1,2},{2,3},{3,0},{4,5},{5,6},{6,7},{7,4},{8,9},{9,10},{10,1... | collective-permute-start | bytes 12296 | tf_op jit(solution)/shard_map/ppermute | solution.py:771
  108.1 3.6 %collective-permute-start.21 = (f32[8,128]{1,0:T(8,128)S(1)}, f32[8,128]{1,0:T(8,128)S(1)}, u32[]{:S(2)}, u32[]{:S(2)}) collective-permute-start(f32[8,128]{1,0:T(8,128)S(1)} %get-tuple-element.97), channel_id=1, source_target_pairs={{0,3},{1,0},{2,1},{3,2},{4,7},{5,4},{6,5},{7,6},{8,11},{9,8},{10,9... | collective-permute-start | bytes 12296 | tf_op jit(solution)/shard_map/ppermute | solution.py:771
  111.7 9.9 %collective-permute-start.22 = (f32[80,256]{1,0:T(8,128)S(1)}, f32[80,256]{1,0:T(8,128)S(1)}, u32[]{:S(2)}, u32[]{:S(2)}) collective-permute-start(f32[80,256]{1,0:T(8,128)S(1)} %get-tuple-element.138), channel_id=1, source_target_pairs={{0,4},{4,8},{8,12},{12,16},{16,20},{20,24},{24,28},{28,0},{1,5},{5... | collective-permute-start | bytes 245768 | tf_op jit(solution)/shard_map/ppermute | solution.py:771
  111.7 9.9 %collective-permute-start.23 = (f32[80,256]{1,0:T(8,128)S(1)}, f32[80,256]{1,0:T(8,128)S(1)}, u32[]{:S(2)}, u32[]{:S(2)}) collective-permute-start(f32[80,256]{1,0:T(8,128)S(1)} %get-tuple-element.137), channel_id=1, source_target_pairs={{0,28},{4,0},{8,4},{12,8},{16,12},{20,16},{24,20},{28,24},{1,29},{... | collective-permute-start | bytes 245768 | tf_op jit(solution)/shard_map/ppermute | solution.py:771
  129.7 6.6 %collective-permute-start.24 = (f32[8,6144]{1,0:T(8,128)S(1)}, f32[8,6144]{1,0:T(8,128)S(1)}, u32[]{:S(2)}, u32[]{:S(2)}) collective-permute-start(f32[8,6144]{1,0:T(8,128)S(1)} %get-tuple-element.104), channel_id=1, source_target_pairs={{0,1},{1,2},{2,3},{3,0},{4,5},{5,6},{6,7},{7,4},{8,9},{9,10},{10,1... | collective-permute-start | bytes 589832 | tf_op jit(solution)/shard_map/ppermute | solution.py:771
  129.8 7.7 %collective-permute-start.25 = (f32[8,6144]{1,0:T(8,128)S(1)}, f32[8,6144]{1,0:T(8,128)S(1)}, u32[]{:S(2)}, u32[]{:S(2)}) collective-permute-start(f32[8,6144]{1,0:T(8,128)S(1)} %get-tuple-element.105), channel_id=1, source_target_pairs={{0,2},{1,3},{2,0},{3,1},{4,6},{5,7},{6,4},{7,5},{8,10},{9,11},{10,... | collective-permute-start | bytes 589832 | tf_op jit(solution)/shard_map/ppermute | solution.py:771
  130.8 8.7 %collective-permute-start.26 = (f32[8,6144]{1,0:T(8,128)S(1)}, f32[8,6144]{1,0:T(8,128)S(1)}, u32[]{:S(2)}, u32[]{:S(2)}) collective-permute-start(f32[8,6144]{1,0:T(8,128)S(1)} %get-tuple-element.106), channel_id=1, source_target_pairs={{0,3},{1,0},{2,1},{3,2},{4,7},{5,4},{6,5},{7,6},{8,11},{9,8},{10,9... | collective-permute-start | bytes 589832 | tf_op jit(solution)/shard_map/ppermute | solution.py:771
  (6 other events, 67.8 us)

commit v7 on v6

--- a/solution.py
+++ b/solution.py
@@ -142,7 +142,7 @@
     blocks = shifted.shape[2]
     rows = shifted.shape[3]
     group = min(limit // ROWS, 2 if width == 3 else 4)
-    unroll = min(slots - start, 16 // group if width == 3 else 32 // group)
+    unroll = min(slots - start, 32 // group)
     forms = shifted.shape[1]
     low_col, low_shift = sources[0]
 
@@ -366,7 +366,7 @@
     both = both_force if outs == 3 else both_density
     sign = -1.0 if outs == 3 else 1.0
     group = min(limit // ROWS, 2 if outs == 3 else 4)
-    unroll = 8
+    unroll = 16
 
     def lane_block(b, carry):
         lanes = pl.ds(pl.multiple_of(b * LANES, LANES), LANES)

time: 142 us -> 139 us (0.979)
  Pallas kernels: 82.2 us -> 78.6 us
    pallas_call x12, Pallas kernels: 45.5 us -> 43.2 us  [own_part(): pl.pallas_call(kernel, out_shape=(sums_shape, kept_shape) if keep else (s...]
  transfers between devices with their start and end apart: 27 -> 27, of which waited for: 8 -> 9; matrix products, arithmetic and copies ran while one was open for 0% -> 0% of each run, Pallas kernels for 33% -> 32%
where the time goes in v7:
time: 139 us; the launch traced here: 138 us
  Pallas kernels  78.6 us (57%)
  starting transfers between devices  43 us (31%)
  waiting for transfers between devices  11.6 us (8%)
  local copies, waits for them, and re-layouts  2.8 us (2%)
    pallas_call x12, Pallas kernels, own_part(): pl.pallas_call(kernel, out_shape=(sums_shape, kept_shape) if keep else (s...  43.2 us
    ppermute x27, starting transfers between devices, pass_on(): lax.ppermute(value, axis, [(i, (i + step) % count) for i in range(count)])  43 us
    pallas_call x3, Pallas kernels, force_rest(): pl.pallas_call(kernel, out_shape=outs, in_specs=[VMEM] * n_in, out_specs=...  18.2 us
    ppermute x27, waiting for transfers between devices, pass_on(): lax.ppermute(value, axis, [(i, (i + step) % count) for i in range(count)])  11.6 us
    pallas_call x3, Pallas kernels, density_rest(): pl.pallas_call(kernel, out_shape=(jax.ShapeDtypeStruct((columns, PRESSURE...  10.1 us
    pallas_call x1, Pallas kernels, compact(): pl.pallas_call(kernel, out_shape=(jax.ShapeDtypeStruct((8, capacity), jnp...  4.63 us
  transfers between devices with their start and end apart: 27, of which 9 were waited for; matrix products, arithmetic and copies ran while one was open for 0% of the time, Pallas kernels for 32%

profile of v7, /device:TPU:0, one launch (start us, length us, event | category | flops | bytes accessed | tf_op | source)
XLA Modules:
  0.0 137.6 jit_solution(2461021604238644665)
XLA Ops:
  4.2 2.0 %collective-permute-start.1 = (f32[32,128]{1,0:T(8,128)S(1)}, f32[32,128]{1,0:T(8,128)S(1)}, u32[]{:S(2)}, u32[]{:S(2)}) collective-permute-start(f32[32,128]{1,0:T(8,128)S(1)} %get-tuple-element.57), channel_id=1, source_target_pairs={{0,3},{1,0},{2,1},{3,2},{4,7},{5,4},{6,5},{7,6},{8,11},{9,8},{10,9... | collective-permute-start | bytes 49160 | tf_op jit(solution)/shard_map/ppermute | solution.py:771
  6.2 2.5 %shard_map.65 = (f32[2,1,32,256]{3,2,1,0:T(8,128)S(1)}, f32[3,2,128,8,128]{4,3,2,1,0:T(8,128)S(1)}) custom-call(f32[2,7,32,256]{3,2,1,0:T(8,128)S(1)} %maximum_bitcast_fusion.motion_ref.own_refs_0_.refs_0_), custom_call_target="tpu_custom_call" | custom-call | flops 471859200 | bytes 1048576 | tf_op jit(solution)/shard_map/pallas_call | solution.py:325
  8.8 2.3 %collective-permute-start.2 = (f32[160,256]{1,0:T(8,128)S(1)}, f32[160,256]{1,0:T(8,128)S(1)}, u32[]{:S(2)}, u32[]{:S(2)}) collective-permute-start(f32[160,256]{1,0:T(8,128)S(1)} %get-tuple-element.132), channel_id=1, source_target_pairs={{0,4},{4,8},{8,12},{12,16},{16,20},{20,24},{24,28},{28,0},{1,5},{5... | collective-permute-start | bytes 491528 | tf_op jit(solution)/shard_map/ppermute | solution.py:771
  11.1 3.1 %collective-permute-start.3 = (f32[160,256]{1,0:T(8,128)S(1)}, f32[160,256]{1,0:T(8,128)S(1)}, u32[]{:S(2)}, u32[]{:S(2)}) collective-permute-start(f32[160,256]{1,0:T(8,128)S(1)} %get-tuple-element.131), channel_id=1, source_target_pairs={{0,28},{4,0},{8,4},{12,8},{16,12},{20,16},{24,20},{28,24},{1,29},{... | collective-permute-start | bytes 491528 | tf_op jit(solution)/shard_map/ppermute | solution.py:771
  14.2 4.5 %shard_map.66 = (f32[2,1,32,256]{3,2,1,0:T(8,128)S(1)}, f32[4,2,128,8,128]{4,3,2,1,0:T(8,128)S(1)}) custom-call(f32[2,7,32,256]{3,2,1,0:T(8,128)S(1)} %maximum_bitcast_fusion.motion_ref.own_refs_0_.refs_0_, f32[32,128]{1,0:T(8,128)S(1)} %collective-permute-done.own_refs_1_.own_refs_2_.own_refs_3_.own_refs_4_.own_refs_5_.own_refs_6_, ...), custom_call_target="tpu_custom_call" | custom-call | flops 943718400 | bytes 1048576 | tf_op jit(solution)/shard_map/pallas_call | solution.py:325
  20.9 5.4 %shard_map.67 = (f32[2,3,32,256]{3,2,1,0:T(8,128)S(1)}, f32[32,128]{1,0:T(8,128)S(1)}, f32[32,128]{1,0:T(8,128)S(1)}, f32[6,2,128,8,128]{4,3,2,1,0:T(8,128)S(1)}) custom-call(f32[2,7,32,256]{3,2,1,0:T(8,128)S(1)} %maximum_bitcast_fusion.motion_ref.own_refs_0_.refs_0_, f32[2,1,32,256]{3,2,1,0:T(8,128)S(1)} %get-tuple-element.62.refs_1_, ...), custom_call_target="tpu_custom_call" | custom-call | flops 707788800 | bytes 1048576 | tf_op jit(solution)/shard_map/pallas_call | solution.py:556
  28.1 4.8 %shard_map.68.own_refs_6_ = f32[2,3,32,256]{3,2,1,0:T(8,128)S(1)} custom-call(f32[2,7,32,256]{3,2,1,0:T(8,128)S(1)} %maximum_bitcast_fusion.motion_ref.own_refs_0_.refs_0_, f32[2,3,32,256]{3,2,1,0:T(8,128)S(1)} %get-tuple-element.63.own_refs_1_.refs_1_.refs_4_, f32[3,2,128,8,128]{4,3,2,1,0:T(8,128)S(1)} %get-tuple-element.66.own_refs_2_), custom_call_target="tpu_custom_call" | custom-call | flops 943718400 | bytes 1048576 | tf_op jit(solution)/shard_map/pallas_call | solution.py:325
  33.3 4.4 %collective-permute-start.7 = (f32[224,256]{1,0:T(8,128)S(1)}, f32[224,256]{1,0:T(8,128)S(1)}, u32[]{:S(2)}, u32[]{:S(2)}) collective-permute-start(f32[224,256]{1,0:T(8,128)S(1)} %get-tuple-element.129), channel_id=1, source_target_pairs={{0,28},{4,0},{8,4},{12,8},{16,12},{20,16},{24,20},{28,24},{1,29},{... | collective-permute-start | bytes 688136 | tf_op jit(solution)/shard_map/ppermute | solution.py:771
  37.8 9.4 %shard_map.69.refs_2_ = f32[2,3,32,256]{3,2,1,0:T(8,128)S(1)} custom-call(f32[2,7,32,256]{3,2,1,0:T(8,128)S(1)} %maximum_bitcast_fusion.motion_ref.own_refs_0_.refs_0_, f32[2,3,32,256]{3,2,1,0:T(8,128)S(1)} %get-tuple-element.63.own_refs_1_.refs_1_.refs_4_, ...), custom_call_target="tpu_custom_call" | custom-call | flops 1887436800 | bytes 1048576 | tf_op jit(solution)/shard_map/pallas_call | solution.py:325
  47.2 9.7 %shard_map.70 = (f32[2,7,32,256]{3,2,1,0:T(8,128)S(1)}, f32[32,128]{1,0:T(8,128)S(1)}, f32[32,128]{1,0:T(8,128)S(1)}) custom-call(f32[2,7,32,256]{3,2,1,0:T(8,128)S(1)} %maximum_bitcast_fusion.motion_ref.own_refs_0_.refs_0_, f32[2,3,32,256]{3,2,1,0:T(8,128)S(1)} %get-tuple-element.63.own_refs_1_.refs_1_.refs_4_, f32[2,3,32,256]{3,2,1,0:T(8,128)S(1)} %shard_map.69.refs_2_, ...), custom_call_target="tpu_custom_call" | custom-call | flops 1415577600 | bytes 1048576 | tf_op jit(solution)/shard_map/pallas_call | solution.py:624
  60.3 4.7 %collective-permute-start.11 = (f32[128,256]{1,0:T(8,128)S(1)}, f32[128,256]{1,0:T(8,128)S(1)}, u32[]{:S(2)}, u32[]{:S(2)}) collective-permute-start(f32[128,256]{1,0:T(8,128)S(1)} %get-tuple-element.127), channel_id=1, source_target_pairs={{0,28},{4,0},{8,4},{12,8},{16,12},{20,16},{24,20},{28,24},{1,29},{... | collective-permute-start | bytes 393224 | tf_op jit(solution)/shard_map/ppermute | solution.py:771
  65.0 3.4 %shard_map.72 = (f32[2,1,16,256]{3,2,1,0:T(8,128)S(1)}, f32[12,2,64,8,128]{4,3,2,1,0:T(8,128)S(1)}) custom-call(f32[2,7,32,256]{3,2,1,0:T(8,128)S(1)} %get-tuple-element.72.own_refs_0_.refs_0_, f32[32,128]{1,0:T(8,128)S(1)} %collective-permute-done.8.own_refs_1_.own_refs_2_.own_refs_3_.own_refs_4_, ...), custom_call_target="tpu_custom_call" | custom-call | flops 471859200 | bytes 1048576 | tf_op jit(solution)/shard_map/pallas_call | solution.py:325
  69.3 3.0 %shard_map.73 = (f32[2,3,32,256]{3,2,1,0:T(8,128)S(1)}, f32[16,128]{1,0:T(8,128)S(1)}, f32[16,128]{1,0:T(8,128)S(1)}, f32[6,2,64,8,128]{4,3,2,1,0:T(8,128)S(1)}) custom-call(f32[2,7,32,256]{3,2,1,0:T(8,128)S(1)} %get-tuple-element.72.own_refs_0_.refs_0_, f32[2,1,16,256]{3,2,1,0:T(8,128)S(1)} %get-tuple-element.79.refs_1_, f32[2,32,256]{2,1,0:T(8,128)S(1)} %bitcast.36, ...), custom_call_target="tpu_custom_call" | custom-call | flops 353894400 | bytes 1048576 | tf_op jit(solution)/shard_map/pallas_call | solution.py:556
  74.0 2.7 %shard_map.74.own_refs_10_ = f32[2,3,16,256]{3,2,1,0:T(8,128)S(1)} custom-call(f32[2,7,32,256]{3,2,1,0:T(8,128)S(1)} %get-tuple-element.72.own_refs_0_.refs_0_, f32[2,3,32,256]{3,2,1,0:T(8,128)S(1)} %get-tuple-element.80.own_refs_1_.refs_1_.refs_4_, f32[5,2,64,8,128]{4,3,2,1,0:T(8,128)S(1)} %get-tuple-element.83.own_refs_2_), custom_call_target="tpu_custom_call" | custom-call | flops 471859200 | bytes 1048576 | tf_op jit(solution)/shard_map/pallas_call | solution.py:325
  76.9 4.7 %collective-permute-start.15 = (f32[160,256]{1,0:T(8,128)S(1)}, f32[160,256]{1,0:T(8,128)S(1)}, u32[]{:S(2)}, u32[]{:S(2)}) collective-permute-start(f32[160,256]{1,0:T(8,128)S(1)} %get-tuple-element.135), channel_id=1, source_target_pairs={{0,28},{4,0},{8,4},{12,8},{16,12},{20,16},{24,20},{28,24},{1,29},{... | collective-permute-start | bytes 491528 | tf_op jit(solution)/shard_map/ppermute | solution.py:771
  81.6 6.1 %shard_map.75.refs_2_ = f32[2,3,16,256]{3,2,1,0:T(8,128)S(1)} custom-call(f32[2,7,32,256]{3,2,1,0:T(8,128)S(1)} %get-tuple-element.72.own_refs_0_.refs_0_, f32[2,3,32,256]{3,2,1,0:T(8,128)S(1)} %get-tuple-element.80.own_refs_1_.refs_1_.refs_4_, f32[32,128]{1,0:T(8,128)S(1)} %collective-permute-done.8.own_refs_1_.own_refs_2_.own_refs_3_.own_refs_4_, ...), custom_call_target="tpu_custom_call" | custom-call | flops 943718400 | bytes 1048576 | tf_op jit(solution)/shard_map/pallas_call | solution.py:325
  87.8 5.2 %shard_map.76 = (f32[2,7,32,256]{3,2,1,0:T(8,128)S(1)}, f32[16,128]{1,0:T(8,128)S(1)}, f32[16,128]{1,0:T(8,128)S(1)}) custom-call(f32[2,7,32,256]{3,2,1,0:T(8,128)S(1)} %get-tuple-element.72.own_refs_0_.refs_0_, f32[2,3,32,256]{3,2,1,0:T(8,128)S(1)} %get-tuple-element.80.own_refs_1_.refs_1_.refs_4_, f32[2,3,16,256]{3,2,1,0:T(8,128)S(1)} %shard_map.75.refs_2_, ...), custom_call_target="tpu_custom_call" | custom-call | flops 707788800 | bytes 1048576 | tf_op jit(solution)/shard_map/pallas_call | solution.py:624
  96.3 4.7 %collective-permute-start.19 = (f32[64,256]{1,0:T(8,128)S(1)}, f32[64,256]{1,0:T(8,128)S(1)}, u32[]{:S(2)}, u32[]{:S(2)}) collective-permute-start(f32[64,256]{1,0:T(8,128)S(1)} %get-tuple-element.133), channel_id=1, source_target_pairs={{0,28},{4,0},{8,4},{12,8},{16,12},{20,16},{24,20},{28,24},{1,29},{... | collective-permute-start | bytes 196616 | tf_op jit(solution)/shard_map/ppermute | solution.py:771
  101.0 2.0 %shard_map.78.refs_1_ = f32[2,1,8,256]{3,2,1,0:T(8,128)S(1)} custom-call(f32[2,7,32,256]{3,2,1,0:T(8,128)S(1)} %get-tuple-element.89.own_refs_0_.refs_0_, f32[16,128]{1,0:T(8,128)S(1)} %collective-permute-done.16.own_refs_1_.own_refs_2_, f32[16,128]{1,0:T(8,128)S(1)} %collective-permute-done.17.own_refs_2_.own_refs_3_, ...), custom_call_target="tpu_custom_call" | custom-call | flops 235929600 | bytes 1048576 | tf_op jit(solution)/shard_map/pallas_call | solution.py:325
  108.9 4.8 %collective-permute-start.23 = (f32[80,256]{1,0:T(8,128)S(1)}, f32[80,256]{1,0:T(8,128)S(1)}, u32[]{:S(2)}, u32[]{:S(2)}) collective-permute-start(f32[80,256]{1,0:T(8,128)S(1)} %get-tuple-element.137), channel_id=1, source_target_pairs={{0,28},{4,0},{8,4},{12,8},{16,12},{20,16},{24,20},{28,24},{1,29},{... | collective-permute-start | bytes 245768 | tf_op jit(solution)/shard_map/ppermute | solution.py:771
  114.6 3.9 %shard_map.81.refs_2_ = f32[2,3,8,256]{3,2,1,0:T(8,128)S(1)} custom-call(f32[2,7,32,256]{3,2,1,0:T(8,128)S(1)} %get-tuple-element.89.own_refs_0_.refs_0_, f32[2,3,32,256]{3,2,1,0:T(8,128)S(1)} %get-tuple-element.95.own_refs_1_.refs_1_.pressure_ref, f32[16,128]{1,0:T(8,128)S(1)} %collective-permute-done.16.own_refs_1_.own_refs_2_, ...), custom_call_target="tpu_custom_call" | custom-call | flops 471859200 | bytes 1048576 | tf_op jit(solution)/shard_map/pallas_call | solution.py:325
  118.6 3.3 %shard_map.82.motion_ref = f32[2,7,32,256]{3,2,1,0:T(8,128)S(1)} custom-call(f32[2,7,32,256]{3,2,1,0:T(8,128)S(1)} %get-tuple-element.89.own_refs_0_.refs_0_, f32[2,3,32,256]{3,2,1,0:T(8,128)S(1)} %get-tuple-element.95.own_refs_1_.refs_1_.pressure_ref, f32[2,3,8,256]{3,2,1,0:T(8,128)S(1)} %shard_map.81.refs_2_, s32[3,2,256]{2,1,0:T(2,128)S(1)} %copy-done, ...), custom_call_target="tpu_custom_call" | custom-call | flops 353894400 | bytes 1048576 | tf_op jit(solution)/shard_map/pallas_call | solution.py:624
  121.9 4.6 %shard_map.84 = (f32[8,6144]{1,0:T(8,128)S(1)}, f32[8,6144]{1,0:T(8,128)S(1)}, f32[8,6144]{1,0:T(8,128)S(1)}, f32[8,6144]{1,0:T(8,128)S(1)}) custom-call(f32[2,7,32,256]{3,2,1,0:T(8,128)S(1)} %shard_map.82.motion_ref, f32[2,3,32,256]{3,2,1,0:T(8,128)S(1)} %get-tuple-element.95.own_refs_1_.refs_1_.pressure_ref, s32[64,256]{1,0:T(8,128)S(1)} %get-tuple-element.101.place_ref, ...), custom_call_target="tpu_custom_call" | custom-call | tf_op jit(solution)/shard_map/pallas_call | solution.py:731
  128.6 4.5 %collective-permute-done.24.refs_1_ = f32[8,6144]{1,0:T(8,128)S(1)} collective-permute-done((f32[8,6144]{1,0:T(8,128)S(1)}, f32[8,6144]{1,0:T(8,128)S(1)}, u32[]{:S(2)}, u32[]{:S(2)}) %collective-permute-start.24) | collective-permute-done | bytes 196640 | tf_op jit(solution)/shard_map/ppermute | solution.py:771
  (90 shorter events, 31.4 us)
Async XLA Ops:
  3.7 5.0 %collective-permute-start = (f32[32,128]{1,0:T(8,128)S(1)}, f32[32,128]{1,0:T(8,128)S(1)}, u32[]{:S(2)}, u32[]{:S(2)}) collective-permute-start(f32[32,128]{1,0:T(8,128)S(1)} %get-tuple-element.56), channel_id=1, source_target_pairs={{0,1},{1,2},{2,3},{3,0},{4,5},{5,6},{6,7},{7,4},{8,9},{9,10},{10,1... | collective-permute-start | bytes 49160 | tf_op jit(solution)/shard_map/ppermute | solution.py:771
  4.2 4.5 %collective-permute-start.1 = (f32[32,128]{1,0:T(8,128)S(1)}, f32[32,128]{1,0:T(8,128)S(1)}, u32[]{:S(2)}, u32[]{:S(2)}) collective-permute-start(f32[32,128]{1,0:T(8,128)S(1)} %get-tuple-element.57), channel_id=1, source_target_pairs={{0,3},{1,0},{2,1},{3,2},{4,7},{5,4},{6,5},{7,6},{8,11},{9,8},{10,9... | collective-permute-start | bytes 49160 | tf_op jit(solution)/shard_map/ppermute | solution.py:771
  8.8 10.3 %collective-permute-start.2 = (f32[160,256]{1,0:T(8,128)S(1)}, f32[160,256]{1,0:T(8,128)S(1)}, u32[]{:S(2)}, u32[]{:S(2)}) collective-permute-start(f32[160,256]{1,0:T(8,128)S(1)} %get-tuple-element.132), channel_id=1, source_target_pairs={{0,4},{4,8},{8,12},{12,16},{16,20},{20,24},{24,28},{28,0},{1,5},{5... | collective-permute-start | bytes 491528 | tf_op jit(solution)/shard_map/ppermute | solution.py:771
  11.1 9.8 %collective-permute-start.3 = (f32[160,256]{1,0:T(8,128)S(1)}, f32[160,256]{1,0:T(8,128)S(1)}, u32[]{:S(2)}, u32[]{:S(2)}) collective-permute-start(f32[160,256]{1,0:T(8,128)S(1)} %get-tuple-element.131), channel_id=1, source_target_pairs={{0,28},{4,0},{8,4},{12,8},{16,12},{20,16},{24,20},{28,24},{1,29},{... | collective-permute-start | bytes 491528 | tf_op jit(solution)/shard_map/ppermute | solution.py:771
  26.3 6.6 %collective-permute-start.4 = (f32[32,128]{1,0:T(8,128)S(1)}, f32[32,128]{1,0:T(8,128)S(1)}, u32[]{:S(2)}, u32[]{:S(2)}) collective-permute-start(f32[32,128]{1,0:T(8,128)S(1)} %get-tuple-element.64), channel_id=1, source_target_pairs={{0,1},{1,2},{2,3},{3,0},{4,5},{5,6},{6,7},{7,4},{8,9},{9,10},{10,1... | collective-permute-start | bytes 49160 | tf_op jit(solution)/shard_map/ppermute | solution.py:771
  26.4 6.5 %collective-permute-start.5 = (f32[32,128]{1,0:T(8,128)S(1)}, f32[32,128]{1,0:T(8,128)S(1)}, u32[]{:S(2)}, u32[]{:S(2)}) collective-permute-start(f32[32,128]{1,0:T(8,128)S(1)} %get-tuple-element.65), channel_id=1, source_target_pairs={{0,3},{1,0},{2,1},{3,2},{4,7},{5,4},{6,5},{7,6},{8,11},{9,8},{10,9... | collective-permute-start | bytes 49160 | tf_op jit(solution)/shard_map/ppermute | solution.py:771
  33.0 14.1 %collective-permute-start.6 = (f32[224,256]{1,0:T(8,128)S(1)}, f32[224,256]{1,0:T(8,128)S(1)}, u32[]{:S(2)}, u32[]{:S(2)}) collective-permute-start(f32[224,256]{1,0:T(8,128)S(1)} %get-tuple-element.130), channel_id=1, source_target_pairs={{0,4},{4,8},{8,12},{12,16},{16,20},{20,24},{24,28},{28,0},{1,5},{5... | collective-permute-start | bytes 688136 | tf_op jit(solution)/shard_map/ppermute | solution.py:771
  33.3 13.8 %collective-permute-start.7 = (f32[224,256]{1,0:T(8,128)S(1)}, f32[224,256]{1,0:T(8,128)S(1)}, u32[]{:S(2)}, u32[]{:S(2)}) collective-permute-start(f32[224,256]{1,0:T(8,128)S(1)} %get-tuple-element.129), channel_id=1, source_target_pairs={{0,28},{4,0},{8,4},{12,8},{16,12},{20,16},{24,20},{28,24},{1,29},{... | collective-permute-start | bytes 688136 | tf_op jit(solution)/shard_map/ppermute | solution.py:771
  56.9 3.2 %collective-permute-start.8 = (f32[32,128]{1,0:T(8,128)S(1)}, f32[32,128]{1,0:T(8,128)S(1)}, u32[]{:S(2)}, u32[]{:S(2)}) collective-permute-start(f32[32,128]{1,0:T(8,128)S(1)} %get-tuple-element.73), channel_id=1, source_target_pairs={{0,1},{1,2},{2,3},{3,0},{4,5},{5,6},{6,7},{7,4},{8,9},{9,10},{10,1... | collective-permute-start | bytes 49160 | tf_op jit(solution)/shard_map/ppermute | solution.py:771
  60.2 8.8 %collective-permute-start.10 = (f32[128,256]{1,0:T(8,128)S(1)}, f32[128,256]{1,0:T(8,128)S(1)}, u32[]{:S(2)}, u32[]{:S(2)}) collective-permute-start(f32[128,256]{1,0:T(8,128)S(1)} %get-tuple-element.128), channel_id=1, source_target_pairs={{0,4},{4,8},{8,12},{12,16},{16,20},{20,24},{24,28},{28,0},{1,5},{5... | collective-permute-start | bytes 393224 | tf_op jit(solution)/shard_map/ppermute | solution.py:771
  60.3 9.0 %collective-permute-start.11 = (f32[128,256]{1,0:T(8,128)S(1)}, f32[128,256]{1,0:T(8,128)S(1)}, u32[]{:S(2)}, u32[]{:S(2)}) collective-permute-start(f32[128,256]{1,0:T(8,128)S(1)} %get-tuple-element.127), channel_id=1, source_target_pairs={{0,28},{4,0},{8,4},{12,8},{16,12},{20,16},{24,20},{28,24},{1,29},{... | collective-permute-start | bytes 393224 | tf_op jit(solution)/shard_map/ppermute | solution.py:771
  72.2 4.5 %collective-permute-start.12 = (f32[16,128]{1,0:T(8,128)S(1)}, f32[16,128]{1,0:T(8,128)S(1)}, u32[]{:S(2)}, u32[]{:S(2)}) collective-permute-start(f32[16,128]{1,0:T(8,128)S(1)} %get-tuple-element.81), channel_id=1, source_target_pairs={{0,1},{1,2},{2,3},{3,0},{4,5},{5,6},{6,7},{7,4},{8,9},{9,10},{10,1... | collective-permute-start | bytes 24584 | tf_op jit(solution)/shard_map/ppermute | solution.py:771
  72.3 4.5 %collective-permute-start.13 = (f32[16,128]{1,0:T(8,128)S(1)}, f32[16,128]{1,0:T(8,128)S(1)}, u32[]{:S(2)}, u32[]{:S(2)}) collective-permute-start(f32[16,128]{1,0:T(8,128)S(1)} %get-tuple-element.82), channel_id=1, source_target_pairs={{0,3},{1,0},{2,1},{3,2},{4,7},{5,4},{6,5},{7,6},{8,11},{9,8},{10,9... | collective-permute-start | bytes 24584 | tf_op jit(solution)/shard_map/ppermute | solution.py:771
  76.8 10.9 %collective-permute-start.14 = (f32[160,256]{1,0:T(8,128)S(1)}, f32[160,256]{1,0:T(8,128)S(1)}, u32[]{:S(2)}, u32[]{:S(2)}) collective-permute-start(f32[160,256]{1,0:T(8,128)S(1)} %get-tuple-element.136), channel_id=1, source_target_pairs={{0,4},{4,8},{8,12},{12,16},{16,20},{20,24},{24,28},{28,0},{1,5},{5... | collective-permute-start | bytes 491528 | tf_op jit(solution)/shard_map/ppermute | solution.py:771
  76.9 10.8 %collective-permute-start.15 = (f32[160,256]{1,0:T(8,128)S(1)}, f32[160,256]{1,0:T(8,128)S(1)}, u32[]{:S(2)}, u32[]{:S(2)}) collective-permute-start(f32[160,256]{1,0:T(8,128)S(1)} %get-tuple-element.135), channel_id=1, source_target_pairs={{0,28},{4,0},{8,4},{12,8},{16,12},{20,16},{24,20},{28,24},{1,29},{... | collective-permute-start | bytes 491528 | tf_op jit(solution)/shard_map/ppermute | solution.py:771
  96.2 7.2 %collective-permute-start.18 = (f32[64,256]{1,0:T(8,128)S(1)}, f32[64,256]{1,0:T(8,128)S(1)}, u32[]{:S(2)}, u32[]{:S(2)}) collective-permute-start(f32[64,256]{1,0:T(8,128)S(1)} %get-tuple-element.134), channel_id=1, source_target_pairs={{0,4},{4,8},{8,12},{12,16},{16,20},{20,24},{24,28},{28,0},{1,5},{5... | collective-permute-start | bytes 196616 | tf_op jit(solution)/shard_map/ppermute | solution.py:771
  96.3 7.1 %collective-permute-start.19 = (f32[64,256]{1,0:T(8,128)S(1)}, f32[64,256]{1,0:T(8,128)S(1)}, u32[]{:S(2)}, u32[]{:S(2)}) collective-permute-start(f32[64,256]{1,0:T(8,128)S(1)} %get-tuple-element.133), channel_id=1, source_target_pairs={{0,28},{4,0},{8,4},{12,8},{16,12},{20,16},{24,20},{28,24},{1,29},{... | collective-permute-start | bytes 196616 | tf_op jit(solution)/shard_map/ppermute | solution.py:771
  105.1 3.6 %collective-permute-start.20 = (f32[8,128]{1,0:T(8,128)S(1)}, f32[8,128]{1,0:T(8,128)S(1)}, u32[]{:S(2)}, u32[]{:S(2)}) collective-permute-start(f32[8,128]{1,0:T(8,128)S(1)} %get-tuple-element.96), channel_id=1, source_target_pairs={{0,1},{1,2},{2,3},{3,0},{4,5},{5,6},{6,7},{7,4},{8,9},{9,10},{10,1... | collective-permute-start | bytes 12296 | tf_op jit(solution)/shard_map/ppermute | solution.py:771
  105.2 3.6 %collective-permute-start.21 = (f32[8,128]{1,0:T(8,128)S(1)}, f32[8,128]{1,0:T(8,128)S(1)}, u32[]{:S(2)}, u32[]{:S(2)}) collective-permute-start(f32[8,128]{1,0:T(8,128)S(1)} %get-tuple-element.97), channel_id=1, source_target_pairs={{0,3},{1,0},{2,1},{3,2},{4,7},{5,4},{6,5},{7,6},{8,11},{9,8},{10,9... | collective-permute-start | bytes 12296 | tf_op jit(solution)/shard_map/ppermute | solution.py:771
  108.8 9.7 %collective-permute-start.22 = (f32[80,256]{1,0:T(8,128)S(1)}, f32[80,256]{1,0:T(8,128)S(1)}, u32[]{:S(2)}, u32[]{:S(2)}) collective-permute-start(f32[80,256]{1,0:T(8,128)S(1)} %get-tuple-element.138), channel_id=1, source_target_pairs={{0,4},{4,8},{8,12},{12,16},{16,20},{20,24},{24,28},{28,0},{1,5},{5... | collective-permute-start | bytes 245768 | tf_op jit(solution)/shard_map/ppermute | solution.py:771
  108.9 9.7 %collective-permute-start.23 = (f32[80,256]{1,0:T(8,128)S(1)}, f32[80,256]{1,0:T(8,128)S(1)}, u32[]{:S(2)}, u32[]{:S(2)}) collective-permute-start(f32[80,256]{1,0:T(8,128)S(1)} %get-tuple-element.137), channel_id=1, source_target_pairs={{0,28},{4,0},{8,4},{12,8},{16,12},{20,16},{24,20},{28,24},{1,29},{... | collective-permute-start | bytes 245768 | tf_op jit(solution)/shard_map/ppermute | solution.py:771
  126.5 6.6 %collective-permute-start.24 = (f32[8,6144]{1,0:T(8,128)S(1)}, f32[8,6144]{1,0:T(8,128)S(1)}, u32[]{:S(2)}, u32[]{:S(2)}) collective-permute-start(f32[8,6144]{1,0:T(8,128)S(1)} %get-tuple-element.104), channel_id=1, source_target_pairs={{0,1},{1,2},{2,3},{3,0},{4,5},{5,6},{6,7},{7,4},{8,9},{9,10},{10,1... | collective-permute-start | bytes 589832 | tf_op jit(solution)/shard_map/ppermute | solution.py:771
  126.6 7.8 %collective-permute-start.25 = (f32[8,6144]{1,0:T(8,128)S(1)}, f32[8,6144]{1,0:T(8,128)S(1)}, u32[]{:S(2)}, u32[]{:S(2)}) collective-permute-start(f32[8,6144]{1,0:T(8,128)S(1)} %get-tuple-element.105), channel_id=1, source_target_pairs={{0,2},{1,3},{2,0},{3,1},{4,6},{5,7},{6,4},{7,5},{8,10},{9,11},{10,... | collective-permute-start | bytes 589832 | tf_op jit(solution)/shard_map/ppermute | solution.py:771
  127.8 8.3 %collective-permute-start.26 = (f32[8,6144]{1,0:T(8,128)S(1)}, f32[8,6144]{1,0:T(8,128)S(1)}, u32[]{:S(2)}, u32[]{:S(2)}) collective-permute-start(f32[8,6144]{1,0:T(8,128)S(1)} %get-tuple-element.106), channel_id=1, source_target_pairs={{0,3},{1,0},{2,1},{3,2},{4,7},{5,4},{6,5},{7,6},{8,11},{9,8},{10,9... | collective-permute-start | bytes 589832 | tf_op jit(solution)/shard_map/ppermute | solution.py:771
  (6 other events, 67.0 us)
